TPU v7x, 256 devices: a whole 4x4x8 slice. The times are simulated.
256 devices in a mesh: section: 8 (over y, z_lo), rows: 4 (over x), hid: 8 (over z_hi, core).
Axes of the slice: x: 4, y: 4, z: 8 (z_hi: 4, z_lo: 2; z = z_hi * 2 + z_lo), core: 2. Of those that a mesh axis runs over, the one named last changes fastest.
Arguments:
- acts: bfloat16 [8, 1024, 4096], P('section', 'rows', 'hid'), may hold values from -11 to 11
- ln_gain: float32 [8, 4096], P('section'), may hold values from 0.1 to 1.9
- ln_bias: float32 [8, 4096], P('section'), may hold values from -1.5 to 1.5
- w_up: bfloat16 [8, 4096, 16384], P('section', None, ('rows', 'hid')), may hold values from -0.09375 to 0.09375
- b_up: float32 [8, 16384], P('section', ('rows', 'hid')), may hold values from -3 to 3
- w_down: bfloat16 [8, 16384, 4096], P('section', ('rows', 'hid')), may hold values from -0.09375 to 0.09375
- b_down: float32 [8, 4096], P('section'), may hold values from -3 to 3
Outputs:
- arrived: bfloat16 [8, 2, 512, 4096], P('section', None, 'rows', 'hid')
All inputs are finite; a program needn't handle non-finite values.
Results may differ from a plain program's by a relative error of at most 0.0041.
Values may be sent and summed in bfloat16 or wider, within the bound.
No kernel may reach another device: no remote copies, remote signals or barrier semaphores. Data moves between devices by JAX's collectives and lax.ppermute only.
A program may use at most 128 MiB of HBM per device.

v0:
```python
import jax
import jax.numpy as jnp
from jax import lax
from jax.sharding import PartitionSpec as P

BATCH = 2
SEQ = 512


def passed_along(block, axis, distance):
    devices = range(lax.axis_size(axis))
    route = [((i - distance) % len(devices), i) for i in devices]
    return lax.ppermute(block, axis, route)


def shards(acts, ln_gain, ln_bias, w_up, b_up, w_down, b_down):
    wide = lax.all_gather(acts, "hid", axis=2, tiled=True)[0]
    values = wide.astype(jnp.float32)
    mean = jnp.mean(values, axis=-1, keepdims=True)
    centered = values - mean
    spread = jnp.mean(centered * centered, axis=-1, keepdims=True)
    normed = (centered * lax.rsqrt(spread + 1e-05) * ln_gain[0] + ln_bias[0]).astype(jnp.bfloat16)
    every_normed, every_input = (
        lax.all_gather(normed, "rows", axis=0, tiled=True),
        lax.all_gather(wide, "rows", axis=0, tiled=True),
    )
    width = every_normed.shape[1]
    pre = jnp.dot(every_normed, w_up[0], preferred_element_type=jnp.float32) + b_up[0]
    hidden = jax.nn.gelu(pre, approximate=True).astype(jnp.bfloat16)
    partial_value = jnp.dot(hidden, w_down[0], preferred_element_type=jnp.float32)
    partial_value = partial_value.reshape(BATCH, SEQ, width)
    seq_part = SEQ // lax.axis_size("rows")
    width_part = width // lax.axis_size("hid")
    seq_start = lax.axis_index("rows") * seq_part
    width_start = lax.axis_index("hid") * width_part
    by_position = lax.psum_scatter(partial_value, "rows", scatter_dimension=1, tiled=True)
    block = lax.psum_scatter(by_position, "hid", scatter_dimension=2, tiled=True)
    shaped_input = every_input.reshape(BATCH, SEQ, width)
    block = block + lax.dynamic_slice(
        shaped_input, (0, seq_start, width_start), (BATCH, seq_part, width_part)
    ).astype(jnp.float32)
    bias_part = lax.dynamic_slice_in_dim(b_down[0], width_start, width_part, 0)
    boundary = (block + bias_part).astype(jnp.bfloat16)[None]
    return passed_along(boundary, "section", 1)


def solution(mesh):
    in_specs = (
        P("section", "rows", "hid"),
        P("section", None),
        P("section", None),
        P("section", None, ("rows", "hid")),
        P("section", ("rows", "hid")),
        P("section", ("rows", "hid"), None),
        P("section", None),
    )
    out_specs = P("section", None, "rows", "hid")
    return jax.shard_map(shards, mesh=mesh, in_specs=in_specs, out_specs=out_specs, check_vma=False)
```

profile of v0, /device:TPU:1, one launch (start us, length us, event | category | flops | bytes accessed | tf_op | source)
XLA Modules:
  0.0 477.1 jit_solution(80501545388020775)
XLA Ops:
  6.5 0.7 all-gather.5.cloned.1.call-update
  7.3 0.0 all-gather.7.cloned.1.call-start
  7.3 42.7 %all-gather.5.cloned.1.call-done = bf16[1,256,4096]{2,1,0:T(8,128)(2,1)} async-done(((bf16[1,256,512]{2,1,0:T(8,128)(2,1)}), bf16[1,256,4096]{2,1,0:T(8,128)(2,1)}) %all-gather.5.cloned.1.call-update) | async-done | bytes 2097168 | tf_op jit(solution)/shard_map/all_gather | solution.py:17
  50.0 2.1 convert_reduce_fusion
  52.1 0.0 copy-start.5
  52.1 2.3 fusion.3
  54.4 2.4 fusion.6
  56.8 0.0 all-gather.7.cloned.1.call-update
  56.8 0.0 reduce-scatter.3.cloned.1.call-start
  56.9 82.9 %all-gather.7.cloned.1.call-done = bf16[1024,4096]{1,0:T(8,128)(2,1)} async-done(((bf16[256,4096]{1,0:T(8,128)(2,1)}), bf16[1024,4096]{1,0:T(8,128)(2,1)}) %all-gather.7.cloned.1.call-update) | async-done | bytes 8388624 | tf_op jit(solution)/shard_map/all_gather | solution.py:24
  139.8 9.7 %fusion.18 = bf16[1024,512]{1,0:T(8,128)(2,1)S(1)} fusion(bf16[1024,4096]{1,0:T(8,128)(2,1)} %all-gather.7.cloned.1.call-done, bf16[1,4096,512]{2,1,0:T(8,128)(2,1)} %param.10, f32[512]{0:T(512)S(1)} %bitcast.39), kind=kOutput, calls=%fused_computation.21 | convolution fusion | flops 4300210176 | bytes 13633536 | tf_op jit(solution)/shard_map/dot_general | solution.py:28
  149.5 8.2 %fusion.7 = f32[2,512,4096]{2,1,0:T(8,128)} fusion(bf16[2,512,512]{2,1,0:T(8,128)(2,1)S(1)} %bitcast.40, bf16[1,512,4096]{2,1,0:T(8,128)(2,1)S(1)} %copy-done.4), kind=kOutput, calls=%fused_computation.9 | convolution fusion | flops 4294967296 | bytes 22020096 | tf_op jit(solution)/shard_map/dot_general | solution.py:30
  157.7 0.0 reduce-scatter.3.cloned.1.call-update
  157.7 0.0 all-gather.9.cloned.1.call-start
  157.7 0.5 all-gather.9.cloned.1.call-update
  158.3 0.0 reduce-scatter.5.cloned.1.call-start
  158.3 151.0 %reduce-scatter.3.cloned.1.call-done = f32[2,128,4096]{2,1,0:T(8,128)} async-done(((f32[2,512,4096]{2,1,0:T(8,128)}), f32[2,128,4096]{2,1,0:T(8,128)}) %reduce-scatter.3.cloned.1.call-update) | async-done | bytes 4194320 | tf_op jit(solution)/shard_map/reduce_scatter | solution.py:36
  309.3 0.0 reduce-scatter.5.cloned.1.call-update
  309.4 87.2 %all-gather.9.cloned.1.call-done = bf16[1,1024,4096]{2,1,0:T(8,128)(2,1)} async-done(((bf16[1,256,4096]{2,1,0:T(8,128)(2,1)}), bf16[1,1024,4096]{2,1,0:T(8,128)(2,1)}) %all-gather.9.cloned.1.call-update) | async-done | bytes 8388624 | tf_op jit(solution)/shard_map/all_gather | solution.py:25
  396.6 61.7 %reduce-scatter.5.cloned.1.call-done = f32[2,128,512]{2,1,0:T(8,128)} async-done(((f32[2,128,4096]{2,1,0:T(8,128)}), f32[2,128,512]{2,1,0:T(8,128)}) %reduce-scatter.5.cloned.1.call-update) | async-done | bytes 524304 | tf_op jit(solution)/shard_map/reduce_scatter | solution.py:37
  458.2 1.2 fusion.21
  459.4 0.1 collective-permute-start
  459.5 10.3 %collective-permute-done = bf16[1,2,128,512]{3,2,1,0:T(8,128)(2,1)S(1)} collective-permute-done((bf16[1,2,128,512]{3,2,1,0:T(8,128)(2,1)S(1)}, bf16[1,2,128,512]{3,2,1,0:T(8,128)(2,1)S(1)}, u32[]{:S(2)}, u32[]{:S(2)}) %collective-permute-start) | collective-permute-done | bytes 262176 | tf_op jit(solution)/shard_map/ppermute | solution.py:13
  469.8 0.7 copy.9
  (15 shorter events, 0.0 us)
Async XLA Ops:
  6.5 302.8 %copy-start = (f32[1,4096]{1,0:T(1,128)S(1)}, f32[1,4096]{1,0:T(1,128)}, u32[]{:S(2)}) copy-start(f32[1,4096]{1,0:T(1,128)} %param.13) | copy-start | bytes 49156
  6.5 47.9 %copy-start.3 = (f32[1,4096]{1,0:T(1,128)S(1)}, f32[1,4096]{1,0:T(1,128)}, u32[]{:S(2)}) copy-start(f32[1,4096]{1,0:T(1,128)} %param.8) | copy-start | bytes 49156
  6.5 47.9 %copy-start.2 = (f32[1,4096]{1,0:T(1,128)S(1)}, f32[1,4096]{1,0:T(1,128)}, u32[]{:S(2)}) copy-start(f32[1,4096]{1,0:T(1,128)} %param.9) | copy-start | bytes 49156
  6.5 43.4 %all-gather.5.cloned.1.call-start = ((), (), s32[]{:S(2)}) async-start(), calls=%async_computation.2 | async-start | bytes 2359296 | tf_op jit(solution)/shard_map/all_gather | solution.py:17
  7.3 132.5 %all-gather.7.cloned.1.call-start = ((), (), s32[]{:S(2)}) async-start(), calls=%async_computation.3 | async-start | bytes 10485760 | tf_op jit(solution)/shard_map/all_gather | solution.py:24
  50.0 4.4 copy-start.1
  52.1 87.7 %copy-start.5 = (f32[1,512]{1,0:T(1,128)S(1)}, f32[1,512]{1,0:T(1,128)}, u32[]{:S(2)}) copy-start(f32[1,512]{1,0:T(1,128)} %param.11) | copy-start | bytes 6148
  56.8 252.5 %reduce-scatter.3.cloned.1.call-start = ((), (), s32[]{:S(2)}) async-start(), calls=%async_computation.4 | async-start | bytes 20971520 | tf_op jit(solution)/shard_map/reduce_scatter | solution.py:36
  139.8 9.7 %copy-start.4 = (bf16[1,512,4096]{2,1,0:T(8,128)(2,1)S(1)}, bf16[1,512,4096]{2,1,0:T(8,128)(2,1)}, u32[]{:S(2)}) copy-start(bf16[1,512,4096]{2,1,0:T(8,128)(2,1)} %param.12) | copy-start | bytes 12582916
  157.7 238.9 %all-gather.9.cloned.1.call-start = ((), (), s32[]{:S(2)}) async-start(), calls=%async_computation.6 | async-start | bytes 10485760 | tf_op jit(solution)/shard_map/all_gather | solution.py:25
  158.3 300.0 %reduce-scatter.5.cloned.1.call-start = ((), (), s32[]{:S(2)}) async-start(), calls=%async_computation.5 | async-start | bytes 4718592 | tf_op jit(solution)/shard_map/reduce_scatter | solution.py:37
  459.4 10.4 %collective-permute-start = (bf16[1,2,128,512]{3,2,1,0:T(8,128)(2,1)S(1)}, bf16[1,2,128,512]{3,2,1,0:T(8,128)(2,1)S(1)}, u32[]{:S(2)}, u32[]{:S(2)}) collective-permute-start(bf16[1,2,128,512]{3,2,1,0:T(8,128)(2,1)S(1)} %fusion.21), channel_id=1, source_target_pairs={{224,0},{0,32},{32,64},{64,96},{96,128},{128,160},{160,192},{192,2... | collective-permute-start | bytes 786440 | tf_op jit(solution)/shard_map/ppermute | solution.py:13
Sparse Core Ops, SparseCore 0:
  9.2 40.7 all-gather.4
  56.9 82.8 all-gather.6
  157.8 151.4 reduce-scatter.2
  311.1 85.3 all-gather.8
  399.1 59.0 reduce-scatter.4
where the time goes:
time: 477 us
  waiting for transfers between devices  437 us (92%)
  matrix products  17.8 us (4%)
  between operations  13.2 us (3%)
  other arithmetic  7.96 us (2%)
    reduce_scatter x1, waiting for transfers between devices, shards(): lax.psum_scatter(partial_value, 'rows', scatter_dimension=1, tiled=True)  151 us
    all_gather x1, waiting for transfers between devices, shards(): lax.all_gather(wide, 'rows', axis=0, tiled=True)  87.2 us
    all_gather x1, waiting for transfers between devices, shards(): lax.all_gather(normed, 'rows', axis=0, tiled=True)  82.9 us
    reduce_scatter x1, waiting for transfers between devices, shards(): lax.psum_scatter(by_position, 'hid', scatter_dimension=2, tiled=True)  61.7 us
    all_gather x1, waiting for transfers between devices, shards(): wide = lax.all_gather(acts, 'hid', axis=2, tiled=True)[0]  42.7 us
    ppermute x1, waiting for transfers between devices, passed_along(): return lax.ppermute(block, axis, route)  10.3 us
    dot_general x1, matrix products, shards(): jnp.dot(every_normed, w_up[0], preferred_element_type=jnp.float32) + b_up[0]  9.67 us
  transfers between devices with their start and end apart: 6, of which 6 were waited for; matrix products, arithmetic and copies ran while one was open for 0% of the time, Pallas kernels for 0%

commit v1 on v0

v1 whole, which is shorter than its diff:
```python
import jax
import jax.numpy as jnp
from jax import lax
from jax.experimental import pallas as pl
from jax.experimental.pallas import tpu as pltpu
from jax.sharding import Mesh
from jax.sharding import PartitionSpec as P

BATCH = 2
RING = 4
TILE = 64
PART = 1024
HALF = PART // 2
UNITS = 512
STEP = 256
ROWS = 16
UNROLL = 4
EPS = 1e-05
MIB = 1024 * 1024
LIMIT = 16
COST = 4
BYTES = MIB


def sent(block, axis, distance):
    return lax.ppermute(block, axis, [(i, (i + distance) % RING) for i in range(RING)])


def swapped(block):
    return lax.ppermute(block, "core", [(0, 1), (1, 0)])


def next_section(block, cross):
    pairs = []
    for section in range(8):
        for core in range(2):
            pairs.append((section * 2 + core, (section + 1) % 8 * 2 + (core ^ cross)))
    return lax.ppermute(block, ("y", "zl", "core"), pairs)


def added(*terms):
    return sum(t.astype(jnp.float32) for t in terms).astype(jnp.bfloat16)


def normalize(pieces, z, gain, bias, normed, at, rows):
    def some(i, _):
        start = pl.multiple_of(i * ROWS, ROWS)
        values = [read(start).astype(jnp.float32) for read in pieces]
        mean = sum(jnp.sum(v, axis=-1, keepdims=True) for v in values) / (RING * PART)
        centered = [v - mean for v in values]
        spread = sum(jnp.sum(v * v, axis=-1, keepdims=True) for v in centered) / (RING * PART)
        scale = lax.rsqrt(spread + EPS)
        for k in range(RING):
            true = (z + k) & 3
            value = centered[k] * scale * gain[pl.ds(true, 1), :] + bias[pl.ds(true, 1), :]
            normed[true, pl.ds(at + start, ROWS), :] = value.astype(jnp.bfloat16)
        return 0

    lax.fori_loop(0, rows // ROWS, some, 0, unroll=UNROLL)


def reader(ref, *lead):
    return lambda start: ref[(*lead, pl.ds(start, ROWS), slice(None))]


def halves(ref, *lead, first=0):
    return lambda start: ref[(*lead, first + start // TILE, pl.ds(pl.multiple_of(start % TILE, ROWS), ROWS), slice(None))]


def up(normed, ups, b_up, store):
    def some(n, _):
        columns = pl.ds(pl.multiple_of((n & 1) * STEP, STEP), STEP)
        pre = b_up[pl.ds(n >> 1, 1), columns]
        for k in range(RING):
            pre = pre + jnp.dot(
                normed[k], ups[n >> 1, pl.ds(k * PART, PART), columns], preferred_element_type=jnp.float32
            )
        store(pl.ds(pl.multiple_of(n * STEP, STEP), STEP), jax.nn.gelu(pre, approximate=True).astype(jnp.bfloat16))
        return 0

    lax.fori_loop(0, 2 * UNITS // STEP, some, 0)


def near_kernel(place, block, zs, zz, xm, sm, mr, xp, sp, ml, gain, bias, b_up, ups, hidden, normed):
    z = place[1]
    for slot, (a, b, c) in enumerate(((block, zs, zz), (xm, sm, mr), (xp, sp, ml))):
        pieces = [halves(a), halves(b, 1), halves(c, first=2 if slot else 0), halves(b, 0)]
        normalize(pieces, z, gain, bias, normed, slot * 2 * TILE, 2 * TILE)

    def store(columns, value):
        for tile in range(6):
            hidden[tile, :, columns] = value[tile * TILE : (tile + 1) * TILE]

    up(normed, ups, b_up, store)


def down(z, hid, downs, offset, stride, group, outs):
    plus, minus, left, right, own = outs
    homes = {
        (0, 0): (own, (0,)), (0, 1): (own, (1,)), (1, 0): (left, ()), (1, 1): (plus, (1,)),
        (2, 0): (plus, (0,)), (2, 1): (minus, (0,)), (3, 0): (minus, (1,)), (3, 1): (right, ()),
    }

    def some(i, _):
        n, t = i >> 1, i & 1
        columns = pl.ds(pl.multiple_of(t * HALF, HALF), HALF)
        start = pl.ds(pl.multiple_of(((z + offset + stride * n) & 3) * PART + t * HALF, HALF), HALF)
        rows = hid[...].reshape(8 * TILE, 2 * UNITS)
        term = jnp.dot(rows[:, :UNITS], downs[0, :, start], preferred_element_type=jnp.float32)
        term = term + jnp.dot(rows[:, UNITS:], downs[1, :, start], preferred_element_type=jnp.float32)
        term = term.astype(jnp.bfloat16)
        for (dest, seq), (ref, lead) in homes.items():
            at = (dest * 2 + seq) * TILE
            ref[(*lead, n, slice(None), columns)] = term[at : at + TILE]
        return 0

    lax.fori_loop(0, group * PART // HALF, some, 0)


def far_kernel(place, ml, mr, nl, nr, gain, bias, b_up, near, ups, downs,
               plus, minus, left, right, own, hid, normed):
    x, z = place[0], place[1]

    def home(j, half):
        row = (x + j) & 3
        return (((row & 1) * 2 + half - x) & 3) * 2 + (row >> 1)

    for half, (a, b) in enumerate(((ml, nl), (mr, nr))):
        pieces = [reader(b, 1), reader(a, 1), reader(b, 0), reader(a, 0)]
        normalize(pieces, z, gain, bias, normed, half * TILE, TILE)
    for slot, j in enumerate((0, 1, 3)):
        for half in range(2):
            hid[home(j, half)] = near[slot * 2 + half]

    def store(columns, value):
        for half in range(2):
            hid[home(2, half), :, columns] = value[half * TILE : (half + 1) * TILE]

    up(normed, ups, b_up, store)
    down(z, hid, downs, 2, 0, 1, (plus, minus, left, right, own))


def side_kernel(place, hid, downs, plus, minus, left, right, own):
    down(place[1], hid, downs, 1, 2, 2, (plus, minus, left, right, own))


def own_kernel(place, hid, downs, block, xm, nl, nr, xp, plus, minus, left, right, own, resid):
    x = place[0]
    for seq in range(2):
        row, half = 2 * seq + (x >> 1), x & 1
        j = (row - x) & 3
        for at, ref in ((0, block), (1, xm), (3, xp)):

            @pl.when(j == at)
            def _(ref=ref):
                resid[seq] = ref[half]

        @pl.when((j == 2) & (half == 0))
        def _():
            resid[seq] = nl[1]

        @pl.when((j == 2) & (half == 1))
        def _():
            resid[seq] = nr[1]

    down(place[1], hid, downs, 0, 0, 1, (plus, minus, left, right, own))


VMEM = pl.BlockSpec(memory_space=pltpu.VMEM)
SMEM = pl.BlockSpec(memory_space=pltpu.SMEM)


def call(kernel, out_shape, scratch, flops, *operands):
    return pl.pallas_call(
        kernel,
        in_specs=[SMEM] + [VMEM] * (len(operands) - 1),
        out_specs=[VMEM] * len(out_shape),
        out_shape=out_shape,
        scratch_shapes=scratch,
        compiler_params=pltpu.CompilerParams(vmem_limit_bytes=LIMIT * MIB),
        cost_estimate=pl.CostEstimate(flops=flops // COST, bytes_accessed=BYTES, transcendentals=0),
    )(*operands)


def group_shapes(group):
    two = jax.ShapeDtypeStruct((2, group, TILE, PART), jnp.bfloat16)
    one = jax.ShapeDtypeStruct((group, TILE, PART), jnp.bfloat16)
    return [two, two, one, one, two]


def load_kernel(own, other, out, token, sems):
    copies = [pltpu.make_async_copy(ref, out.at[i], sems.at[i]) for i, ref in enumerate((own, other))]
    for copy in copies:
        copy.start()
    token[...] = jnp.zeros_like(token)
    for copy in copies:
        copy.wait()


def loaded(own, other):
    return pl.pallas_call(
        load_kernel,
        in_specs=[pl.BlockSpec(memory_space=pltpu.HBM)] * 2,
        out_specs=[VMEM, VMEM],
        out_shape=[pltpu.VMEM((2, *own.shape), own.dtype), jax.ShapeDtypeStruct((8, 128), jnp.float32)],
        scratch_shapes=[pltpu.SemaphoreType.DMA((2,))],
        compiler_params=pltpu.CompilerParams(vmem_limit_bytes=LIMIT * MIB),
        cost_estimate=pl.CostEstimate(flops=0, bytes_accessed=16 * MIB, transcendentals=0),
    )(own, other)


def compute(place, block, zs, zz, xm, sm, mr, xp, sp, ml, nl, nr,
            gain, bias, b_all, ups, downs):
    mul = 2 * 2 * UNITS * RING * PART
    near = call(
        near_kernel,
        [jax.ShapeDtypeStruct((6, TILE, 2 * UNITS), jnp.bfloat16)],
        [pltpu.VMEM((RING, 6 * TILE, PART), jnp.bfloat16)],
        6 * TILE * mul,
        place, block, zs, zz, xm, sm, mr, xp, sp, ml, gain, bias, b_all, ups,
    )[0]
    *two, hid = call(
        far_kernel,
        group_shapes(1) + [jax.ShapeDtypeStruct((8, TILE, 2 * UNITS), jnp.bfloat16)],
        [pltpu.VMEM((RING, 2 * TILE, PART), jnp.bfloat16)],
        2 * TILE * mul + 2 * TILE * mul,
        place, ml, mr, nl, nr, gain, bias, b_all, near, ups, downs,
    )
    side = call(
        side_kernel, group_shapes(2), [], 4 * TILE * mul,
        place, hid, downs,
    )
    return two, side, hid


def shards(acts, ln_gain, ln_bias, w_up, b_up, w_down, b_down):
    x, z, core = (lax.axis_index(a) for a in ("x", "zh", "core"))
    place = jnp.stack([x, z]).astype(jnp.int32)
    up_o, down_o = w_up[0], w_down[0]
    gain, bias = ln_gain[0].reshape(RING, PART), ln_bias[0].reshape(RING, PART)

    split = acts[0].reshape(2, 2, TILE, HALF)
    mine = lax.dynamic_index_in_dim(split, core, 1, keepdims=False)
    theirs = lax.dynamic_index_in_dim(split, 1 - core, 1, keepdims=False)
    got, b_up_s = lax.optimization_barrier((swapped(theirs), swapped(b_up)))
    low = jnp.where(core == 0, mine, got)
    high = jnp.where(core == 0, got, mine)
    block = jnp.concatenate([low, high], axis=-1)
    block, up_o = lax.optimization_barrier((block, up_o))
    b_all = jnp.concatenate([b_up, b_up_s], axis=0)

    zp, zm = sent(block, "zh", 1), sent(block, "zh", -1)
    xp, xm = sent(block, "x", 1), sent(block, "x", -1)
    up_s = swapped(up_o)
    zp, zm, xp, xm, up_s, down_o = lax.optimization_barrier((zp, zm, xp, xm, up_s, down_o))
    zs = jnp.stack([zp, zm])
    za, zb = sent(zp[0], "zh", 1), sent(zm[1], "zh", -1)
    sp, sm = sent(zs, "x", 1), sent(zs, "x", -1)
    down_s = swapped(down_o)
    ups, token = loaded(up_o, up_s)
    za, zb, sp, sm, xp, xm, token = lax.optimization_barrier((za, zb, sp, sm, xp, xm, token))
    place = place + token[0, :2].astype(jnp.int32)
    zz = jnp.stack([za, zb])
    ml = sent(jnp.concatenate([sp[:, 0], zz]), "x", 1)
    mr = sent(jnp.concatenate([sm[:, 1], zz]), "x", -1)
    downs, token = loaded(down_o, down_s)
    ml, mr, xp, xm, token = lax.optimization_barrier((ml, mr, xp, xm, token))
    place = place + token[0, :2].astype(jnp.int32)
    nl = sent(jnp.stack([ml[2], xp[0]]), "x", 1)
    nr = sent(jnp.stack([mr[3], xm[1]]), "x", -1)

    two, side, hid = compute(place, block, zs, zz, xm, sm, mr, xp, sp, ml, nl, nr,
                             gain, bias, b_all, ups, downs)

    def first_step(plus, minus, *_):
        return lax.optimization_barrier((sent(plus, "x", 1), sent(minus, "x", -1)))

    def second_step(parts, l, r):
        return lax.optimization_barrier((sent(added(parts[2], l[0]), "x", 1), sent(added(parts[3], r[0]), "x", -1)))

    def summed(parts, l, r, fl, fr):
        own = parts[4]
        return added(own[0], fl, r[1]), added(own[1], l[1], fr)

    l2, r2 = first_step(*two)
    l2, r2, hid = lax.optimization_barrier((l2, r2, hid))
    *last, resid = call(
        own_kernel, group_shapes(1) + [jax.ShapeDtypeStruct((2, TILE, PART), jnp.bfloat16)], [], 2 * TILE * 2 * 2 * UNITS * RING * PART,
        place, hid, downs, block, xm, nl, nr, xp,
    )
    fl2, fr2 = second_step(two, l2, r2)
    l1, r1 = first_step(*side)
    s0, s1 = summed(two, l2, r2, fl2, fr2)
    zl, zr = lax.optimization_barrier((sent(s0, "zh", 1), sent(s1, "zh", -1)))
    plus, minus, l1, r1 = lax.optimization_barrier((*last[:2], l1, r1))
    fl1, fr1 = second_step(side, l1, r1)
    l0, r0 = first_step(plus, minus)
    t0, t1 = summed(side, l1, r1, fl1, fr1)
    zfl = sent(jnp.stack([added(t0[:1], zl), t1[:1]]), "zh", 1)
    zfr = sent(jnp.stack([t0[1:], added(t1[1:], zr)]), "zh", -1)
    fl0, fr0 = second_step(last, l0, r0)
    shift = lax.dynamic_slice_in_dim(b_down[0], z * PART, PART, 0)
    own = last[4]
    value = jnp.concatenate(
        [
            added(own[0], fl0, r0[1], zfl[0], zfr[0], resid[:1], shift),
            added(own[1], l0[1], fr0, zfl[1], zfr[1], resid[1:], shift),
        ]
    )
    low, high = value[..., :HALF], value[..., HALF:]
    keep = next_section(jnp.where(core == 0, low, high), 0)
    cross = next_section(jnp.where(core == 0, high, low), 1)
    out = jnp.stack([jnp.where(core == 0, keep, cross), jnp.where(core == 0, cross, keep)], axis=1)
    return out.reshape(1, BATCH, 2 * TILE, HALF)


def solution(mesh):
    fine = Mesh(mesh.devices.reshape(4, 2, 4, 4, 2), ("y", "zl", "x", "zh", "core"))
    section, rows, hid = ("y", "zl"), "x", ("zh", "core")
    in_specs = (
        P(section, rows, hid),
        P(section, None),
        P(section, None),
        P(section, None, ("x", "zh", "core")),
        P(section, ("x", "zh", "core")),
        P(section, ("x", "zh", "core"), None),
        P(section, None),
    )
    out_specs = P(section, None, rows, hid)
    return jax.shard_map(shards, mesh=fine, in_specs=in_specs, out_specs=out_specs, check_vma=False)
```

time: 477 us -> 142 us (0.30)
  waiting for transfers between devices: 437 us -> 54.3 us
  starting transfers between devices: 0.25 us -> 50.7 us
  Pallas kernels: 0 us -> 21.1 us
  matrix products: 17.8 us -> 0 us
  between operations: 13.2 us -> 0.43 us
  local copies, waits for them, and re-layouts: 0.74 us -> 10.1 us
    all_gather x3 -> x0, waiting for transfers between devices: 213 us -> none  [the longest x1 87.2 us: shards(): lax.all_gather(wide, 'rows', axis=0, tiled=True)]
    reduce_scatter x2 -> x0, waiting for transfers between devices: 213 us -> none  [the longest x1 151 us: shards(): lax.psum_scatter(partial_value, 'rows', scatter_dimension=1, tiled=True)]
    ppermute x1 -> x34, starting transfers between devices: 0.08 us -> 50.7 us  [the longest x28 34.5 us: sent(): lax.ppermute(block, axis, [(i, (i + distance) % RING) for i in range(RING)])]
    ppermute x1 -> x34, waiting for transfers between devices: 10.3 us -> 54.3 us  [the longest x28 46.9 us: sent(): lax.ppermute(block, axis, [(i, (i + distance) % RING) for i in range(RING)])]
    pallas_call x0 -> x6, Pallas kernels: none -> 21.1 us  [the longest x4 17.6 us: call(): pl.pallas_call(kernel, in_specs=[SMEM] + [VMEM] * (len(operands) - 1), ou...]
    dot_general x2 -> x0, matrix products: 17.8 us -> none  [the longest x1 9.67 us: shards(): jnp.dot(every_normed, w_up[0], preferred_element_type=jnp.float32) + b_up[0]]
    unnamed x13 -> x21, local copies, waits for them, and re-layouts: 0.73 us -> 8.35 us
  transfers between devices with their start and end apart: 6 -> 34, of which waited for: 6 -> 20; matrix products, arithmetic and copies ran while one was open for 0% -> 3% of each run, Pallas kernels for 0% -> 11%
where the time goes in v1:
time: 142 us
  waiting for transfers between devices  54.3 us (38%)
  starting transfers between devices  50.7 us (36%)
  Pallas kernels  21.1 us (15%)
  local copies, waits for them, and re-layouts  10.1 us (7%)
  other arithmetic  5.56 us (4%)
    ppermute x28, waiting for transfers between devices, sent(): lax.ppermute(block, axis, [(i, (i + distance) % RING) for i in range(RING)])  46.9 us
    ppermute x28, starting transfers between devices, sent(): lax.ppermute(block, axis, [(i, (i + distance) % RING) for i in range(RING)])  34.5 us
    pallas_call x4, Pallas kernels, call(): pl.pallas_call(kernel, in_specs=[SMEM] + [VMEM] * (len(operands) - 1), ou...  17.6 us
    ppermute x4, starting transfers between devices, swapped(): return lax.ppermute(block, 'core', [(0, 1), (1, 0)])  9.14 us
    unnamed x21, local copies, waits for them, and re-layouts  8.35 us
    ppermute x2, starting transfers between devices, next_section(): return lax.ppermute(block, ('y', 'zl', 'core'), pairs)  7.04 us
    ppermute x2, waiting for transfers between devices, next_section(): return lax.ppermute(block, ('y', 'zl', 'core'), pairs)  6.11 us
    pallas_call x2, Pallas kernels, loaded(): pl.pallas_call(load_kernel, in_specs=[pl.BlockSpec(memory_space=pltpu.HBM...  3.42 us
  transfers between devices with their start and end apart: 34, of which 20 were waited for; matrix products, arithmetic and copies ran while one was open for 3% of the time, Pallas kernels for 11%

profile of v1, /device:TPU:1, one launch (start us, length us, event | category | flops | bytes accessed | tf_op | source)
XLA Modules:
  0.0 142.1 jit_solution(12777919434695021864)
XLA Ops:
  0.9 3.3 %collective-permute-start = (bf16[2,64,512]{2,1,0:T(8,128)(2,1)S(1)}, bf16[2,64,512]{2,1,0:T(8,128)(2,1)S(1)}, u32[]{:S(2)}, u32[]{:S(2)}) collective-permute-start(bf16[2,64,512]{2,1,0:T(8,128)(2,1)S(1)} %dynamic-slice_bitcast_fusion), channel_id=1, source_target_pairs={{0,1},{1,0},{2,3},{3,2},{4,5},{5,4},{6,7},{7,6},{8,9},{9,8},{10,11... | collective-permute-start | bytes 393224 | tf_op jit(solution)/shard_map/ppermute | solution.py:30
  8.3 5.3 %collective-permute-start.3 = (bf16[2,64,1024]{2,1,0:T(8,128)(2,1)S(1)}, bf16[2,64,1024]{2,1,0:T(8,128)(2,1)S(1)}, u32[]{:S(2)}, u32[]{:S(2)}) collective-permute-start(bf16[2,64,1024]{2,1,0:T(8,128)(2,1)S(1)} %pad_maximum_fusion.5.block), channel_id=1, source_target_pairs={{0,6},{2,0},{4,2},{6,4},{1,7},{3,1},{5,3},{7,5},{8,14},{10,8},{12,... | collective-permute-start | bytes 786440 | tf_op jit(solution)/shard_map/ppermute | solution.py:26
  16.1 6.3 %collective-permute-done.3 = bf16[2,64,1024]{2,1,0:T(8,128)(2,1)S(1)} collective-permute-done((bf16[2,64,1024]{2,1,0:T(8,128)(2,1)S(1)}, bf16[2,64,1024]{2,1,0:T(8,128)(2,1)S(1)}, u32[]{:S(2)}, u32[]{:S(2)}) %collective-permute-start.3) | collective-permute-done | bytes 262176 | tf_op jit(solution)/shard_map/ppermute | solution.py:26
  24.2 5.4 %collective-permute-start.13 = (bf16[512,4096]{1,0:T(8,128)(2,1)}, bf16[512,4096]{1,0:T(8,128)(2,1)}, u32[]{:S(2)}, u32[]{:S(2)}) collective-permute-start(bf16[512,4096]{1,0:T(8,128)(2,1)} %bitcast.114), channel_id=1, source_target_pairs={{0,1},{1,0},{2,3},{3,2},{4,5},{5,4},{6,7},{7,6},{8,9},{9,8},{10,11... | collective-permute-start | bytes 12582920 | tf_op jit(solution)/shard_map/ppermute | solution.py:30
  29.7 2.8 %collective-permute-start.10 = (bf16[2,2,64,1024]{3,2,1,0:T(8,128)(2,1)S(1)}, bf16[2,2,64,1024]{3,2,1,0:T(8,128)(2,1)S(1)}, u32[]{:S(2)}, u32[]{:S(2)}) collective-permute-start(bf16[2,2,64,1024]{3,2,1,0:T(8,128)(2,1)S(1)} %pad_maximum_fusion.4.zs), channel_id=1, source_target_pairs={{0,24},{8,0},{16,8},{24,16},{1,25},{9,1},{17,9},{25,17},{2,26},{10... | collective-permute-start | bytes 1572872 | tf_op jit(solution)/shard_map/ppermute | solution.py:26
  35.0 2.2 %copy-done.3 = bf16[1,4096,512]{2,1,0:T(8,128)(2,1)S(1)} copy-done((bf16[1,4096,512]{2,1,0:T(8,128)(2,1)S(1)}, bf16[1,4096,512]{2,1,0:T(8,128)(2,1)}, u32[]{:S(2)}) %copy-start.3) | copy-done | bytes 4194328
  37.7 3.3 %copy-done.1 = bf16[2,4096,512]{2,1,0:T(8,128)(2,1)} copy-done((bf16[2,4096,512]{2,1,0:T(8,128)(2,1)}, bf16[2,4096,512]{2,1,0:T(8,128)(2,1)S(1)}, u32[]{:S(2)}) %copy-start.1) | copy-done | bytes 8388632
  43.8 3.1 %collective-permute-done.9.sp = bf16[2,2,64,1024]{3,2,1,0:T(8,128)(2,1)S(1)} collective-permute-done((bf16[2,2,64,1024]{3,2,1,0:T(8,128)(2,1)S(1)}, bf16[2,2,64,1024]{3,2,1,0:T(8,128)(2,1)S(1)}, u32[]{:S(2)}, u32[]{:S(2)}) %collective-permute-start.9) | collective-permute-done | bytes 524320 | tf_op jit(solution)/shard_map/ppermute | solution.py:26
  52.3 2.3 %copy-done.4 = bf16[1,512,4096]{2,1,0:T(8,128)(2,1)S(1)} copy-done((bf16[1,512,4096]{2,1,0:T(8,128)(2,1)S(1)}, bf16[1,512,4096]{2,1,0:T(8,128)(2,1)}, u32[]{:S(2)}) %copy-start.4) | copy-done | bytes 4194328
  54.6 2.8 %shard_map.74 = (bf16[2,512,4096]{2,1,0:T(8,128)(2,1)S(1)}, f32[8,128]{1,0:T(8,128)S(1)}) custom-call(bf16[512,4096]{1,0:T(8,128)(2,1)S(1)} %bitcast.115, bf16[512,4096]{1,0:T(8,128)(2,1)} %collective-permute-done.13.other), custom_call_target="tpu_custom_call" | custom-call | bytes 16777216 | tf_op jit(solution)/shard_map/pallas_call | solution.py:201
  57.5 3.1 %collective-permute-done.12.mr = bf16[4,64,1024]{2,1,0:T(8,128)(2,1)S(1)} collective-permute-done((bf16[4,64,1024]{2,1,0:T(8,128)(2,1)}, bf16[4,64,1024]{2,1,0:T(8,128)(2,1)S(1)}, u32[]{:S(2)}, u32[]{:S(2)}) %collective-permute-start.12) | collective-permute-done | bytes 524320 | tf_op jit(solution)/shard_map/ppermute | solution.py:26
  64.1 7.3 %shard_map.75.near = bf16[6,64,1024]{2,1,0:T(8,128)(2,1)S(1)} custom-call(s32[2]{0:T(128)S(1)} %fusion.19.place, bf16[2,64,1024]{2,1,0:T(8,128)(2,1)S(1)} %pad_maximum_fusion.5.block, bf16[2,2,64,1024]{3,2,1,0:T(8,128)(2,1)S(1)} %pad_maximum_fusion.4.zs, bf16[2,64,1024]{2,1,0:T(8,128)(2,1)S(1)} %pad_maximum_fusion.8.zz, ...), custom_call_target="tpu_custom_call" | custom-call | flops 805306368 | bytes 1048576 | tf_op jit(solution)/shard_map/pallas_call | solution.py:174
  71.5 4.9 %shard_map.76 = (bf16[2,1,64,1024]{3,2,1,0:T(8,128)(2,1)S(1)}, bf16[2,1,64,1024]{3,2,1,0:T(8,128)(2,1)S(1)}, bf16[1,64,1024]{2,1,0:T(8,128)(2,1)S(1)}, bf16[1,64...) custom-call(s32[2]{0:T(128)S(1)} %fusion.19.place, ...), custom_call_target="tpu_custom_call" | custom-call | flops 536870912 | bytes 1048576 | tf_op jit(solution)/shard_map/pallas_call | solution.py:174
  76.5 2.7 %collective-permute-start.17 = (bf16[2,1,64,1024]{3,2,1,0:T(8,128)(2,1)S(1)}, bf16[2,1,64,1024]{3,2,1,0:T(8,128)(2,1)S(1)}, u32[]{:S(2)}, u32[]{:S(2)}) collective-permute-start(bf16[2,1,64,1024]{3,2,1,0:T(8,128)(2,1)S(1)} %get-tuple-element.96), channel_id=1, source_target_pairs={{0,24},{8,0},{16,8},{24,16},{1,25},{9,1},{17,9},{25,17},{2,26},{10... | collective-permute-start | bytes 786440 | tf_op jit(solution)/shard_map/ppermute | solution.py:26
  79.1 3.4 %shard_map.78 = (bf16[2,2,64,1024]{3,2,1,0:T(8,128)(2,1)S(1)}, bf16[2,2,64,1024]{3,2,1,0:T(8,128)(2,1)S(1)}, bf16[2,64,1024]{2,1,0:T(8,128)(2,1)S(1)}, bf16[2,64...) custom-call(s32[2]{0:T(128)S(1)} %fusion.19.place, bf16[8,64,1024]{2,1,0:T(8,128)(2,1)S(1)} %get-tuple-element.100.hid, ...), custom_call_target="tpu_custom_call" | custom-call | flops 536870912 | bytes 1048576 | tf_op jit(solution)/shard_map/pallas_call | solution.py:174
  82.6 2.7 %collective-permute-start.19 = (bf16[2,2,64,1024]{3,2,1,0:T(8,128)(2,1)S(1)}, bf16[2,2,64,1024]{3,2,1,0:T(8,128)(2,1)S(1)}, u32[]{:S(2)}, u32[]{:S(2)}) collective-permute-start(bf16[2,2,64,1024]{3,2,1,0:T(8,128)(2,1)S(1)} %get-tuple-element.106), channel_id=1, source_target_pairs={{0,24},{8,0},{16,8},{24,16},{1,25},{9,1},{17,9},{25,17},{2,26},{10... | collective-permute-start | bytes 1572872 | tf_op jit(solution)/shard_map/ppermute | solution.py:26
  89.1 6.9 %collective-permute-done.27 = bf16[1,64,1024]{2,1,0:T(8,128)(2,1)S(1)} collective-permute-done((bf16[1,64,1024]{2,1,0:T(8,128)(2,1)S(1)}, bf16[1,64,1024]{2,1,0:T(8,128)(2,1)S(1)}, u32[]{:S(2)}, u32[]{:S(2)}) %collective-permute-start.27) | collective-permute-done | bytes 131104 | tf_op jit(solution)/shard_map/ppermute | solution.py:26
  99.7 2.6 %collective-permute-start.21 = (bf16[2,1,64,1024]{3,2,1,0:T(8,128)(2,1)S(1)}, bf16[2,1,64,1024]{3,2,1,0:T(8,128)(2,1)S(1)}, u32[]{:S(2)}, u32[]{:S(2)}) collective-permute-start(bf16[2,1,64,1024]{3,2,1,0:T(8,128)(2,1)S(1)} %get-tuple-element.110), channel_id=1, source_target_pairs={{0,24},{8,0},{16,8},{24,16},{1,25},{9,1},{17,9},{25,17},{2,26},{10... | collective-permute-start | bytes 786440 | tf_op jit(solution)/shard_map/ppermute | solution.py:26
  106.1 2.8 %collective-permute-start.23 = (bf16[1,64,1024]{2,1,0:T(8,128)(2,1)S(1)}, bf16[1,64,1024]{2,1,0:T(8,128)(2,1)S(1)}, u32[]{:S(2)}, u32[]{:S(2)}) collective-permute-start(bf16[1,64,1024]{2,1,0:T(8,128)(2,1)S(1)} %fusion.13), channel_id=1, source_target_pairs={{0,24},{8,0},{16,8},{24,16},{1,25},{9,1},{17,9},{25,17},{2,26},{10... | collective-permute-start | bytes 393224 | tf_op jit(solution)/shard_map/ppermute | solution.py:26
  108.9 3.5 %collective-permute-done.24 = bf16[2,64,1024]{2,1,0:T(8,128)(2,1)S(1)} collective-permute-done((bf16[2,64,1024]{2,1,0:T(8,128)(2,1)S(1)}, bf16[2,64,1024]{2,1,0:T(8,128)(2,1)S(1)}, u32[]{:S(2)}, u32[]{:S(2)}) %collective-permute-start.24) | collective-permute-done | bytes 262176 | tf_op jit(solution)/shard_map/ppermute | solution.py:26
  115.5 5.0 %collective-permute-done.22 = bf16[1,64,1024]{2,1,0:T(8,128)(2,1)S(1)} collective-permute-done((bf16[1,64,1024]{2,1,0:T(8,128)(2,1)S(1)}, bf16[1,64,1024]{2,1,0:T(8,128)(2,1)S(1)}, u32[]{:S(2)}, u32[]{:S(2)}) %collective-permute-start.22) | collective-permute-done | bytes 131104 | tf_op jit(solution)/shard_map/ppermute | solution.py:26
  122.6 5.3 %collective-permute-done.30 = bf16[2,1,64,1024]{3,2,1,0:T(8,128)(2,1)S(1)} collective-permute-done((bf16[2,1,64,1024]{3,2,1,0:T(8,128)(2,1)S(1)}, bf16[2,1,64,1024]{3,2,1,0:T(8,128)(2,1)S(1)}, u32[]{:S(2)}, u32[]{:S(2)}) %collective-permute-start.30) | collective-permute-done | bytes 262176 | tf_op jit(solution)/shard_map/ppermute | solution.py:26
  128.3 7.0 %collective-permute-start.33 = (bf16[2,64,512]{2,1,0:T(8,128)(2,1)S(1)}, bf16[2,64,512]{2,1,0:T(8,128)(2,1)S(1)}, u32[]{:S(2)}, u32[]{:S(2)}) collective-permute-start(bf16[2,64,512]{2,1,0:T(8,128)(2,1)S(1)} %get-tuple-element.142), channel_id=1, source_target_pairs={{0,33},{1,32},{32,65},{33,64},{64,97},{65,96},{96,129},{97,128},{1... | collective-permute-start | bytes 393224 | tf_op jit(solution)/shard_map/ppermute | solution.py:38
  135.3 6.1 %collective-permute-done.33 = bf16[2,64,512]{2,1,0:T(8,128)(2,1)S(1)} collective-permute-done((bf16[2,64,512]{2,1,0:T(8,128)(2,1)S(1)}, bf16[2,64,512]{2,1,0:T(8,128)(2,1)S(1)}, u32[]{:S(2)}, u32[]{:S(2)}) %collective-permute-start.33) | collective-permute-done | bytes 131104 | tf_op jit(solution)/shard_map/ppermute | solution.py:38
  (112 shorter events, 41.9 us)
Async XLA Ops:
  6.6 17.6 %collective-permute-start.6 = (bf16[4096,512]{1,0:T(8,128)(2,1)}, bf16[4096,512]{1,0:T(8,128)(2,1)S(1)}, u32[]{:S(2)}, u32[]{:S(2)}) collective-permute-start(bf16[4096,512]{1,0:T(8,128)(2,1)} %bitcast.112), channel_id=1, source_target_pairs={{0,1},{1,0},{2,3},{3,2},{4,5},{5,4},{6,7},{7,6},{8,9},{9,8},{10,11... | collective-permute-start | bytes 12582920 | tf_op jit(solution)/shard_map/ppermute | solution.py:30
  7.6 8.5 %collective-permute-start.4 = (bf16[2,64,1024]{2,1,0:T(8,128)(2,1)S(1)}, bf16[2,64,1024]{2,1,0:T(8,128)(2,1)S(1)}, u32[]{:S(2)}, u32[]{:S(2)}) collective-permute-start(bf16[2,64,1024]{2,1,0:T(8,128)(2,1)S(1)} %pad_maximum_fusion.5.block), channel_id=1, source_target_pairs={{0,8},{8,16},{16,24},{24,0},{1,9},{9,17},{17,25},{25,1},{2,10},{10... | collective-permute-start | bytes 786440 | tf_op jit(solution)/shard_map/ppermute | solution.py:26
  8.3 14.0 %collective-permute-start.3 = (bf16[2,64,1024]{2,1,0:T(8,128)(2,1)S(1)}, bf16[2,64,1024]{2,1,0:T(8,128)(2,1)S(1)}, u32[]{:S(2)}, u32[]{:S(2)}) collective-permute-start(bf16[2,64,1024]{2,1,0:T(8,128)(2,1)S(1)} %pad_maximum_fusion.5.block), channel_id=1, source_target_pairs={{0,6},{2,0},{4,2},{6,4},{1,7},{3,1},{5,3},{7,5},{8,14},{10,8},{12,... | collective-permute-start | bytes 786440 | tf_op jit(solution)/shard_map/ppermute | solution.py:26
  13.6 10.6 %collective-permute-start.2 = (bf16[2,64,1024]{2,1,0:T(8,128)(2,1)S(1)}, bf16[2,64,1024]{2,1,0:T(8,128)(2,1)S(1)}, u32[]{:S(2)}, u32[]{:S(2)}) collective-permute-start(bf16[2,64,1024]{2,1,0:T(8,128)(2,1)S(1)} %pad_maximum_fusion.5.block), channel_id=1, source_target_pairs={{0,2},{2,4},{4,6},{6,0},{1,3},{3,5},{5,7},{7,1},{8,10},{10,12},{12... | collective-permute-start | bytes 786440 | tf_op jit(solution)/shard_map/ppermute | solution.py:26
  24.2 28.1 %collective-permute-start.13 = (bf16[512,4096]{1,0:T(8,128)(2,1)}, bf16[512,4096]{1,0:T(8,128)(2,1)}, u32[]{:S(2)}, u32[]{:S(2)}) collective-permute-start(bf16[512,4096]{1,0:T(8,128)(2,1)} %bitcast.114), channel_id=1, source_target_pairs={{0,1},{1,0},{2,3},{3,2},{4,5},{5,4},{6,7},{7,6},{8,9},{9,8},{10,11... | collective-permute-start | bytes 12582920 | tf_op jit(solution)/shard_map/ppermute | solution.py:30
  29.7 14.1 %collective-permute-start.10 = (bf16[2,2,64,1024]{3,2,1,0:T(8,128)(2,1)S(1)}, bf16[2,2,64,1024]{3,2,1,0:T(8,128)(2,1)S(1)}, u32[]{:S(2)}, u32[]{:S(2)}) collective-permute-start(bf16[2,2,64,1024]{3,2,1,0:T(8,128)(2,1)S(1)} %pad_maximum_fusion.4.zs), channel_id=1, source_target_pairs={{0,24},{8,0},{16,8},{24,16},{1,25},{9,1},{17,9},{25,17},{2,26},{10... | collective-permute-start | bytes 1572872 | tf_op jit(solution)/shard_map/ppermute | solution.py:26
  32.4 14.4 %collective-permute-start.9 = (bf16[2,2,64,1024]{3,2,1,0:T(8,128)(2,1)S(1)}, bf16[2,2,64,1024]{3,2,1,0:T(8,128)(2,1)S(1)}, u32[]{:S(2)}, u32[]{:S(2)}) collective-permute-start(bf16[2,2,64,1024]{3,2,1,0:T(8,128)(2,1)S(1)} %pad_maximum_fusion.4.zs), channel_id=1, source_target_pairs={{0,8},{8,16},{16,24},{24,0},{1,9},{9,17},{17,25},{25,1},{2,10},{10... | collective-permute-start | bytes 1572872 | tf_op jit(solution)/shard_map/ppermute | solution.py:26
  32.5 8.6 %collective-permute-start.8 = (bf16[64,1024]{1,0:T(8,128)(2,1)S(1)}, bf16[64,1024]{1,0:T(8,128)(2,1)S(1)}, u32[]{:S(2)}, u32[]{:S(2)}) collective-permute-start(bf16[64,1024]{1,0:T(8,128)(2,1)S(1)} %slice_bitcast_fusion.8), channel_id=1, source_target_pairs={{0,6},{2,0},{4,2},{6,4},{1,7},{3,1},{5,3},{7,5},{8,14},{10,8},{12,... | collective-permute-start | bytes 393224 | tf_op jit(solution)/shard_map/ppermute | solution.py:26
  33.0 9.4 %collective-permute-start.7 = (bf16[64,1024]{1,0:T(8,128)(2,1)S(1)}, bf16[64,1024]{1,0:T(8,128)(2,1)S(1)}, u32[]{:S(2)}, u32[]{:S(2)}) collective-permute-start(bf16[64,1024]{1,0:T(8,128)(2,1)S(1)} %slice_bitcast_fusion.9), channel_id=1, source_target_pairs={{0,2},{2,4},{4,6},{6,0},{1,3},{3,5},{5,7},{7,1},{8,10},{10,12},{12... | collective-permute-start | bytes 393224 | tf_op jit(solution)/shard_map/ppermute | solution.py:26
  48.0 12.5 %collective-permute-start.12 = (bf16[4,64,1024]{2,1,0:T(8,128)(2,1)}, bf16[4,64,1024]{2,1,0:T(8,128)(2,1)S(1)}, u32[]{:S(2)}, u32[]{:S(2)}) collective-permute-start(bf16[4,64,1024]{2,1,0:T(8,128)(2,1)} %get-tuple-element.145), channel_id=1, source_target_pairs={{0,24},{8,0},{16,8},{24,16},{1,25},{9,1},{17,9},{25,17},{2,26},{10... | collective-permute-start | bytes 1572872 | tf_op jit(solution)/shard_map/ppermute | solution.py:26
  48.3 13.8 %collective-permute-start.11 = (bf16[4,64,1024]{2,1,0:T(8,128)(2,1)}, bf16[4,64,1024]{2,1,0:T(8,128)(2,1)S(1)}, u32[]{:S(2)}, u32[]{:S(2)}) collective-permute-start(bf16[4,64,1024]{2,1,0:T(8,128)(2,1)} %get-tuple-element.146), channel_id=1, source_target_pairs={{0,8},{8,16},{16,24},{24,0},{1,9},{9,17},{17,25},{25,1},{2,10},{10... | collective-permute-start | bytes 1572872 | tf_op jit(solution)/shard_map/ppermute | solution.py:26
  62.2 9.2 %collective-permute-start.15 = (bf16[2,64,1024]{2,1,0:T(8,128)(2,1)S(1)}, bf16[2,64,1024]{2,1,0:T(8,128)(2,1)S(1)}, u32[]{:S(2)}, u32[]{:S(2)}) collective-permute-start(bf16[2,64,1024]{2,1,0:T(8,128)(2,1)S(1)} %pad_maximum_fusion.7), channel_id=1, source_target_pairs={{0,24},{8,0},{16,8},{24,16},{1,25},{9,1},{17,9},{25,17},{2,26},{10... | collective-permute-start | bytes 786440 | tf_op jit(solution)/shard_map/ppermute | solution.py:26
  62.6 8.8 %collective-permute-start.14 = (bf16[2,64,1024]{2,1,0:T(8,128)(2,1)S(1)}, bf16[2,64,1024]{2,1,0:T(8,128)(2,1)S(1)}, u32[]{:S(2)}, u32[]{:S(2)}) collective-permute-start(bf16[2,64,1024]{2,1,0:T(8,128)(2,1)S(1)} %pad_maximum_fusion.6), channel_id=1, source_target_pairs={{0,8},{8,16},{16,24},{24,0},{1,9},{9,17},{17,25},{25,1},{2,10},{10... | collective-permute-start | bytes 786440 | tf_op jit(solution)/shard_map/ppermute | solution.py:26
  76.4 8.9 %collective-permute-start.16 = (bf16[2,1,64,1024]{3,2,1,0:T(8,128)(2,1)S(1)}, bf16[2,1,64,1024]{3,2,1,0:T(8,128)(2,1)S(1)}, u32[]{:S(2)}, u32[]{:S(2)}) collective-permute-start(bf16[2,1,64,1024]{3,2,1,0:T(8,128)(2,1)S(1)} %get-tuple-element.95), channel_id=1, source_target_pairs={{0,8},{8,16},{16,24},{24,0},{1,9},{9,17},{17,25},{25,1},{2,10},{10... | collective-permute-start | bytes 786440 | tf_op jit(solution)/shard_map/ppermute | solution.py:26
  76.5 8.8 %collective-permute-start.17 = (bf16[2,1,64,1024]{3,2,1,0:T(8,128)(2,1)S(1)}, bf16[2,1,64,1024]{3,2,1,0:T(8,128)(2,1)S(1)}, u32[]{:S(2)}, u32[]{:S(2)}) collective-permute-start(bf16[2,1,64,1024]{3,2,1,0:T(8,128)(2,1)S(1)} %get-tuple-element.96), channel_id=1, source_target_pairs={{0,24},{8,0},{16,8},{24,16},{1,25},{9,1},{17,9},{25,17},{2,26},{10... | collective-permute-start | bytes 786440 | tf_op jit(solution)/shard_map/ppermute | solution.py:26
  82.5 17.0 %collective-permute-start.18 = (bf16[2,2,64,1024]{3,2,1,0:T(8,128)(2,1)S(1)}, bf16[2,2,64,1024]{3,2,1,0:T(8,128)(2,1)S(1)}, u32[]{:S(2)}, u32[]{:S(2)}) collective-permute-start(bf16[2,2,64,1024]{3,2,1,0:T(8,128)(2,1)S(1)} %get-tuple-element.105), channel_id=1, source_target_pairs={{0,8},{8,16},{16,24},{24,0},{1,9},{9,17},{17,25},{25,1},{2,10},{10... | collective-permute-start | bytes 1572872 | tf_op jit(solution)/shard_map/ppermute | solution.py:26
  82.6 16.9 %collective-permute-start.19 = (bf16[2,2,64,1024]{3,2,1,0:T(8,128)(2,1)S(1)}, bf16[2,2,64,1024]{3,2,1,0:T(8,128)(2,1)S(1)}, u32[]{:S(2)}, u32[]{:S(2)}) collective-permute-start(bf16[2,2,64,1024]{3,2,1,0:T(8,128)(2,1)S(1)} %get-tuple-element.106), channel_id=1, source_target_pairs={{0,24},{8,0},{16,8},{24,16},{1,25},{9,1},{17,9},{25,17},{2,26},{10... | collective-permute-start | bytes 1572872 | tf_op jit(solution)/shard_map/ppermute | solution.py:26
  85.3 10.6 %collective-permute-start.27 = (bf16[1,64,1024]{2,1,0:T(8,128)(2,1)S(1)}, bf16[1,64,1024]{2,1,0:T(8,128)(2,1)S(1)}, u32[]{:S(2)}, u32[]{:S(2)}) collective-permute-start(bf16[1,64,1024]{2,1,0:T(8,128)(2,1)S(1)} %fusion.11), channel_id=1, source_target_pairs={{0,24},{8,0},{16,8},{24,16},{1,25},{9,1},{17,9},{25,17},{2,26},{10... | collective-permute-start | bytes 393224 | tf_op jit(solution)/shard_map/ppermute | solution.py:26
  85.7 11.2 %collective-permute-start.26 = (bf16[1,64,1024]{2,1,0:T(8,128)(2,1)S(1)}, bf16[1,64,1024]{2,1,0:T(8,128)(2,1)S(1)}, u32[]{:S(2)}, u32[]{:S(2)}) collective-permute-start(bf16[1,64,1024]{2,1,0:T(8,128)(2,1)S(1)} %fusion.12), channel_id=1, source_target_pairs={{0,8},{8,16},{16,24},{24,0},{1,9},{9,17},{17,25},{25,1},{2,10},{10... | collective-permute-start | bytes 393224 | tf_op jit(solution)/shard_map/ppermute | solution.py:26
  103.6 8.8 %collective-permute-start.24 = (bf16[2,64,1024]{2,1,0:T(8,128)(2,1)S(1)}, bf16[2,64,1024]{2,1,0:T(8,128)(2,1)S(1)}, u32[]{:S(2)}, u32[]{:S(2)}) collective-permute-start(bf16[2,64,1024]{2,1,0:T(8,128)(2,1)S(1)} %fusion.2), channel_id=1, source_target_pairs={{0,8},{8,16},{16,24},{24,0},{1,9},{9,17},{17,25},{25,1},{2,10},{10... | collective-permute-start | bytes 786440 | tf_op jit(solution)/shard_map/ppermute | solution.py:26
  106.1 9.4 %collective-permute-start.23 = (bf16[1,64,1024]{2,1,0:T(8,128)(2,1)S(1)}, bf16[1,64,1024]{2,1,0:T(8,128)(2,1)S(1)}, u32[]{:S(2)}, u32[]{:S(2)}) collective-permute-start(bf16[1,64,1024]{2,1,0:T(8,128)(2,1)S(1)} %fusion.13), channel_id=1, source_target_pairs={{0,24},{8,0},{16,8},{24,16},{1,25},{9,1},{17,9},{25,17},{2,26},{10... | collective-permute-start | bytes 393224 | tf_op jit(solution)/shard_map/ppermute | solution.py:26
  112.8 9.8 %collective-permute-start.31 = (bf16[2,1,64,1024]{3,2,1,0:T(8,128)(2,1)S(1)}, bf16[2,1,64,1024]{3,2,1,0:T(8,128)(2,1)S(1)}, u32[]{:S(2)}, u32[]{:S(2)}) collective-permute-start(bf16[2,1,64,1024]{3,2,1,0:T(8,128)(2,1)S(1)} %pad_maximum_fusion.10), channel_id=1, source_target_pairs={{0,6},{2,0},{4,2},{6,4},{1,7},{3,1},{5,3},{7,5},{8,14},{10,8},{12,... | collective-permute-start | bytes 786440 | tf_op jit(solution)/shard_map/ppermute | solution.py:26
  114.5 13.3 %collective-permute-start.30 = (bf16[2,1,64,1024]{3,2,1,0:T(8,128)(2,1)S(1)}, bf16[2,1,64,1024]{3,2,1,0:T(8,128)(2,1)S(1)}, u32[]{:S(2)}, u32[]{:S(2)}) collective-permute-start(bf16[2,1,64,1024]{3,2,1,0:T(8,128)(2,1)S(1)} %pad_maximum_fusion.9), channel_id=1, source_target_pairs={{0,2},{2,4},{4,6},{6,0},{1,3},{3,5},{5,7},{7,1},{8,10},{10,12},{12... | collective-permute-start | bytes 786440 | tf_op jit(solution)/shard_map/ppermute | solution.py:26
  128.3 13.1 %collective-permute-start.33 = (bf16[2,64,512]{2,1,0:T(8,128)(2,1)S(1)}, bf16[2,64,512]{2,1,0:T(8,128)(2,1)S(1)}, u32[]{:S(2)}, u32[]{:S(2)}) collective-permute-start(bf16[2,64,512]{2,1,0:T(8,128)(2,1)S(1)} %get-tuple-element.142), channel_id=1, source_target_pairs={{0,33},{1,32},{32,65},{33,64},{64,97},{65,96},{96,129},{97,128},{1... | collective-permute-start | bytes 393224 | tf_op jit(solution)/shard_map/ppermute | solution.py:38
  (20 other events, 262.0 us)

commit v2 on v1

v2 whole, which is shorter than its diff:
```python
import jax
import jax.numpy as jnp
from jax import lax
from jax.experimental import pallas as pl
from jax.experimental.pallas import tpu as pltpu
from jax.sharding import Mesh
from jax.sharding import PartitionSpec as P

BATCH = 2
RING = 4
TILE = 64
PART = 1024
HALF = PART // 2
UNITS = 512
STEP = 256
ROWS = 16
UNROLL = 4
EPS = 1e-05
MIB = 1024 * 1024
LIMIT = 8
COST = 4
BYTES = MIB


def sent(block, axis, distance):
    return lax.ppermute(block, axis, [(i, (i + distance) % RING) for i in range(RING)])


def swapped(block):
    return lax.ppermute(block, "core", [(0, 1), (1, 0)])


def next_section(block, cross):
    pairs = []
    for section in range(8):
        for core in range(2):
            pairs.append((section * 2 + core, (section + 1) % 8 * 2 + (core ^ cross)))
    return lax.ppermute(block, ("y", "zl", "core"), pairs)


def added(*terms):
    return sum(t.astype(jnp.float32) for t in terms).astype(jnp.bfloat16)


def normalize(pieces, z, gain, bias, normed, at, rows):
    def some(i, _):
        start = pl.multiple_of(i * ROWS, ROWS)
        values = [read(start).astype(jnp.float32) for read in pieces]
        mean = sum(jnp.sum(v, axis=-1, keepdims=True) for v in values) / (RING * PART)
        centered = [v - mean for v in values]
        spread = sum(jnp.sum(v * v, axis=-1, keepdims=True) for v in centered) / (RING * PART)
        scale = lax.rsqrt(spread + EPS)
        for k in range(RING):
            true = (z + k) & 3
            value = centered[k] * scale * gain[pl.ds(true, 1), :] + bias[pl.ds(true, 1), :]
            normed[true, pl.ds(at + start, ROWS), :] = value.astype(jnp.bfloat16)
        return 0

    lax.fori_loop(0, rows // ROWS, some, 0, unroll=UNROLL)


def reader(ref, *lead):
    return lambda start: ref[(*lead, pl.ds(start, ROWS), slice(None))]


def halves(ref, *lead):
    return lambda start: ref[(*lead, start // TILE, pl.ds(pl.multiple_of(start % TILE, ROWS), ROWS), slice(None))]


def up(normed, ups, b_up, store):
    def some(n, _):
        columns = pl.ds(pl.multiple_of((n & 1) * STEP, STEP), STEP)
        pre = b_up[pl.ds(n >> 1, 1), columns]
        for k in range(RING):
            pre = pre + jnp.dot(
                normed[k], ups[n >> 1, pl.ds(k * PART, PART), columns], preferred_element_type=jnp.float32
            )
        store(pl.ds(pl.multiple_of(n * STEP, STEP), STEP), jax.nn.gelu(pre, approximate=True).astype(jnp.bfloat16))
        return 0

    lax.fori_loop(0, 2 * UNITS // STEP, some, 0)


def near_kernel(place, block, zs, zz, xm, sm, qm, xp, sp, qp, gain, bias, b_up, ups, hidden, normed):
    z = place[1]
    for slot, (a, b, c) in enumerate(((block, zs, zz), (xm, sm, qm), (xp, sp, qp))):
        pieces = [halves(a), halves(b, 1), halves(c), halves(b, 0)]
        normalize(pieces, z, gain, bias, normed, slot * 2 * TILE, 2 * TILE)

    def store(columns, value):
        for tile in range(6):
            hidden[tile, :, columns] = value[tile * TILE : (tile + 1) * TILE]

    up(normed, ups, b_up, store)


def down(z, rows, downs, store):
    def some(i, _):
        n, t = i >> 1, i & 1
        k = jnp.where(n == 0, 2, jnp.where(n == 3, 0, 2 * n - 1))
        start = pl.ds(pl.multiple_of(((z + k) & 3) * PART + t * HALF, HALF), HALF)
        value = rows()
        term = jnp.dot(value[:, :UNITS], downs[0, :, start], preferred_element_type=jnp.float32)
        term = term + jnp.dot(value[:, UNITS:], downs[1, :, start], preferred_element_type=jnp.float32)
        store(n, pl.ds(pl.multiple_of(t * HALF, HALF), HALF), term.astype(jnp.bfloat16))
        return 0

    lax.fori_loop(0, RING * PART // HALF, some, 0)


def far_kernel(place, ml, mr, gain, bias, b_up, near, ups, downs, plus, minus, hid, normed):
    x, z = place[0], place[1]

    def home(j, half):
        row = (x + j) & 3
        dest = ((row & 1) * 2 + half - x) & 3
        return (dest ^ (dest >> 1)) * 2 + (row >> 1)

    for half, a in enumerate((ml, mr)):
        pieces = [reader(a, 3), reader(a, 1), reader(a, 2), reader(a, 0)]
        normalize(pieces, z, gain, bias, normed, half * TILE, TILE)
    for slot, j in enumerate((0, 1, 3)):
        for half in range(2):
            hid[home(j, half)] = near[slot * 2 + half]

    def store(columns, value):
        for half in range(2):
            hid[home(2, half), :, columns] = value[half * TILE : (half + 1) * TILE]

    up(normed, ups, b_up, store)

    def send(n, columns, value):
        plus[n, :, columns] = value[:TILE]
        minus[n, :, columns] = value[TILE:]

    down(z, lambda: hid[6:8].reshape(2 * TILE, 2 * UNITS), downs, send)


def rest_kernel(place, hid, downs, block, xm, ml, mr, xp, own, plus, minus, resid):
    x, z = place[0], place[1]
    for seq in range(2):
        row, half = 2 * seq + (x >> 1), x & 1
        j = (row - x) & 3
        for at, ref in ((0, block), (1, xm), (3, xp)):

            @pl.when(j == at)
            def _(ref=ref):
                resid[seq] = ref[half]

        @pl.when((j == 2) & (half == 0))
        def _():
            resid[seq] = ml[3]

        @pl.when((j == 2) & (half == 1))
        def _():
            resid[seq] = mr[3]

    def store(n, columns, value):
        for k, ref in enumerate((own, plus, minus)):
            for seq in range(2):
                at = (k * 2 + seq) * TILE
                ref[seq, n, :, columns] = value[at : at + TILE]

    down(z, lambda: hid[0:6].reshape(6 * TILE, 2 * UNITS), downs, store)


VMEM = pl.BlockSpec(memory_space=pltpu.VMEM)
SMEM = pl.BlockSpec(memory_space=pltpu.SMEM)


def call(kernel, out_shape, scratch, flops, *operands):
    return pl.pallas_call(
        kernel,
        in_specs=[SMEM] + [VMEM] * (len(operands) - 1),
        out_specs=[VMEM] * len(out_shape),
        out_shape=out_shape,
        scratch_shapes=scratch,
        compiler_params=pltpu.CompilerParams(vmem_limit_bytes=LIMIT * MIB),
        cost_estimate=pl.CostEstimate(flops=flops // COST, bytes_accessed=BYTES, transcendentals=0),
    )(*operands)


def load_kernel(own, other, after, out, token, sems):
    del after
    copies = [pltpu.make_async_copy(ref, out.at[i], sems.at[i]) for i, ref in enumerate((own, other))]
    for copy in copies:
        copy.start()
    token[...] = jnp.zeros_like(token)
    for copy in copies:
        copy.wait()


def loaded(own, other, after):
    return pl.pallas_call(
        load_kernel,
        in_specs=[pl.BlockSpec(memory_space=pltpu.HBM)] * 2 + [pl.BlockSpec(memory_space=pl.ANY)],
        out_specs=[VMEM, VMEM],
        out_shape=[pltpu.VMEM((2, *own.shape), own.dtype), jax.ShapeDtypeStruct((8, 128), jnp.float32)],
        scratch_shapes=[pltpu.SemaphoreType.DMA((2,))],
        compiler_params=pltpu.CompilerParams(vmem_limit_bytes=LIMIT * MIB),
        cost_estimate=pl.CostEstimate(flops=0, bytes_accessed=16 * MIB, transcendentals=0),
    )(own, other, after)


def compute(place, far_place, near, block, xm, xp, ml, mr, gain, bias, b_all, ups, downs):
    mul = 2 * 2 * UNITS * RING * PART
    far = call(
        far_kernel,
        [jax.ShapeDtypeStruct((RING, TILE, PART), jnp.bfloat16)] * 2
        + [jax.ShapeDtypeStruct((8, TILE, 2 * UNITS), jnp.bfloat16)],
        [pltpu.VMEM((RING, 2 * TILE, PART), jnp.bfloat16)],
        4 * TILE * mul,
        far_place, ml, mr, gain, bias, b_all, near, ups, downs,
    )
    rest = call(
        rest_kernel,
        [jax.ShapeDtypeStruct((2, RING, TILE, PART), jnp.bfloat16)] * 3
        + [jax.ShapeDtypeStruct((2, TILE, PART), jnp.bfloat16)],
        [],
        6 * TILE * mul,
        place, far[2], downs, block, xm, ml, mr, xp,
    )
    return far[:2], rest


def shards(acts, ln_gain, ln_bias, w_up, b_up, w_down, b_down):
    x, z, core = (lax.axis_index(a) for a in ("x", "zh", "core"))
    place = jnp.stack([x, z]).astype(jnp.int32)
    up_o, down_o = w_up[0], w_down[0]
    gain, bias = ln_gain[0].reshape(RING, PART), ln_bias[0].reshape(RING, PART)

    split = acts[0].reshape(2, 2, TILE, HALF)
    mine = lax.dynamic_index_in_dim(split, core, 1, keepdims=False)
    theirs = lax.dynamic_index_in_dim(split, 1 - core, 1, keepdims=False)
    got, b_up_s = lax.optimization_barrier((swapped(theirs), swapped(b_up)))
    low = jnp.where(core == 0, mine, got)
    high = jnp.where(core == 0, got, mine)
    block = jnp.concatenate([low, high], axis=-1)
    block, up_o = lax.optimization_barrier((block, up_o))
    b_all = jnp.concatenate([b_up, b_up_s], axis=0)

    zp, zm = sent(block, "zh", 1), sent(block, "zh", -1)
    xp, xm = sent(block, "x", 1), sent(block, "x", -1)
    up_s = swapped(up_o)
    zp, zm, xp, xm, up_s, down_o = lax.optimization_barrier((zp, zm, xp, xm, up_s, down_o))
    zs = jnp.stack([zp, zm])
    sp, sm = sent(zs, "x", 1), sent(zs, "x", -1)
    za, zb = sent(zp[0], "zh", 1), sent(zm[1], "zh", -1)
    za, zb = lax.optimization_barrier((za, zb))
    zz = jnp.stack([za, zb])
    qp, qm = sent(zz, "x", 1), sent(zz, "x", -1)
    down_s = swapped(down_o)
    ups, token = loaded(up_o, up_s, b_all)
    sp, sm, qp, qm, xp, xm, token = lax.optimization_barrier((sp, sm, qp, qm, xp, xm, token))
    place = place + token[0, :2].astype(jnp.int32)
    ml = sent(jnp.stack([sp[0, 0], sp[1, 0], qp[0], xp[0]]), "x", 1)
    mr = sent(jnp.stack([sm[0, 1], sm[1, 1], qm[1], xm[1]]), "x", -1)
    near = call(
        near_kernel,
        [jax.ShapeDtypeStruct((6, TILE, 2 * UNITS), jnp.bfloat16)],
        [pltpu.VMEM((RING, 6 * TILE, PART), jnp.bfloat16)],
        6 * TILE * 4 * UNITS * RING * PART,
        place, block, zs, zz, xm, sm, qm, xp, sp, qp, gain, bias, b_all, ups,
    )[0]
    downs, token = loaded(down_o, down_s, near)
    far_place = place + token[0, :2].astype(jnp.int32)

    (far_l, far_r), (own, plus, minus, resid) = compute(
        place, far_place, near, block, xm, xp, ml, mr, gain, bias, b_all, ups, downs
    )
    l, r = lax.optimization_barrier((sent(far_l, "x", 1), sent(far_r, "x", -1)))

    def over_x(first, last):
        to_left = jnp.stack([added(plus[0, first:last], l[first:last]), plus[1, first:last]])
        to_right = jnp.stack([minus[0, first:last], added(minus[1, first:last], r[first:last])])
        return lax.optimization_barrier((sent(to_left, "x", 1), sent(to_right, "x", -1)))

    fl2, fr2 = over_x(0, 1)
    fl1, fr1 = over_x(1, 3)
    fl0, fr0 = over_x(3, 4)
    s2 = added(own[:, 0], fl2[:, 0], fr2[:, 0])
    zl, zr = lax.optimization_barrier((sent(s2[0], "zh", 1), sent(s2[1], "zh", -1)))
    t = added(own[:, 1:3], fl1, fr1)
    zfl = sent(jnp.stack([added(t[0, 0], zl), t[1, 0]]), "zh", 1)
    zfr = sent(jnp.stack([t[0, 1], added(t[1, 1], zr)]), "zh", -1)
    zfl, zfr, fl0, fr0 = lax.optimization_barrier((zfl, zfr, fl0, fr0))
    shift = lax.dynamic_slice_in_dim(b_down[0], z * PART, PART, 0)
    value = added(own[:, 3], fl0[:, 0], fr0[:, 0], zfl, zfr, resid, shift)
    low, high = value[..., :HALF], value[..., HALF:]
    keep = next_section(jnp.where(core == 0, low, high), 0)
    cross = next_section(jnp.where(core == 0, high, low), 1)
    out = jnp.stack([jnp.where(core == 0, keep, cross), jnp.where(core == 0, cross, keep)], axis=1)
    return out.reshape(1, BATCH, 2 * TILE, HALF)


def solution(mesh):
    fine = Mesh(mesh.devices.reshape(4, 2, 4, 4, 2), ("y", "zl", "x", "zh", "core"))
    section, rows, hid = ("y", "zl"), "x", ("zh", "core")
    in_specs = (
        P(section, rows, hid),
        P(section, None),
        P(section, None),
        P(section, None, ("x", "zh", "core")),
        P(section, ("x", "zh", "core")),
        P(section, ("x", "zh", "core"), None),
        P(section, None),
    )
    out_specs = P(section, None, rows, hid)
    return jax.shard_map(shards, mesh=fine, in_specs=in_specs, out_specs=out_specs, check_vma=False)
```

time: 142 us -> 138 us (0.972)
  waiting for transfers between devices: 54.3 us -> 42.9 us
  starting transfers between devices: 50.7 us -> 58.1 us
    ppermute x28 -> x24, waiting for transfers between devices: 46.9 us -> 34.8 us  [sent(): lax.ppermute(block, axis, [(i, (i + distance) % RING) for i in range(RING)])]
    ppermute x2, starting transfers between devices: 7.04 us -> 18.3 us  [next_section(): return lax.ppermute(block, ('y', 'zl', 'core'), pairs)]
    ppermute x4, starting transfers between devices: 9.14 us -> 4.62 us  [swapped(): return lax.ppermute(block, 'core', [(0, 1), (1, 0)])]
    unnamed x2, other arithmetic: 1.2 us -> 2.73 us
    unnamed x21 -> x11, local copies, waits for them, and re-layouts: 8.35 us -> 6.89 us
    pallas_call x4 -> x3, Pallas kernels: 17.6 us -> 18.6 us  [call(): pl.pallas_call(kernel, in_specs=[SMEM] + [VMEM] * (len(operands) - 1), ou...]
    ppermute x28 -> x24, starting transfers between devices: 34.5 us -> 35.1 us  [sent(): lax.ppermute(block, axis, [(i, (i + distance) % RING) for i in range(RING)])]
  transfers between devices with their start and end apart: 34 -> 30, of which waited for: 20 -> 14; matrix products, arithmetic and copies ran while one was open for 3% -> 4% of each run, Pallas kernels for 11% -> 11%
where the time goes in v2:
time: 138 us
  starting transfers between devices  58.1 us (42%)
  waiting for transfers between devices  42.9 us (31%)
  Pallas kernels  21.6 us (16%)
  local copies, waits for them, and re-layouts  8.86 us (6%)
  other arithmetic  6.12 us (4%)
    ppermute x24, starting transfers between devices, sent(): lax.ppermute(block, axis, [(i, (i + distance) % RING) for i in range(RING)])  35.1 us
    ppermute x24, waiting for transfers between devices, sent(): lax.ppermute(block, axis, [(i, (i + distance) % RING) for i in range(RING)])  34.8 us
    pallas_call x3, Pallas kernels, call(): pl.pallas_call(kernel, in_specs=[SMEM] + [VMEM] * (len(operands) - 1), ou...  18.6 us
    ppermute x2, starting transfers between devices, next_section(): return lax.ppermute(block, ('y', 'zl', 'core'), pairs)  18.3 us
    unnamed x11, local copies, waits for them, and re-layouts  6.89 us
    ppermute x2, waiting for transfers between devices, next_section(): return lax.ppermute(block, ('y', 'zl', 'core'), pairs)  6.8 us
    ppermute x4, starting transfers between devices, swapped(): return lax.ppermute(block, 'core', [(0, 1), (1, 0)])  4.62 us
    pallas_call x2, Pallas kernels, loaded(): pl.pallas_call(load_kernel, in_specs=[pl.BlockSpec(memory_space=pltpu.HBM...  3.06 us
  transfers between devices with their start and end apart: 30, of which 14 were waited for; matrix products, arithmetic and copies ran while one was open for 4% of the time, Pallas kernels for 11%

profile of v2, /device:TPU:1, one launch (start us, length us, event | category | flops | bytes accessed | tf_op | source)
XLA Modules:
  0.0 138.0 jit_solution(3440653033270900905)
XLA Ops:
  0.9 3.3 %collective-permute-start = (bf16[2,64,512]{2,1,0:T(8,128)(2,1)S(1)}, bf16[2,64,512]{2,1,0:T(8,128)(2,1)S(1)}, u32[]{:S(2)}, u32[]{:S(2)}) collective-permute-start(bf16[2,64,512]{2,1,0:T(8,128)(2,1)S(1)} %dynamic-slice_bitcast_fusion), channel_id=1, source_target_pairs={{0,1},{1,0},{2,3},{3,2},{4,5},{5,4},{6,7},{7,6},{8,9},{9,8},{10,11... | collective-permute-start | bytes 393224 | tf_op jit(solution)/shard_map/ppermute | solution.py:30
  8.1 3.0 %collective-permute-start.3 = (bf16[2,64,1024]{2,1,0:T(8,128)(2,1)S(1)}, bf16[2,64,1024]{2,1,0:T(8,128)(2,1)S(1)}, u32[]{:S(2)}, u32[]{:S(2)}) collective-permute-start(bf16[2,64,1024]{2,1,0:T(8,128)(2,1)S(1)} %pad_maximum_fusion.5.block), channel_id=1, source_target_pairs={{0,6},{2,0},{4,2},{6,4},{1,7},{3,1},{5,3},{7,5},{8,14},{10,8},{12,... | collective-permute-start | bytes 786440 | tf_op jit(solution)/shard_map/ppermute | solution.py:26
  13.8 5.3 %collective-permute-done.2 = bf16[2,64,1024]{2,1,0:T(8,128)(2,1)S(1)} collective-permute-done((bf16[2,64,1024]{2,1,0:T(8,128)(2,1)S(1)}, bf16[2,64,1024]{2,1,0:T(8,128)(2,1)S(1)}, u32[]{:S(2)}, u32[]{:S(2)}) %collective-permute-start.2) | collective-permute-done | bytes 262176 | tf_op jit(solution)/shard_map/ppermute | solution.py:26
  19.2 5.1 %collective-permute-done.3 = bf16[2,64,1024]{2,1,0:T(8,128)(2,1)S(1)} collective-permute-done((bf16[2,64,1024]{2,1,0:T(8,128)(2,1)S(1)}, bf16[2,64,1024]{2,1,0:T(8,128)(2,1)S(1)}, u32[]{:S(2)}, u32[]{:S(2)}) %collective-permute-start.3) | collective-permute-done | bytes 262176 | tf_op jit(solution)/shard_map/ppermute | solution.py:26
  30.0 2.5 %collective-permute-start.10 = (bf16[64,1024]{1,0:T(8,128)(2,1)S(1)}, bf16[64,1024]{1,0:T(8,128)(2,1)S(1)}, u32[]{:S(2)}, u32[]{:S(2)}) collective-permute-start(bf16[64,1024]{1,0:T(8,128)(2,1)S(1)} %slice_bitcast_fusion.10), channel_id=1, source_target_pairs={{0,6},{2,0},{4,2},{6,4},{1,7},{3,1},{5,3},{7,5},{8,14},{10,8},{12,... | collective-permute-start | bytes 393224 | tf_op jit(solution)/shard_map/ppermute | solution.py:26
  33.7 6.6 %collective-permute-done.10 = bf16[64,1024]{1,0:T(8,128)(2,1)S(1)} collective-permute-done((bf16[64,1024]{1,0:T(8,128)(2,1)S(1)}, bf16[64,1024]{1,0:T(8,128)(2,1)S(1)}, u32[]{:S(2)}, u32[]{:S(2)}) %collective-permute-start.10) | collective-permute-done | bytes 131104 | tf_op jit(solution)/shard_map/ppermute | solution.py:26
  40.7 2.7 %collective-permute-start.12 = (bf16[2,64,1024]{2,1,0:T(8,128)(2,1)S(1)}, bf16[2,64,1024]{2,1,0:T(8,128)(2,1)S(1)}, u32[]{:S(2)}, u32[]{:S(2)}) collective-permute-start(bf16[2,64,1024]{2,1,0:T(8,128)(2,1)S(1)} %pad_maximum_fusion.6.zz), channel_id=1, source_target_pairs={{0,24},{8,0},{16,8},{24,16},{1,25},{9,1},{17,9},{25,17},{2,26},{10... | collective-permute-start | bytes 786440 | tf_op jit(solution)/shard_map/ppermute | solution.py:26
  49.6 2.2 %copy-done.4 = bf16[4096,512]{1,0:T(8,128)(2,1)S(1)} copy-done((bf16[4096,512]{1,0:T(8,128)(2,1)S(1)}, bf16[4096,512]{1,0:T(8,128)(2,1)}, u32[]{:S(2)}) %copy-start.4) | copy-done | bytes 4194328
  54.5 7.3 %shard_map.74.after.near = bf16[6,64,1024]{2,1,0:T(8,128)(2,1)S(1)} custom-call(s32[2]{0:T(128)S(1)} %add_add_fusion.place, bf16[2,64,1024]{2,1,0:T(8,128)(2,1)S(1)} %pad_maximum_fusion.5.block, bf16[2,2,64,1024]{3,2,1,0:T(8,128)(2,1)S(1)} %pad_maximum_fusion.zs, bf16[2,64,1024]{2,1,0:T(8,128)(2,1)S(1)} %pad_maximum_fusion.6.zz, ...), custom_call_target="tpu_custom_call" | custom-call | flops 805306368 | bytes 1048576 | tf_op jit(solution)/shard_map/pallas_call | solution.py:172
  61.8 2.5 %shard_map.75 = (bf16[2,512,4096]{2,1,0:T(8,128)(2,1)S(1)}, f32[8,128]{1,0:T(8,128)S(1)}) custom-call(bf16[512,4096]{1,0:T(8,128)(2,1)S(1)} %bitcast.109, bf16[512,4096]{1,0:T(8,128)(2,1)} %collective-permute-done.13.other, bf16[6,64,1024]{2,1,0:T(8,128)(2,1)S(1)} %shard_map.74.after.near), custom_call_target="tpu_custom_call" | custom-call | bytes 16777216 | tf_op jit(solution)/shard_map/pallas_call | solution.py:194
  64.4 6.0 %shard_map.76 = (bf16[4,64,1024]{2,1,0:T(8,128)(2,1)S(1)}, bf16[4,64,1024]{2,1,0:T(8,128)(2,1)S(1)}, bf16[8,64,1024]{2,1,0:T(8,128)(2,1)S(1)}) custom-call(s32[2]{0:T(128)S(1)} %bitcast_add_fusion.2.place, bf16[4,64,1024]{2,1,0:T(8,128)(2,1)S(1)} %collective-permute-done.14.ml, bf16[4,64,1024]{2,1,0:T(8,128)(2,1)S(1)} %collective-permute-done.15.mr, ...), custom_call_target="tpu_custom_call" | custom-call | flops 536870912 | bytes 1048576 | tf_op jit(solution)/shard_map/pallas_call | solution.py:172
  70.6 2.6 %collective-permute-start.17 = (bf16[4,64,1024]{2,1,0:T(8,128)(2,1)S(1)}, bf16[4,64,1024]{2,1,0:T(8,128)(2,1)S(1)}, u32[]{:S(2)}, u32[]{:S(2)}) collective-permute-start(bf16[4,64,1024]{2,1,0:T(8,128)(2,1)S(1)} %get-tuple-element.76), channel_id=1, source_target_pairs={{0,24},{8,0},{16,8},{24,16},{1,25},{9,1},{17,9},{25,17},{2,26},{10... | collective-permute-start | bytes 1572872 | tf_op jit(solution)/shard_map/ppermute | solution.py:26
  73.2 5.3 %shard_map.77 = (bf16[2,4,64,1024]{3,2,1,0:T(8,128)(2,1)S(1)}, bf16[2,4,64,1024]{3,2,1,0:T(8,128)(2,1)S(1)}, bf16[2,4,64,1024]{3,2,1,0:T(8,128)(2,1)S(1)}, bf16[2,64,1024]{2,1,0:T(8,128)(2,1)S(1)}) custom-call(s32[2]{0:T(128)S(1)} %add_add_fusion.place, bf16[8,64,1024]{2,1,0:T(8,128)(2,1)S(1)} %get-tuple-element.72.hid, ...), custom_call_target="tpu_custom_call" | custom-call | flops 805306368 | bytes 1048576 | tf_op jit(solution)/shard_map/pallas_call | solution.py:172
  78.7 2.3 %collective-permute-done.16 = bf16[4,64,1024]{2,1,0:T(8,128)(2,1)S(1)} collective-permute-done((bf16[4,64,1024]{2,1,0:T(8,128)(2,1)S(1)}, bf16[4,64,1024]{2,1,0:T(8,128)(2,1)S(1)}, u32[]{:S(2)}, u32[]{:S(2)}) %collective-permute-start.16) | collective-permute-done | bytes 524320 | tf_op jit(solution)/shard_map/ppermute | solution.py:26
  81.3 2.5 %collective-permute-start.21 = (bf16[2,1,64,1024]{3,2,1,0:T(8,128)(2,1)S(1)}, bf16[2,1,64,1024]{3,2,1,0:T(8,128)(2,1)S(1)}, u32[]{:S(2)}, u32[]{:S(2)}) collective-permute-start(bf16[2,1,64,1024]{3,2,1,0:T(8,128)(2,1)S(1)} %pad_maximum_fusion.8), channel_id=1, source_target_pairs={{0,24},{8,0},{16,8},{24,16},{1,25},{9,1},{17,9},{25,17},{2,26},{10... | collective-permute-start | bytes 786440 | tf_op jit(solution)/shard_map/ppermute | solution.py:26
  83.9 2.7 %collective-permute-start.19 = (bf16[2,2,64,1024]{3,2,1,0:T(8,128)(2,1)S(1)}, bf16[2,2,64,1024]{3,2,1,0:T(8,128)(2,1)S(1)}, u32[]{:S(2)}, u32[]{:S(2)}) collective-permute-start(bf16[2,2,64,1024]{3,2,1,0:T(8,128)(2,1)S(1)} %pad_maximum_fusion.4), channel_id=1, source_target_pairs={{0,24},{8,0},{16,8},{24,16},{1,25},{9,1},{17,9},{25,17},{2,26},{10... | collective-permute-start | bytes 1572872 | tf_op jit(solution)/shard_map/ppermute | solution.py:26
  87.8 2.5 %collective-permute-done.20 = bf16[2,1,64,1024]{3,2,1,0:T(8,128)(2,1)S(1)} collective-permute-done((bf16[2,1,64,1024]{3,2,1,0:T(8,128)(2,1)S(1)}, bf16[2,1,64,1024]{3,2,1,0:T(8,128)(2,1)S(1)}, u32[]{:S(2)}, u32[]{:S(2)}) %collective-permute-start.20) | collective-permute-done | bytes 262176 | tf_op jit(solution)/shard_map/ppermute | solution.py:26
  90.5 3.7 %collective-permute-start.22 = (bf16[64,1024]{1,0:T(8,128)(2,1)S(1)}, bf16[64,1024]{1,0:T(8,128)(2,1)S(1)}, u32[]{:S(2)}, u32[]{:S(2)}) collective-permute-start(bf16[64,1024]{1,0:T(8,128)(2,1)S(1)} %get-tuple-element.114), channel_id=1, source_target_pairs={{0,2},{2,4},{4,6},{6,0},{1,3},{3,5},{5,7},{7,1},{8,10},{10,12},{12... | collective-permute-start | bytes 393224 | tf_op jit(solution)/shard_map/ppermute | solution.py:26
  96.6 3.7 %collective-permute-done.23 = bf16[64,1024]{1,0:T(8,128)(2,1)S(1)} collective-permute-done((bf16[64,1024]{1,0:T(8,128)(2,1)S(1)}, bf16[64,1024]{1,0:T(8,128)(2,1)S(1)}, u32[]{:S(2)}, u32[]{:S(2)}) %collective-permute-start.23) | collective-permute-done | bytes 131104 | tf_op jit(solution)/shard_map/ppermute | solution.py:26
  102.4 3.2 %collective-permute-start.24 = (bf16[2,64,1024]{2,1,0:T(8,128)(2,1)S(1)}, bf16[2,64,1024]{2,1,0:T(8,128)(2,1)S(1)}, u32[]{:S(2)}, u32[]{:S(2)}) collective-permute-start(bf16[2,64,1024]{2,1,0:T(8,128)(2,1)S(1)} %pad_maximum_fusion.9), channel_id=1, source_target_pairs={{0,2},{2,4},{4,6},{6,0},{1,3},{3,5},{5,7},{7,1},{8,10},{10,12},{12... | collective-permute-start | bytes 786440 | tf_op jit(solution)/shard_map/ppermute | solution.py:26
  106.2 5.2 %collective-permute-done.25 = bf16[2,64,1024]{2,1,0:T(8,128)(2,1)S(1)} collective-permute-done((bf16[2,64,1024]{2,1,0:T(8,128)(2,1)S(1)}, bf16[2,64,1024]{2,1,0:T(8,128)(2,1)S(1)}, u32[]{:S(2)}, u32[]{:S(2)}) %collective-permute-start.25) | collective-permute-done | bytes 262176 | tf_op jit(solution)/shard_map/ppermute | solution.py:26
  112.1 5.4 %collective-permute-start.28 = (bf16[2,64,512]{2,1,0:T(8,128)(2,1)S(1)}, bf16[2,64,512]{2,1,0:T(8,128)(2,1)S(1)}, u32[]{:S(2)}, u32[]{:S(2)}) collective-permute-start(bf16[2,64,512]{2,1,0:T(8,128)(2,1)S(1)} %get-tuple-element.111), channel_id=1, source_target_pairs={{0,32},{1,33},{32,64},{33,65},{64,96},{65,97},{96,128},{97,129},{1... | collective-permute-start | bytes 393224 | tf_op jit(solution)/shard_map/ppermute | solution.py:38
  117.5 12.9 %collective-permute-start.29 = (bf16[2,64,512]{2,1,0:T(8,128)(2,1)S(1)}, bf16[2,64,512]{2,1,0:T(8,128)(2,1)S(1)}, u32[]{:S(2)}, u32[]{:S(2)}) collective-permute-start(bf16[2,64,512]{2,1,0:T(8,128)(2,1)S(1)} %get-tuple-element.112), channel_id=1, source_target_pairs={{0,33},{1,32},{32,65},{33,64},{64,97},{65,96},{96,129},{97,128},{1... | collective-permute-start | bytes 393224 | tf_op jit(solution)/shard_map/ppermute | solution.py:38
  130.5 6.8 %collective-permute-done.29 = bf16[2,64,512]{2,1,0:T(8,128)(2,1)S(1)} collective-permute-done((bf16[2,64,512]{2,1,0:T(8,128)(2,1)S(1)}, bf16[2,64,512]{2,1,0:T(8,128)(2,1)S(1)}, u32[]{:S(2)}, u32[]{:S(2)}) %collective-permute-start.29) | collective-permute-done | bytes 131104 | tf_op jit(solution)/shard_map/ppermute | solution.py:38
  (102 shorter events, 32.3 us)
Async XLA Ops:
  6.6 17.7 %collective-permute-start.6 = (bf16[4096,512]{1,0:T(8,128)(2,1)}, bf16[4096,512]{1,0:T(8,128)(2,1)S(1)}, u32[]{:S(2)}, u32[]{:S(2)}) collective-permute-start(bf16[4096,512]{1,0:T(8,128)(2,1)} %bitcast.110), channel_id=1, source_target_pairs={{0,1},{1,0},{2,3},{3,2},{4,5},{5,4},{6,7},{7,6},{8,9},{9,8},{10,11... | collective-permute-start | bytes 12582920 | tf_op jit(solution)/shard_map/ppermute | solution.py:30
  6.9 12.3 %collective-permute-start.2 = (bf16[2,64,1024]{2,1,0:T(8,128)(2,1)S(1)}, bf16[2,64,1024]{2,1,0:T(8,128)(2,1)S(1)}, u32[]{:S(2)}, u32[]{:S(2)}) collective-permute-start(bf16[2,64,1024]{2,1,0:T(8,128)(2,1)S(1)} %pad_maximum_fusion.5.block), channel_id=1, source_target_pairs={{0,2},{2,4},{4,6},{6,0},{1,3},{3,5},{5,7},{7,1},{8,10},{10,12},{12... | collective-permute-start | bytes 786440 | tf_op jit(solution)/shard_map/ppermute | solution.py:26
  8.1 16.2 %collective-permute-start.3 = (bf16[2,64,1024]{2,1,0:T(8,128)(2,1)S(1)}, bf16[2,64,1024]{2,1,0:T(8,128)(2,1)S(1)}, u32[]{:S(2)}, u32[]{:S(2)}) collective-permute-start(bf16[2,64,1024]{2,1,0:T(8,128)(2,1)S(1)} %pad_maximum_fusion.5.block), channel_id=1, source_target_pairs={{0,6},{2,0},{4,2},{6,4},{1,7},{3,1},{5,3},{7,5},{8,14},{10,8},{12,... | collective-permute-start | bytes 786440 | tf_op jit(solution)/shard_map/ppermute | solution.py:26
  11.2 13.1 %collective-permute-start.4 = (bf16[2,64,1024]{2,1,0:T(8,128)(2,1)S(1)}, bf16[2,64,1024]{2,1,0:T(8,128)(2,1)S(1)}, u32[]{:S(2)}, u32[]{:S(2)}) collective-permute-start(bf16[2,64,1024]{2,1,0:T(8,128)(2,1)S(1)} %pad_maximum_fusion.5.block), channel_id=1, source_target_pairs={{0,8},{8,16},{16,24},{24,0},{1,9},{9,17},{17,25},{25,1},{2,10},{10... | collective-permute-start | bytes 786440 | tf_op jit(solution)/shard_map/ppermute | solution.py:26
  12.4 11.9 %collective-permute-start.5 = (bf16[2,64,1024]{2,1,0:T(8,128)(2,1)S(1)}, bf16[2,64,1024]{2,1,0:T(8,128)(2,1)S(1)}, u32[]{:S(2)}, u32[]{:S(2)}) collective-permute-start(bf16[2,64,1024]{2,1,0:T(8,128)(2,1)S(1)} %pad_maximum_fusion.5.block), channel_id=1, source_target_pairs={{0,24},{8,0},{16,8},{24,16},{1,25},{9,1},{17,9},{25,17},{2,26},{10... | collective-permute-start | bytes 786440 | tf_op jit(solution)/shard_map/ppermute | solution.py:26
  26.3 35.5 %collective-permute-start.13 = (bf16[512,4096]{1,0:T(8,128)(2,1)}, bf16[512,4096]{1,0:T(8,128)(2,1)}, u32[]{:S(2)}, u32[]{:S(2)}) collective-permute-start(bf16[512,4096]{1,0:T(8,128)(2,1)} %bitcast.108), channel_id=1, source_target_pairs={{0,1},{1,0},{2,3},{3,2},{4,5},{5,4},{6,7},{7,6},{8,9},{9,8},{10,11... | collective-permute-start | bytes 12582920 | tf_op jit(solution)/shard_map/ppermute | solution.py:30
  27.2 25.1 %collective-permute-start.7 = (bf16[2,2,64,1024]{3,2,1,0:T(8,128)(2,1)S(1)}, bf16[2,2,64,1024]{3,2,1,0:T(8,128)(2,1)S(1)}, u32[]{:S(2)}, u32[]{:S(2)}) collective-permute-start(bf16[2,2,64,1024]{3,2,1,0:T(8,128)(2,1)S(1)} %pad_maximum_fusion.zs), channel_id=1, source_target_pairs={{0,8},{8,16},{16,24},{24,0},{1,9},{9,17},{17,25},{25,1},{2,10},{10... | collective-permute-start | bytes 1572872 | tf_op jit(solution)/shard_map/ppermute | solution.py:26
  28.5 23.8 %collective-permute-start.8 = (bf16[2,2,64,1024]{3,2,1,0:T(8,128)(2,1)S(1)}, bf16[2,2,64,1024]{3,2,1,0:T(8,128)(2,1)S(1)}, u32[]{:S(2)}, u32[]{:S(2)}) collective-permute-start(bf16[2,2,64,1024]{3,2,1,0:T(8,128)(2,1)S(1)} %pad_maximum_fusion.zs), channel_id=1, source_target_pairs={{0,24},{8,0},{16,8},{24,16},{1,25},{9,1},{17,9},{25,17},{2,26},{10... | collective-permute-start | bytes 1572872 | tf_op jit(solution)/shard_map/ppermute | solution.py:26
  30.0 10.2 %collective-permute-start.10 = (bf16[64,1024]{1,0:T(8,128)(2,1)S(1)}, bf16[64,1024]{1,0:T(8,128)(2,1)S(1)}, u32[]{:S(2)}, u32[]{:S(2)}) collective-permute-start(bf16[64,1024]{1,0:T(8,128)(2,1)S(1)} %slice_bitcast_fusion.10), channel_id=1, source_target_pairs={{0,6},{2,0},{4,2},{6,4},{1,7},{3,1},{5,3},{7,5},{8,14},{10,8},{12,... | collective-permute-start | bytes 393224 | tf_op jit(solution)/shard_map/ppermute | solution.py:26
  32.5 8.1 %collective-permute-start.9 = (bf16[64,1024]{1,0:T(8,128)(2,1)S(1)}, bf16[64,1024]{1,0:T(8,128)(2,1)S(1)}, u32[]{:S(2)}, u32[]{:S(2)}) collective-permute-start(bf16[64,1024]{1,0:T(8,128)(2,1)S(1)} %slice_bitcast_fusion.11), channel_id=1, source_target_pairs={{0,2},{2,4},{4,6},{6,0},{1,3},{3,5},{5,7},{7,1},{8,10},{10,12},{12... | collective-permute-start | bytes 393224 | tf_op jit(solution)/shard_map/ppermute | solution.py:26
  40.6 11.7 %collective-permute-start.11 = (bf16[2,64,1024]{2,1,0:T(8,128)(2,1)S(1)}, bf16[2,64,1024]{2,1,0:T(8,128)(2,1)S(1)}, u32[]{:S(2)}, u32[]{:S(2)}) collective-permute-start(bf16[2,64,1024]{2,1,0:T(8,128)(2,1)S(1)} %pad_maximum_fusion.6.zz), channel_id=1, source_target_pairs={{0,8},{8,16},{16,24},{24,0},{1,9},{9,17},{17,25},{25,1},{2,10},{10... | collective-permute-start | bytes 786440 | tf_op jit(solution)/shard_map/ppermute | solution.py:26
  40.7 11.6 %collective-permute-start.12 = (bf16[2,64,1024]{2,1,0:T(8,128)(2,1)S(1)}, bf16[2,64,1024]{2,1,0:T(8,128)(2,1)S(1)}, u32[]{:S(2)}, u32[]{:S(2)}) collective-permute-start(bf16[2,64,1024]{2,1,0:T(8,128)(2,1)S(1)} %pad_maximum_fusion.6.zz), channel_id=1, source_target_pairs={{0,24},{8,0},{16,8},{24,16},{1,25},{9,1},{17,9},{25,17},{2,26},{10... | collective-permute-start | bytes 786440 | tf_op jit(solution)/shard_map/ppermute | solution.py:26
  52.5 11.9 %collective-permute-start.15 = (bf16[4,64,1024]{2,1,0:T(8,128)(2,1)S(1)}, bf16[4,64,1024]{2,1,0:T(8,128)(2,1)S(1)}, u32[]{:S(2)}, u32[]{:S(2)}) collective-permute-start(bf16[4,64,1024]{2,1,0:T(8,128)(2,1)S(1)} %pad_maximum_fusion.2), channel_id=1, source_target_pairs={{0,24},{8,0},{16,8},{24,16},{1,25},{9,1},{17,9},{25,17},{2,26},{10... | collective-permute-start | bytes 1572872 | tf_op jit(solution)/shard_map/ppermute | solution.py:26
  52.8 11.6 %collective-permute-start.14 = (bf16[4,64,1024]{2,1,0:T(8,128)(2,1)S(1)}, bf16[4,64,1024]{2,1,0:T(8,128)(2,1)S(1)}, u32[]{:S(2)}, u32[]{:S(2)}) collective-permute-start(bf16[4,64,1024]{2,1,0:T(8,128)(2,1)S(1)} %pad_maximum_fusion.1), channel_id=1, source_target_pairs={{0,8},{8,16},{16,24},{24,0},{1,9},{9,17},{17,25},{25,1},{2,10},{10... | collective-permute-start | bytes 1572872 | tf_op jit(solution)/shard_map/ppermute | solution.py:26
  70.4 10.5 %collective-permute-start.16 = (bf16[4,64,1024]{2,1,0:T(8,128)(2,1)S(1)}, bf16[4,64,1024]{2,1,0:T(8,128)(2,1)S(1)}, u32[]{:S(2)}, u32[]{:S(2)}) collective-permute-start(bf16[4,64,1024]{2,1,0:T(8,128)(2,1)S(1)} %get-tuple-element.75), channel_id=1, source_target_pairs={{0,8},{8,16},{16,24},{24,0},{1,9},{9,17},{17,25},{25,1},{2,10},{10... | collective-permute-start | bytes 1572872 | tf_op jit(solution)/shard_map/ppermute | solution.py:26
  70.6 10.4 %collective-permute-start.17 = (bf16[4,64,1024]{2,1,0:T(8,128)(2,1)S(1)}, bf16[4,64,1024]{2,1,0:T(8,128)(2,1)S(1)}, u32[]{:S(2)}, u32[]{:S(2)}) collective-permute-start(bf16[4,64,1024]{2,1,0:T(8,128)(2,1)S(1)} %get-tuple-element.76), channel_id=1, source_target_pairs={{0,24},{8,0},{16,8},{24,16},{1,25},{9,1},{17,9},{25,17},{2,26},{10... | collective-permute-start | bytes 1572872 | tf_op jit(solution)/shard_map/ppermute | solution.py:26
  83.9 16.4 %collective-permute-start.19 = (bf16[2,2,64,1024]{3,2,1,0:T(8,128)(2,1)S(1)}, bf16[2,2,64,1024]{3,2,1,0:T(8,128)(2,1)S(1)}, u32[]{:S(2)}, u32[]{:S(2)}) collective-permute-start(bf16[2,2,64,1024]{3,2,1,0:T(8,128)(2,1)S(1)} %pad_maximum_fusion.4), channel_id=1, source_target_pairs={{0,24},{8,0},{16,8},{24,16},{1,25},{9,1},{17,9},{25,17},{2,26},{10... | collective-permute-start | bytes 1572872 | tf_op jit(solution)/shard_map/ppermute | solution.py:26
  86.8 13.5 %collective-permute-start.18 = (bf16[2,2,64,1024]{3,2,1,0:T(8,128)(2,1)S(1)}, bf16[2,2,64,1024]{3,2,1,0:T(8,128)(2,1)S(1)}, u32[]{:S(2)}, u32[]{:S(2)}) collective-permute-start(bf16[2,2,64,1024]{3,2,1,0:T(8,128)(2,1)S(1)} %pad_maximum_fusion.3), channel_id=1, source_target_pairs={{0,8},{8,16},{16,24},{24,0},{1,9},{9,17},{17,25},{25,1},{2,10},{10... | collective-permute-start | bytes 1572872 | tf_op jit(solution)/shard_map/ppermute | solution.py:26
  94.2 11.4 %collective-permute-start.27 = (bf16[2,1,64,1024]{3,2,0,1:T(8,128)(2,1)S(1)}, bf16[2,1,64,1024]{3,2,0,1:T(8,128)(2,1)S(1)}, u32[]{:S(2)}, u32[]{:S(2)}) collective-permute-start(bf16[2,1,64,1024]{3,2,0,1:T(8,128)(2,1)S(1)} %pad_maximum_fusion.12), channel_id=1, source_target_pairs={{0,24},{8,0},{16,8},{24,16},{1,25},{9,1},{17,9},{25,17},{2,26},{10... | collective-permute-start | bytes 786440 | tf_op jit(solution)/shard_map/ppermute | solution.py:26
  96.6 9.6 %collective-permute-start.26 = (bf16[2,1,64,1024]{3,2,1,0:T(8,128)(2,1)S(1)}, bf16[2,1,64,1024]{3,2,1,0:T(8,128)(2,1)S(1)}, u32[]{:S(2)}, u32[]{:S(2)}) collective-permute-start(bf16[2,1,64,1024]{3,2,1,0:T(8,128)(2,1)S(1)} %pad_maximum_fusion.11), channel_id=1, source_target_pairs={{0,8},{8,16},{16,24},{24,0},{1,9},{9,17},{17,25},{25,1},{2,10},{10... | collective-permute-start | bytes 786440 | tf_op jit(solution)/shard_map/ppermute | solution.py:26
  100.7 10.6 %collective-permute-start.25 = (bf16[2,64,1024]{2,1,0:T(8,128)(2,1)S(1)}, bf16[2,64,1024]{2,1,0:T(8,128)(2,1)S(1)}, u32[]{:S(2)}, u32[]{:S(2)}) collective-permute-start(bf16[2,64,1024]{2,1,0:T(8,128)(2,1)S(1)} %pad_maximum_fusion.10), channel_id=1, source_target_pairs={{0,6},{2,0},{4,2},{6,4},{1,7},{3,1},{5,3},{7,5},{8,14},{10,8},{12,... | collective-permute-start | bytes 786440 | tf_op jit(solution)/shard_map/ppermute | solution.py:26
  102.4 9.4 %collective-permute-start.24 = (bf16[2,64,1024]{2,1,0:T(8,128)(2,1)S(1)}, bf16[2,64,1024]{2,1,0:T(8,128)(2,1)S(1)}, u32[]{:S(2)}, u32[]{:S(2)}) collective-permute-start(bf16[2,64,1024]{2,1,0:T(8,128)(2,1)S(1)} %pad_maximum_fusion.9), channel_id=1, source_target_pairs={{0,2},{2,4},{4,6},{6,0},{1,3},{3,5},{5,7},{7,1},{8,10},{10,12},{12... | collective-permute-start | bytes 786440 | tf_op jit(solution)/shard_map/ppermute | solution.py:26
  112.1 18.3 %collective-permute-start.28 = (bf16[2,64,512]{2,1,0:T(8,128)(2,1)S(1)}, bf16[2,64,512]{2,1,0:T(8,128)(2,1)S(1)}, u32[]{:S(2)}, u32[]{:S(2)}) collective-permute-start(bf16[2,64,512]{2,1,0:T(8,128)(2,1)S(1)} %get-tuple-element.111), channel_id=1, source_target_pairs={{0,32},{1,33},{32,64},{33,65},{64,96},{65,97},{96,128},{97,129},{1... | collective-permute-start | bytes 393224 | tf_op jit(solution)/shard_map/ppermute | solution.py:38
  117.5 19.7 %collective-permute-start.29 = (bf16[2,64,512]{2,1,0:T(8,128)(2,1)S(1)}, bf16[2,64,512]{2,1,0:T(8,128)(2,1)S(1)}, u32[]{:S(2)}, u32[]{:S(2)}) collective-permute-start(bf16[2,64,512]{2,1,0:T(8,128)(2,1)S(1)} %get-tuple-element.112), channel_id=1, source_target_pairs={{0,33},{1,32},{32,65},{33,64},{64,97},{65,96},{96,129},{97,128},{1... | collective-permute-start | bytes 393224 | tf_op jit(solution)/shard_map/ppermute | solution.py:38
  (11 other events, 150.5 us)

commit v3 on v2

--- a/solution.py
+++ b/solution.py
@@ -67,7 +67,7 @@
     return lambda start: ref[(*lead, start // TILE, pl.ds(pl.multiple_of(start % TILE, ROWS), ROWS), slice(None))]
 
 
-def up(normed, ups, b_up, store):
+def up(normed, ups, b_up, store, unroll=1):
     def some(n, _):
         columns = pl.ds(pl.multiple_of((n & 1) * STEP, STEP), STEP)
         pre = b_up[pl.ds(n >> 1, 1), columns]
@@ -78,7 +78,7 @@
         store(pl.ds(pl.multiple_of(n * STEP, STEP), STEP), jax.nn.gelu(pre, approximate=True).astype(jnp.bfloat16))
         return 0
 
-    lax.fori_loop(0, 2 * UNITS // STEP, some, 0)
+    lax.fori_loop(0, 2 * UNITS // STEP, some, 0, unroll=unroll)
 
 
 def near_kernel(place, block, zs, zz, xm, sm, qm, xp, sp, qp, gain, bias, b_up, ups, hidden, normed):
@@ -94,18 +94,20 @@
     up(normed, ups, b_up, store)
 
 
-def down(z, rows, downs, store):
+def down(z, rows, downs, store, wide=HALF, unroll=1):
+    each = PART // wide
+
     def some(i, _):
-        n, t = i >> 1, i & 1
+        n, t = i // each, i % each
         k = jnp.where(n == 0, 2, jnp.where(n == 3, 0, 2 * n - 1))
-        start = pl.ds(pl.multiple_of(((z + k) & 3) * PART + t * HALF, HALF), HALF)
+        start = pl.ds(pl.multiple_of(((z + k) & 3) * PART + t * wide, wide), wide)
         value = rows()
         term = jnp.dot(value[:, :UNITS], downs[0, :, start], preferred_element_type=jnp.float32)
         term = term + jnp.dot(value[:, UNITS:], downs[1, :, start], preferred_element_type=jnp.float32)
-        store(n, pl.ds(pl.multiple_of(t * HALF, HALF), HALF), term.astype(jnp.bfloat16))
+        store(n, pl.ds(pl.multiple_of(t * wide, wide), wide), term.astype(jnp.bfloat16))
         return 0
 
-    lax.fori_loop(0, RING * PART // HALF, some, 0)
+    lax.fori_loop(0, RING * each, some, 0, unroll=unroll)
 
 
 def far_kernel(place, ml, mr, gain, bias, b_up, near, ups, downs, plus, minus, hid, normed):
@@ -127,13 +129,13 @@
         for half in range(2):
             hid[home(2, half), :, columns] = value[half * TILE : (half + 1) * TILE]
 
-    up(normed, ups, b_up, store)
+    up(normed, ups, b_up, store, unroll=4)
 
     def send(n, columns, value):
         plus[n, :, columns] = value[:TILE]
         minus[n, :, columns] = value[TILE:]
 
-    down(z, lambda: hid[6:8].reshape(2 * TILE, 2 * UNITS), downs, send)
+    down(z, lambda: hid[6:8].reshape(2 * TILE, 2 * UNITS), downs, send, unroll=4)
 
 
 def rest_kernel(place, hid, downs, block, xm, ml, mr, xp, own, plus, minus, resid):
@@ -230,9 +232,9 @@
     gain, bias = ln_gain[0].reshape(RING, PART), ln_bias[0].reshape(RING, PART)
 
     split = acts[0].reshape(2, 2, TILE, HALF)
+    got, b_up_s = lax.optimization_barrier((swapped(acts[0]), swapped(b_up)))
     mine = lax.dynamic_index_in_dim(split, core, 1, keepdims=False)
-    theirs = lax.dynamic_index_in_dim(split, 1 - core, 1, keepdims=False)
-    got, b_up_s = lax.optimization_barrier((swapped(theirs), swapped(b_up)))
+    got = lax.dynamic_index_in_dim(got.reshape(2, 2, TILE, HALF), core, 1, keepdims=False)
     low = jnp.where(core == 0, mine, got)
     high = jnp.where(core == 0, got, mine)
     block = jnp.concatenate([low, high], axis=-1)

time: 138 us -> 136 us (0.986)
  Pallas kernels: 21.6 us -> 19.9 us
    pallas_call x3, Pallas kernels: 18.6 us -> 16.8 us  [call(): pl.pallas_call(kernel, in_specs=[SMEM] + [VMEM] * (len(operands) - 1), ou...]
  transfers between devices with their start and end apart: 30 -> 30, of which waited for: 14 -> 14; matrix products, arithmetic and copies ran while one was open for 4% -> 4% of each run, Pallas kernels for 11% -> 12%
where the time goes in v3:
time: 136 us
  starting transfers between devices  58.1 us (43%)
  waiting for transfers between devices  43.1 us (32%)
  Pallas kernels  19.9 us (15%)
  local copies, waits for them, and re-layouts  7.93 us (6%)
  other arithmetic  6.12 us (4%)
    ppermute x24, starting transfers between devices, sent(): lax.ppermute(block, axis, [(i, (i + distance) % RING) for i in range(RING)])  35.2 us
    ppermute x24, waiting for transfers between devices, sent(): lax.ppermute(block, axis, [(i, (i + distance) % RING) for i in range(RING)])  34.8 us
    ppermute x2, starting transfers between devices, next_section(): return lax.ppermute(block, ('y', 'zl', 'core'), pairs)  18.3 us
    pallas_call x3, Pallas kernels, call(): pl.pallas_call(kernel, in_specs=[SMEM] + [VMEM] * (len(operands) - 1), ou...  16.8 us
    unnamed x11, local copies, waits for them, and re-layouts  6.89 us
    ppermute x2, waiting for transfers between devices, next_section(): return lax.ppermute(block, ('y', 'zl', 'core'), pairs)  6.87 us
    ppermute x4, starting transfers between devices, swapped(): return lax.ppermute(block, 'core', [(0, 1), (1, 0)])  4.6 us
    pallas_call x2, Pallas kernels, loaded(): pl.pallas_call(load_kernel, in_specs=[pl.BlockSpec(memory_space=pltpu.HBM...  3.06 us
  transfers between devices with their start and end apart: 30, of which 14 were waited for; matrix products, arithmetic and copies ran while one was open for 4% of the time, Pallas kernels for 12%

profile of v3, /device:TPU:1, one launch (start us, length us, event | category | flops | bytes accessed | tf_op | source)
XLA Modules:
  0.0 135.6 jit_solution(9439432340592814857)
XLA Ops:
  0.0 3.2 %collective-permute-start = (bf16[256,512]{1,0:T(8,128)(2,1)}, bf16[256,512]{1,0:T(8,128)(2,1)S(1)}, u32[]{:S(2)}, u32[]{:S(2)}) collective-permute-start(bf16[256,512]{1,0:T(8,128)(2,1)} %bitcast.123), channel_id=1, source_target_pairs={{0,1},{1,0},{2,3},{3,2},{4,5},{5,4},{6,7},{7,6},{8,9},{9,8},{10,11... | collective-permute-start | bytes 786440 | tf_op jit(solution)/shard_map/ppermute | solution.py:30
  7.3 3.0 %collective-permute-start.3 = (bf16[2,64,1024]{2,1,0:T(8,128)(2,1)S(1)}, bf16[2,64,1024]{2,1,0:T(8,128)(2,1)S(1)}, u32[]{:S(2)}, u32[]{:S(2)}) collective-permute-start(bf16[2,64,1024]{2,1,0:T(8,128)(2,1)S(1)} %pad_maximum_fusion.5.block), channel_id=1, source_target_pairs={{0,6},{2,0},{4,2},{6,4},{1,7},{3,1},{5,3},{7,5},{8,14},{10,8},{12,... | collective-permute-start | bytes 786440 | tf_op jit(solution)/shard_map/ppermute | solution.py:26
  13.0 5.4 %collective-permute-done.2 = bf16[2,64,1024]{2,1,0:T(8,128)(2,1)S(1)} collective-permute-done((bf16[2,64,1024]{2,1,0:T(8,128)(2,1)S(1)}, bf16[2,64,1024]{2,1,0:T(8,128)(2,1)S(1)}, u32[]{:S(2)}, u32[]{:S(2)}) %collective-permute-start.2) | collective-permute-done | bytes 262176 | tf_op jit(solution)/shard_map/ppermute | solution.py:26
  18.5 5.0 %collective-permute-done.3 = bf16[2,64,1024]{2,1,0:T(8,128)(2,1)S(1)} collective-permute-done((bf16[2,64,1024]{2,1,0:T(8,128)(2,1)S(1)}, bf16[2,64,1024]{2,1,0:T(8,128)(2,1)S(1)}, u32[]{:S(2)}, u32[]{:S(2)}) %collective-permute-start.3) | collective-permute-done | bytes 262176 | tf_op jit(solution)/shard_map/ppermute | solution.py:26
  29.2 2.5 %collective-permute-start.10 = (bf16[64,1024]{1,0:T(8,128)(2,1)S(1)}, bf16[64,1024]{1,0:T(8,128)(2,1)S(1)}, u32[]{:S(2)}, u32[]{:S(2)}) collective-permute-start(bf16[64,1024]{1,0:T(8,128)(2,1)S(1)} %slice_bitcast_fusion.10), channel_id=1, source_target_pairs={{0,6},{2,0},{4,2},{6,4},{1,7},{3,1},{5,3},{7,5},{8,14},{10,8},{12,... | collective-permute-start | bytes 393224 | tf_op jit(solution)/shard_map/ppermute | solution.py:26
  32.9 6.6 %collective-permute-done.10 = bf16[64,1024]{1,0:T(8,128)(2,1)S(1)} collective-permute-done((bf16[64,1024]{1,0:T(8,128)(2,1)S(1)}, bf16[64,1024]{1,0:T(8,128)(2,1)S(1)}, u32[]{:S(2)}, u32[]{:S(2)}) %collective-permute-start.10) | collective-permute-done | bytes 131104 | tf_op jit(solution)/shard_map/ppermute | solution.py:26
  39.9 2.7 %collective-permute-start.12 = (bf16[2,64,1024]{2,1,0:T(8,128)(2,1)S(1)}, bf16[2,64,1024]{2,1,0:T(8,128)(2,1)S(1)}, u32[]{:S(2)}, u32[]{:S(2)}) collective-permute-start(bf16[2,64,1024]{2,1,0:T(8,128)(2,1)S(1)} %pad_maximum_fusion.6.zz), channel_id=1, source_target_pairs={{0,24},{8,0},{16,8},{24,16},{1,25},{9,1},{17,9},{25,17},{2,26},{10... | collective-permute-start | bytes 786440 | tf_op jit(solution)/shard_map/ppermute | solution.py:26
  48.7 2.2 %copy-done.4 = bf16[4096,512]{1,0:T(8,128)(2,1)S(1)} copy-done((bf16[4096,512]{1,0:T(8,128)(2,1)S(1)}, bf16[4096,512]{1,0:T(8,128)(2,1)}, u32[]{:S(2)}) %copy-start.4) | copy-done | bytes 4194328
  53.7 7.3 %shard_map.74.after.near = bf16[6,64,1024]{2,1,0:T(8,128)(2,1)S(1)} custom-call(s32[2]{0:T(128)S(1)} %add_add_fusion.place, bf16[2,64,1024]{2,1,0:T(8,128)(2,1)S(1)} %pad_maximum_fusion.5.block, bf16[2,2,64,1024]{3,2,1,0:T(8,128)(2,1)S(1)} %pad_maximum_fusion.zs, bf16[2,64,1024]{2,1,0:T(8,128)(2,1)S(1)} %pad_maximum_fusion.6.zz, ...), custom_call_target="tpu_custom_call" | custom-call | flops 805306368 | bytes 1048576 | tf_op jit(solution)/shard_map/pallas_call | solution.py:174
  61.0 2.5 %shard_map.75 = (bf16[2,512,4096]{2,1,0:T(8,128)(2,1)S(1)}, f32[8,128]{1,0:T(8,128)S(1)}) custom-call(bf16[512,4096]{1,0:T(8,128)(2,1)S(1)} %bitcast.116, bf16[512,4096]{1,0:T(8,128)(2,1)} %collective-permute-done.13.other, bf16[6,64,1024]{2,1,0:T(8,128)(2,1)S(1)} %shard_map.74.after.near), custom_call_target="tpu_custom_call" | custom-call | bytes 16777216 | tf_op jit(solution)/shard_map/pallas_call | solution.py:196
  63.6 4.3 %shard_map.76 = (bf16[4,64,1024]{2,1,0:T(8,128)(2,1)S(1)}, bf16[4,64,1024]{2,1,0:T(8,128)(2,1)S(1)}, bf16[8,64,1024]{2,1,0:T(8,128)(2,1)S(1)}) custom-call(s32[2]{0:T(128)S(1)} %bitcast_add_fusion.2.place, bf16[4,64,1024]{2,1,0:T(8,128)(2,1)S(1)} %collective-permute-done.14.ml, bf16[4,64,1024]{2,1,0:T(8,128)(2,1)S(1)} %collective-permute-done.15.mr, ...), custom_call_target="tpu_custom_call" | custom-call | flops 536870912 | bytes 1048576 | tf_op jit(solution)/shard_map/pallas_call | solution.py:174
  68.1 2.6 %collective-permute-start.17 = (bf16[4,64,1024]{2,1,0:T(8,128)(2,1)S(1)}, bf16[4,64,1024]{2,1,0:T(8,128)(2,1)S(1)}, u32[]{:S(2)}, u32[]{:S(2)}) collective-permute-start(bf16[4,64,1024]{2,1,0:T(8,128)(2,1)S(1)} %get-tuple-element.76), channel_id=1, source_target_pairs={{0,24},{8,0},{16,8},{24,16},{1,25},{9,1},{17,9},{25,17},{2,26},{10... | collective-permute-start | bytes 1572872 | tf_op jit(solution)/shard_map/ppermute | solution.py:26
  70.6 5.3 %shard_map.77 = (bf16[2,4,64,1024]{3,2,1,0:T(8,128)(2,1)S(1)}, bf16[2,4,64,1024]{3,2,1,0:T(8,128)(2,1)S(1)}, bf16[2,4,64,1024]{3,2,1,0:T(8,128)(2,1)S(1)}, bf16[2,64,1024]{2,1,0:T(8,128)(2,1)S(1)}) custom-call(s32[2]{0:T(128)S(1)} %add_add_fusion.place, bf16[8,64,1024]{2,1,0:T(8,128)(2,1)S(1)} %get-tuple-element.72.hid, ...), custom_call_target="tpu_custom_call" | custom-call | flops 805306368 | bytes 1048576 | tf_op jit(solution)/shard_map/pallas_call | solution.py:174
  76.1 2.3 %collective-permute-done.16 = bf16[4,64,1024]{2,1,0:T(8,128)(2,1)S(1)} collective-permute-done((bf16[4,64,1024]{2,1,0:T(8,128)(2,1)S(1)}, bf16[4,64,1024]{2,1,0:T(8,128)(2,1)S(1)}, u32[]{:S(2)}, u32[]{:S(2)}) %collective-permute-start.16) | collective-permute-done | bytes 524320 | tf_op jit(solution)/shard_map/ppermute | solution.py:26
  78.7 2.5 %collective-permute-start.21 = (bf16[2,1,64,1024]{3,2,1,0:T(8,128)(2,1)S(1)}, bf16[2,1,64,1024]{3,2,1,0:T(8,128)(2,1)S(1)}, u32[]{:S(2)}, u32[]{:S(2)}) collective-permute-start(bf16[2,1,64,1024]{3,2,1,0:T(8,128)(2,1)S(1)} %pad_maximum_fusion.8), channel_id=1, source_target_pairs={{0,24},{8,0},{16,8},{24,16},{1,25},{9,1},{17,9},{25,17},{2,26},{10... | collective-permute-start | bytes 786440 | tf_op jit(solution)/shard_map/ppermute | solution.py:26
  81.4 2.7 %collective-permute-start.19 = (bf16[2,2,64,1024]{3,2,1,0:T(8,128)(2,1)S(1)}, bf16[2,2,64,1024]{3,2,1,0:T(8,128)(2,1)S(1)}, u32[]{:S(2)}, u32[]{:S(2)}) collective-permute-start(bf16[2,2,64,1024]{3,2,1,0:T(8,128)(2,1)S(1)} %pad_maximum_fusion.4), channel_id=1, source_target_pairs={{0,24},{8,0},{16,8},{24,16},{1,25},{9,1},{17,9},{25,17},{2,26},{10... | collective-permute-start | bytes 1572872 | tf_op jit(solution)/shard_map/ppermute | solution.py:26
  85.2 2.5 %collective-permute-done.20 = bf16[2,1,64,1024]{3,2,1,0:T(8,128)(2,1)S(1)} collective-permute-done((bf16[2,1,64,1024]{3,2,1,0:T(8,128)(2,1)S(1)}, bf16[2,1,64,1024]{3,2,1,0:T(8,128)(2,1)S(1)}, u32[]{:S(2)}, u32[]{:S(2)}) %collective-permute-start.20) | collective-permute-done | bytes 262176 | tf_op jit(solution)/shard_map/ppermute | solution.py:26
  87.9 3.7 %collective-permute-start.22 = (bf16[64,1024]{1,0:T(8,128)(2,1)S(1)}, bf16[64,1024]{1,0:T(8,128)(2,1)S(1)}, u32[]{:S(2)}, u32[]{:S(2)}) collective-permute-start(bf16[64,1024]{1,0:T(8,128)(2,1)S(1)} %get-tuple-element.114), channel_id=1, source_target_pairs={{0,2},{2,4},{4,6},{6,0},{1,3},{3,5},{5,7},{7,1},{8,10},{10,12},{12... | collective-permute-start | bytes 393224 | tf_op jit(solution)/shard_map/ppermute | solution.py:26
  94.0 3.8 %collective-permute-done.23 = bf16[64,1024]{1,0:T(8,128)(2,1)S(1)} collective-permute-done((bf16[64,1024]{1,0:T(8,128)(2,1)S(1)}, bf16[64,1024]{1,0:T(8,128)(2,1)S(1)}, u32[]{:S(2)}, u32[]{:S(2)}) %collective-permute-start.23) | collective-permute-done | bytes 131104 | tf_op jit(solution)/shard_map/ppermute | solution.py:26
  99.9 3.2 %collective-permute-start.24 = (bf16[2,64,1024]{2,1,0:T(8,128)(2,1)S(1)}, bf16[2,64,1024]{2,1,0:T(8,128)(2,1)S(1)}, u32[]{:S(2)}, u32[]{:S(2)}) collective-permute-start(bf16[2,64,1024]{2,1,0:T(8,128)(2,1)S(1)} %pad_maximum_fusion.9), channel_id=1, source_target_pairs={{0,2},{2,4},{4,6},{6,0},{1,3},{3,5},{5,7},{7,1},{8,10},{10,12},{12... | collective-permute-start | bytes 786440 | tf_op jit(solution)/shard_map/ppermute | solution.py:26
  103.6 5.4 %collective-permute-done.25 = bf16[2,64,1024]{2,1,0:T(8,128)(2,1)S(1)} collective-permute-done((bf16[2,64,1024]{2,1,0:T(8,128)(2,1)S(1)}, bf16[2,64,1024]{2,1,0:T(8,128)(2,1)S(1)}, u32[]{:S(2)}, u32[]{:S(2)}) %collective-permute-start.25) | collective-permute-done | bytes 262176 | tf_op jit(solution)/shard_map/ppermute | solution.py:26
  109.6 5.4 %collective-permute-start.28 = (bf16[2,64,512]{2,1,0:T(8,128)(2,1)S(1)}, bf16[2,64,512]{2,1,0:T(8,128)(2,1)S(1)}, u32[]{:S(2)}, u32[]{:S(2)}) collective-permute-start(bf16[2,64,512]{2,1,0:T(8,128)(2,1)S(1)} %get-tuple-element.111), channel_id=1, source_target_pairs={{0,32},{1,33},{32,64},{33,65},{64,96},{65,97},{96,128},{97,129},{1... | collective-permute-start | bytes 393224 | tf_op jit(solution)/shard_map/ppermute | solution.py:38
  115.0 12.9 %collective-permute-start.29 = (bf16[2,64,512]{2,1,0:T(8,128)(2,1)S(1)}, bf16[2,64,512]{2,1,0:T(8,128)(2,1)S(1)}, u32[]{:S(2)}, u32[]{:S(2)}) collective-permute-start(bf16[2,64,512]{2,1,0:T(8,128)(2,1)S(1)} %get-tuple-element.112), channel_id=1, source_target_pairs={{0,33},{1,32},{32,65},{33,64},{64,97},{65,96},{96,129},{97,128},{1... | collective-permute-start | bytes 393224 | tf_op jit(solution)/shard_map/ppermute | solution.py:38
  127.9 6.9 %collective-permute-done.29 = bf16[2,64,512]{2,1,0:T(8,128)(2,1)S(1)} collective-permute-done((bf16[2,64,512]{2,1,0:T(8,128)(2,1)S(1)}, bf16[2,64,512]{2,1,0:T(8,128)(2,1)S(1)}, u32[]{:S(2)}, u32[]{:S(2)}) %collective-permute-start.29) | collective-permute-done | bytes 131104 | tf_op jit(solution)/shard_map/ppermute | solution.py:38
  (101 shorter events, 31.3 us)
Async XLA Ops:
  5.6 17.9 %collective-permute-start.6 = (bf16[4096,512]{1,0:T(8,128)(2,1)}, bf16[4096,512]{1,0:T(8,128)(2,1)S(1)}, u32[]{:S(2)}, u32[]{:S(2)}) collective-permute-start(bf16[4096,512]{1,0:T(8,128)(2,1)} %bitcast.117), channel_id=1, source_target_pairs={{0,1},{1,0},{2,3},{3,2},{4,5},{5,4},{6,7},{7,6},{8,9},{9,8},{10,11... | collective-permute-start | bytes 12582920 | tf_op jit(solution)/shard_map/ppermute | solution.py:30
  6.0 12.4 %collective-permute-start.2 = (bf16[2,64,1024]{2,1,0:T(8,128)(2,1)S(1)}, bf16[2,64,1024]{2,1,0:T(8,128)(2,1)S(1)}, u32[]{:S(2)}, u32[]{:S(2)}) collective-permute-start(bf16[2,64,1024]{2,1,0:T(8,128)(2,1)S(1)} %pad_maximum_fusion.5.block), channel_id=1, source_target_pairs={{0,2},{2,4},{4,6},{6,0},{1,3},{3,5},{5,7},{7,1},{8,10},{10,12},{12... | collective-permute-start | bytes 786440 | tf_op jit(solution)/shard_map/ppermute | solution.py:26
  7.3 16.2 %collective-permute-start.3 = (bf16[2,64,1024]{2,1,0:T(8,128)(2,1)S(1)}, bf16[2,64,1024]{2,1,0:T(8,128)(2,1)S(1)}, u32[]{:S(2)}, u32[]{:S(2)}) collective-permute-start(bf16[2,64,1024]{2,1,0:T(8,128)(2,1)S(1)} %pad_maximum_fusion.5.block), channel_id=1, source_target_pairs={{0,6},{2,0},{4,2},{6,4},{1,7},{3,1},{5,3},{7,5},{8,14},{10,8},{12,... | collective-permute-start | bytes 786440 | tf_op jit(solution)/shard_map/ppermute | solution.py:26
  10.3 13.2 %collective-permute-start.4 = (bf16[2,64,1024]{2,1,0:T(8,128)(2,1)S(1)}, bf16[2,64,1024]{2,1,0:T(8,128)(2,1)S(1)}, u32[]{:S(2)}, u32[]{:S(2)}) collective-permute-start(bf16[2,64,1024]{2,1,0:T(8,128)(2,1)S(1)} %pad_maximum_fusion.5.block), channel_id=1, source_target_pairs={{0,8},{8,16},{16,24},{24,0},{1,9},{9,17},{17,25},{25,1},{2,10},{10... | collective-permute-start | bytes 786440 | tf_op jit(solution)/shard_map/ppermute | solution.py:26
  11.5 11.9 %collective-permute-start.5 = (bf16[2,64,1024]{2,1,0:T(8,128)(2,1)S(1)}, bf16[2,64,1024]{2,1,0:T(8,128)(2,1)S(1)}, u32[]{:S(2)}, u32[]{:S(2)}) collective-permute-start(bf16[2,64,1024]{2,1,0:T(8,128)(2,1)S(1)} %pad_maximum_fusion.5.block), channel_id=1, source_target_pairs={{0,24},{8,0},{16,8},{24,16},{1,25},{9,1},{17,9},{25,17},{2,26},{10... | collective-permute-start | bytes 786440 | tf_op jit(solution)/shard_map/ppermute | solution.py:26
  25.5 35.5 %collective-permute-start.13 = (bf16[512,4096]{1,0:T(8,128)(2,1)}, bf16[512,4096]{1,0:T(8,128)(2,1)}, u32[]{:S(2)}, u32[]{:S(2)}) collective-permute-start(bf16[512,4096]{1,0:T(8,128)(2,1)} %bitcast.115), channel_id=1, source_target_pairs={{0,1},{1,0},{2,3},{3,2},{4,5},{5,4},{6,7},{7,6},{8,9},{9,8},{10,11... | collective-permute-start | bytes 12582920 | tf_op jit(solution)/shard_map/ppermute | solution.py:30
  26.4 25.1 %collective-permute-start.7 = (bf16[2,2,64,1024]{3,2,1,0:T(8,128)(2,1)S(1)}, bf16[2,2,64,1024]{3,2,1,0:T(8,128)(2,1)S(1)}, u32[]{:S(2)}, u32[]{:S(2)}) collective-permute-start(bf16[2,2,64,1024]{3,2,1,0:T(8,128)(2,1)S(1)} %pad_maximum_fusion.zs), channel_id=1, source_target_pairs={{0,8},{8,16},{16,24},{24,0},{1,9},{9,17},{17,25},{25,1},{2,10},{10... | collective-permute-start | bytes 1572872 | tf_op jit(solution)/shard_map/ppermute | solution.py:26
  27.7 23.8 %collective-permute-start.8 = (bf16[2,2,64,1024]{3,2,1,0:T(8,128)(2,1)S(1)}, bf16[2,2,64,1024]{3,2,1,0:T(8,128)(2,1)S(1)}, u32[]{:S(2)}, u32[]{:S(2)}) collective-permute-start(bf16[2,2,64,1024]{3,2,1,0:T(8,128)(2,1)S(1)} %pad_maximum_fusion.zs), channel_id=1, source_target_pairs={{0,24},{8,0},{16,8},{24,16},{1,25},{9,1},{17,9},{25,17},{2,26},{10... | collective-permute-start | bytes 1572872 | tf_op jit(solution)/shard_map/ppermute | solution.py:26
  29.2 10.2 %collective-permute-start.10 = (bf16[64,1024]{1,0:T(8,128)(2,1)S(1)}, bf16[64,1024]{1,0:T(8,128)(2,1)S(1)}, u32[]{:S(2)}, u32[]{:S(2)}) collective-permute-start(bf16[64,1024]{1,0:T(8,128)(2,1)S(1)} %slice_bitcast_fusion.10), channel_id=1, source_target_pairs={{0,6},{2,0},{4,2},{6,4},{1,7},{3,1},{5,3},{7,5},{8,14},{10,8},{12,... | collective-permute-start | bytes 393224 | tf_op jit(solution)/shard_map/ppermute | solution.py:26
  31.7 8.1 %collective-permute-start.9 = (bf16[64,1024]{1,0:T(8,128)(2,1)S(1)}, bf16[64,1024]{1,0:T(8,128)(2,1)S(1)}, u32[]{:S(2)}, u32[]{:S(2)}) collective-permute-start(bf16[64,1024]{1,0:T(8,128)(2,1)S(1)} %slice_bitcast_fusion.11), channel_id=1, source_target_pairs={{0,2},{2,4},{4,6},{6,0},{1,3},{3,5},{5,7},{7,1},{8,10},{10,12},{12... | collective-permute-start | bytes 393224 | tf_op jit(solution)/shard_map/ppermute | solution.py:26
  39.8 11.7 %collective-permute-start.11 = (bf16[2,64,1024]{2,1,0:T(8,128)(2,1)S(1)}, bf16[2,64,1024]{2,1,0:T(8,128)(2,1)S(1)}, u32[]{:S(2)}, u32[]{:S(2)}) collective-permute-start(bf16[2,64,1024]{2,1,0:T(8,128)(2,1)S(1)} %pad_maximum_fusion.6.zz), channel_id=1, source_target_pairs={{0,8},{8,16},{16,24},{24,0},{1,9},{9,17},{17,25},{25,1},{2,10},{10... | collective-permute-start | bytes 786440 | tf_op jit(solution)/shard_map/ppermute | solution.py:26
  39.9 11.6 %collective-permute-start.12 = (bf16[2,64,1024]{2,1,0:T(8,128)(2,1)S(1)}, bf16[2,64,1024]{2,1,0:T(8,128)(2,1)S(1)}, u32[]{:S(2)}, u32[]{:S(2)}) collective-permute-start(bf16[2,64,1024]{2,1,0:T(8,128)(2,1)S(1)} %pad_maximum_fusion.6.zz), channel_id=1, source_target_pairs={{0,24},{8,0},{16,8},{24,16},{1,25},{9,1},{17,9},{25,17},{2,26},{10... | collective-permute-start | bytes 786440 | tf_op jit(solution)/shard_map/ppermute | solution.py:26
  51.7 11.9 %collective-permute-start.15 = (bf16[4,64,1024]{2,1,0:T(8,128)(2,1)S(1)}, bf16[4,64,1024]{2,1,0:T(8,128)(2,1)S(1)}, u32[]{:S(2)}, u32[]{:S(2)}) collective-permute-start(bf16[4,64,1024]{2,1,0:T(8,128)(2,1)S(1)} %pad_maximum_fusion.2), channel_id=1, source_target_pairs={{0,24},{8,0},{16,8},{24,16},{1,25},{9,1},{17,9},{25,17},{2,26},{10... | collective-permute-start | bytes 1572872 | tf_op jit(solution)/shard_map/ppermute | solution.py:26
  52.0 11.6 %collective-permute-start.14 = (bf16[4,64,1024]{2,1,0:T(8,128)(2,1)S(1)}, bf16[4,64,1024]{2,1,0:T(8,128)(2,1)S(1)}, u32[]{:S(2)}, u32[]{:S(2)}) collective-permute-start(bf16[4,64,1024]{2,1,0:T(8,128)(2,1)S(1)} %pad_maximum_fusion.1), channel_id=1, source_target_pairs={{0,8},{8,16},{16,24},{24,0},{1,9},{9,17},{17,25},{25,1},{2,10},{10... | collective-permute-start | bytes 1572872 | tf_op jit(solution)/shard_map/ppermute | solution.py:26
  67.9 10.5 %collective-permute-start.16 = (bf16[4,64,1024]{2,1,0:T(8,128)(2,1)S(1)}, bf16[4,64,1024]{2,1,0:T(8,128)(2,1)S(1)}, u32[]{:S(2)}, u32[]{:S(2)}) collective-permute-start(bf16[4,64,1024]{2,1,0:T(8,128)(2,1)S(1)} %get-tuple-element.75), channel_id=1, source_target_pairs={{0,8},{8,16},{16,24},{24,0},{1,9},{9,17},{17,25},{25,1},{2,10},{10... | collective-permute-start | bytes 1572872 | tf_op jit(solution)/shard_map/ppermute | solution.py:26
  68.1 10.3 %collective-permute-start.17 = (bf16[4,64,1024]{2,1,0:T(8,128)(2,1)S(1)}, bf16[4,64,1024]{2,1,0:T(8,128)(2,1)S(1)}, u32[]{:S(2)}, u32[]{:S(2)}) collective-permute-start(bf16[4,64,1024]{2,1,0:T(8,128)(2,1)S(1)} %get-tuple-element.76), channel_id=1, source_target_pairs={{0,24},{8,0},{16,8},{24,16},{1,25},{9,1},{17,9},{25,17},{2,26},{10... | collective-permute-start | bytes 1572872 | tf_op jit(solution)/shard_map/ppermute | solution.py:26
  81.4 16.4 %collective-permute-start.19 = (bf16[2,2,64,1024]{3,2,1,0:T(8,128)(2,1)S(1)}, bf16[2,2,64,1024]{3,2,1,0:T(8,128)(2,1)S(1)}, u32[]{:S(2)}, u32[]{:S(2)}) collective-permute-start(bf16[2,2,64,1024]{3,2,1,0:T(8,128)(2,1)S(1)} %pad_maximum_fusion.4), channel_id=1, source_target_pairs={{0,24},{8,0},{16,8},{24,16},{1,25},{9,1},{17,9},{25,17},{2,26},{10... | collective-permute-start | bytes 1572872 | tf_op jit(solution)/shard_map/ppermute | solution.py:26
  84.2 13.6 %collective-permute-start.18 = (bf16[2,2,64,1024]{3,2,1,0:T(8,128)(2,1)S(1)}, bf16[2,2,64,1024]{3,2,1,0:T(8,128)(2,1)S(1)}, u32[]{:S(2)}, u32[]{:S(2)}) collective-permute-start(bf16[2,2,64,1024]{3,2,1,0:T(8,128)(2,1)S(1)} %pad_maximum_fusion.3), channel_id=1, source_target_pairs={{0,8},{8,16},{16,24},{24,0},{1,9},{9,17},{17,25},{25,1},{2,10},{10... | collective-permute-start | bytes 1572872 | tf_op jit(solution)/shard_map/ppermute | solution.py:26
  91.6 11.5 %collective-permute-start.27 = (bf16[2,1,64,1024]{3,2,0,1:T(8,128)(2,1)S(1)}, bf16[2,1,64,1024]{3,2,0,1:T(8,128)(2,1)S(1)}, u32[]{:S(2)}, u32[]{:S(2)}) collective-permute-start(bf16[2,1,64,1024]{3,2,0,1:T(8,128)(2,1)S(1)} %pad_maximum_fusion.12), channel_id=1, source_target_pairs={{0,24},{8,0},{16,8},{24,16},{1,25},{9,1},{17,9},{25,17},{2,26},{10... | collective-permute-start | bytes 786440 | tf_op jit(solution)/shard_map/ppermute | solution.py:26
  94.0 9.6 %collective-permute-start.26 = (bf16[2,1,64,1024]{3,2,1,0:T(8,128)(2,1)S(1)}, bf16[2,1,64,1024]{3,2,1,0:T(8,128)(2,1)S(1)}, u32[]{:S(2)}, u32[]{:S(2)}) collective-permute-start(bf16[2,1,64,1024]{3,2,1,0:T(8,128)(2,1)S(1)} %pad_maximum_fusion.11), channel_id=1, source_target_pairs={{0,8},{8,16},{16,24},{24,0},{1,9},{9,17},{17,25},{25,1},{2,10},{10... | collective-permute-start | bytes 786440 | tf_op jit(solution)/shard_map/ppermute | solution.py:26
  98.2 10.8 %collective-permute-start.25 = (bf16[2,64,1024]{2,1,0:T(8,128)(2,1)S(1)}, bf16[2,64,1024]{2,1,0:T(8,128)(2,1)S(1)}, u32[]{:S(2)}, u32[]{:S(2)}) collective-permute-start(bf16[2,64,1024]{2,1,0:T(8,128)(2,1)S(1)} %pad_maximum_fusion.10), channel_id=1, source_target_pairs={{0,6},{2,0},{4,2},{6,4},{1,7},{3,1},{5,3},{7,5},{8,14},{10,8},{12,... | collective-permute-start | bytes 786440 | tf_op jit(solution)/shard_map/ppermute | solution.py:26
  99.9 9.4 %collective-permute-start.24 = (bf16[2,64,1024]{2,1,0:T(8,128)(2,1)S(1)}, bf16[2,64,1024]{2,1,0:T(8,128)(2,1)S(1)}, u32[]{:S(2)}, u32[]{:S(2)}) collective-permute-start(bf16[2,64,1024]{2,1,0:T(8,128)(2,1)S(1)} %pad_maximum_fusion.9), channel_id=1, source_target_pairs={{0,2},{2,4},{4,6},{6,0},{1,3},{3,5},{5,7},{7,1},{8,10},{10,12},{12... | collective-permute-start | bytes 786440 | tf_op jit(solution)/shard_map/ppermute | solution.py:26
  109.6 18.3 %collective-permute-start.28 = (bf16[2,64,512]{2,1,0:T(8,128)(2,1)S(1)}, bf16[2,64,512]{2,1,0:T(8,128)(2,1)S(1)}, u32[]{:S(2)}, u32[]{:S(2)}) collective-permute-start(bf16[2,64,512]{2,1,0:T(8,128)(2,1)S(1)} %get-tuple-element.111), channel_id=1, source_target_pairs={{0,32},{1,33},{32,64},{33,65},{64,96},{65,97},{96,128},{97,129},{1... | collective-permute-start | bytes 393224 | tf_op jit(solution)/shard_map/ppermute | solution.py:38
  115.0 19.8 %collective-permute-start.29 = (bf16[2,64,512]{2,1,0:T(8,128)(2,1)S(1)}, bf16[2,64,512]{2,1,0:T(8,128)(2,1)S(1)}, u32[]{:S(2)}, u32[]{:S(2)}) collective-permute-start(bf16[2,64,512]{2,1,0:T(8,128)(2,1)S(1)} %get-tuple-element.112), channel_id=1, source_target_pairs={{0,33},{1,32},{32,65},{33,64},{64,97},{65,96},{96,129},{97,128},{1... | collective-permute-start | bytes 393224 | tf_op jit(solution)/shard_map/ppermute | solution.py:38
  (11 other events, 148.1 us)

commit v4 on v3

--- a/solution.py
+++ b/solution.py
@@ -232,13 +232,12 @@
     gain, bias = ln_gain[0].reshape(RING, PART), ln_bias[0].reshape(RING, PART)
 
     split = acts[0].reshape(2, 2, TILE, HALF)
-    got, b_up_s = lax.optimization_barrier((swapped(acts[0]), swapped(b_up)))
+    got, b_up_s, up_o = lax.optimization_barrier((swapped(acts[0]), swapped(b_up), up_o))
     mine = lax.dynamic_index_in_dim(split, core, 1, keepdims=False)
     got = lax.dynamic_index_in_dim(got.reshape(2, 2, TILE, HALF), core, 1, keepdims=False)
     low = jnp.where(core == 0, mine, got)
     high = jnp.where(core == 0, got, mine)
     block = jnp.concatenate([low, high], axis=-1)
-    block, up_o = lax.optimization_barrier((block, up_o))
     b_all = jnp.concatenate([b_up, b_up_s], axis=0)
 
     zp, zm = sent(block, "zh", 1), sent(block, "zh", -1)

time: 136 us -> 134 us (0.985)
  local copies, waits for them, and re-layouts: 7.93 us -> 3.8 us
  Pallas kernels: 19.9 us -> 21.8 us
    unnamed x11 -> x7, local copies, waits for them, and re-layouts: 6.89 us -> 2.77 us
    pallas_call x2, Pallas kernels: 3.06 us -> 4.97 us  [loaded(): pl.pallas_call(load_kernel, in_specs=[pl.BlockSpec(memory_space=pltpu.HBM...]
  transfers between devices with their start and end apart: 30 -> 30, of which waited for: 14 -> 14; matrix products, arithmetic and copies ran while one was open for 4% -> 5% of each run, Pallas kernels for 12% -> 13%
where the time goes in v4:
time: 134 us
  starting transfers between devices  58.5 us (44%)
  waiting for transfers between devices  43.1 us (32%)
  Pallas kernels  21.8 us (16%)
  other arithmetic  6.16 us (5%)
  local copies, waits for them, and re-layouts  3.8 us (3%)
    ppermute x24, starting transfers between devices, sent(): lax.ppermute(block, axis, [(i, (i + distance) % RING) for i in range(RING)])  35.4 us
    ppermute x24, waiting for transfers between devices, sent(): lax.ppermute(block, axis, [(i, (i + distance) % RING) for i in range(RING)])  34.7 us
    ppermute x2, starting transfers between devices, next_section(): return lax.ppermute(block, ('y', 'zl', 'core'), pairs)  18.6 us
    pallas_call x3, Pallas kernels, call(): pl.pallas_call(kernel, in_specs=[SMEM] + [VMEM] * (len(operands) - 1), ou...  16.8 us
    ppermute x2, waiting for transfers between devices, next_section(): return lax.ppermute(block, ('y', 'zl', 'core'), pairs)  7.02 us
    pallas_call x2, Pallas kernels, loaded(): pl.pallas_call(load_kernel, in_specs=[pl.BlockSpec(memory_space=pltpu.HBM...  4.97 us
    ppermute x4, starting transfers between devices, swapped(): return lax.ppermute(block, 'core', [(0, 1), (1, 0)])  4.6 us
    unnamed x2, other arithmetic  2.78 us
  transfers between devices with their start and end apart: 30, of which 14 were waited for; matrix products, arithmetic and copies ran while one was open for 5% of the time, Pallas kernels for 13%

profile of v4, /device:TPU:1, one launch (start us, length us, event | category | flops | bytes accessed | tf_op | source)
XLA Modules:
  0.0 133.8 jit_solution(732905603694764617)
XLA Ops:
  0.0 3.2 %collective-permute-start = (bf16[256,512]{1,0:T(8,128)(2,1)}, bf16[256,512]{1,0:T(8,128)(2,1)S(1)}, u32[]{:S(2)}, u32[]{:S(2)}) collective-permute-start(bf16[256,512]{1,0:T(8,128)(2,1)} %bitcast.123), channel_id=1, source_target_pairs={{0,1},{1,0},{2,3},{3,2},{4,5},{5,4},{6,7},{7,6},{8,9},{9,8},{10,11... | collective-permute-start | bytes 786440 | tf_op jit(solution)/shard_map/ppermute | solution.py:30
  7.3 3.1 %collective-permute-start.3 = (bf16[2,64,1024]{2,1,0:T(8,128)(2,1)S(1)}, bf16[2,64,1024]{2,1,0:T(8,128)(2,1)S(1)}, u32[]{:S(2)}, u32[]{:S(2)}) collective-permute-start(bf16[2,64,1024]{2,1,0:T(8,128)(2,1)S(1)} %pad_maximum_fusion.5.block), channel_id=1, source_target_pairs={{0,6},{2,0},{4,2},{6,4},{1,7},{3,1},{5,3},{7,5},{8,14},{10,8},{12,... | collective-permute-start | bytes 786440 | tf_op jit(solution)/shard_map/ppermute | solution.py:26
  13.1 5.3 %collective-permute-done.2 = bf16[2,64,1024]{2,1,0:T(8,128)(2,1)S(1)} collective-permute-done((bf16[2,64,1024]{2,1,0:T(8,128)(2,1)S(1)}, bf16[2,64,1024]{2,1,0:T(8,128)(2,1)S(1)}, u32[]{:S(2)}, u32[]{:S(2)}) %collective-permute-start.2) | collective-permute-done | bytes 262176 | tf_op jit(solution)/shard_map/ppermute | solution.py:26
  18.4 5.0 %collective-permute-done.3 = bf16[2,64,1024]{2,1,0:T(8,128)(2,1)S(1)} collective-permute-done((bf16[2,64,1024]{2,1,0:T(8,128)(2,1)S(1)}, bf16[2,64,1024]{2,1,0:T(8,128)(2,1)S(1)}, u32[]{:S(2)}, u32[]{:S(2)}) %collective-permute-start.3) | collective-permute-done | bytes 262176 | tf_op jit(solution)/shard_map/ppermute | solution.py:26
  27.3 2.6 %collective-permute-start.10 = (bf16[64,1024]{1,0:T(8,128)(2,1)S(1)}, bf16[64,1024]{1,0:T(8,128)(2,1)S(1)}, u32[]{:S(2)}, u32[]{:S(2)}) collective-permute-start(bf16[64,1024]{1,0:T(8,128)(2,1)S(1)} %slice_bitcast_fusion.10), channel_id=1, source_target_pairs={{0,6},{2,0},{4,2},{6,4},{1,7},{3,1},{5,3},{7,5},{8,14},{10,8},{12,... | collective-permute-start | bytes 393224 | tf_op jit(solution)/shard_map/ppermute | solution.py:26
  31.0 6.6 %collective-permute-done.10 = bf16[64,1024]{1,0:T(8,128)(2,1)S(1)} collective-permute-done((bf16[64,1024]{1,0:T(8,128)(2,1)S(1)}, bf16[64,1024]{1,0:T(8,128)(2,1)S(1)}, u32[]{:S(2)}, u32[]{:S(2)}) %collective-permute-start.10) | collective-permute-done | bytes 131104 | tf_op jit(solution)/shard_map/ppermute | solution.py:26
  37.9 2.7 %collective-permute-start.12 = (bf16[2,64,1024]{2,1,0:T(8,128)(2,1)S(1)}, bf16[2,64,1024]{2,1,0:T(8,128)(2,1)S(1)}, u32[]{:S(2)}, u32[]{:S(2)}) collective-permute-start(bf16[2,64,1024]{2,1,0:T(8,128)(2,1)S(1)} %pad_maximum_fusion.6.zz), channel_id=1, source_target_pairs={{0,24},{8,0},{16,8},{24,16},{1,25},{9,1},{17,9},{25,17},{2,26},{10... | collective-permute-start | bytes 786440 | tf_op jit(solution)/shard_map/ppermute | solution.py:26
  46.8 2.5 %shard_map.73 = (bf16[2,4096,512]{2,1,0:T(8,128)(2,1)S(1)}, f32[8,128]{1,0:T(8,128)S(1)}) custom-call(bf16[4096,512]{1,0:T(8,128)(2,1)S(1)} %bitcast.118, bf16[4096,512]{1,0:T(8,128)(2,1)} %collective-permute-done.6.other, f32[2,512]{1,0:T(2,128)S(1)} %pad_maximum_fusion.14.after.b_up), custom_call_target="tpu_custom_call" | custom-call | bytes 16777216 | tf_op jit(solution)/shard_map/pallas_call | solution.py:196
  51.5 7.3 %shard_map.74.after.near = bf16[6,64,1024]{2,1,0:T(8,128)(2,1)S(1)} custom-call(s32[2]{0:T(128)S(1)} %add_add_fusion.place, bf16[2,64,1024]{2,1,0:T(8,128)(2,1)S(1)} %pad_maximum_fusion.5.block, bf16[2,2,64,1024]{3,2,1,0:T(8,128)(2,1)S(1)} %pad_maximum_fusion.zs, bf16[2,64,1024]{2,1,0:T(8,128)(2,1)S(1)} %pad_maximum_fusion.6.zz, ...), custom_call_target="tpu_custom_call" | custom-call | flops 805306368 | bytes 1048576 | tf_op jit(solution)/shard_map/pallas_call | solution.py:174
  58.8 2.5 %shard_map.75 = (bf16[2,512,4096]{2,1,0:T(8,128)(2,1)S(1)}, f32[8,128]{1,0:T(8,128)S(1)}) custom-call(bf16[512,4096]{1,0:T(8,128)(2,1)S(1)} %bitcast.116, bf16[512,4096]{1,0:T(8,128)(2,1)} %collective-permute-done.13.other, bf16[6,64,1024]{2,1,0:T(8,128)(2,1)S(1)} %shard_map.74.after.near), custom_call_target="tpu_custom_call" | custom-call | bytes 16777216 | tf_op jit(solution)/shard_map/pallas_call | solution.py:196
  61.4 4.3 %shard_map.76 = (bf16[4,64,1024]{2,1,0:T(8,128)(2,1)S(1)}, bf16[4,64,1024]{2,1,0:T(8,128)(2,1)S(1)}, bf16[8,64,1024]{2,1,0:T(8,128)(2,1)S(1)}) custom-call(s32[2]{0:T(128)S(1)} %bitcast_add_fusion.2.place, bf16[4,64,1024]{2,1,0:T(8,128)(2,1)S(1)} %collective-permute-done.14.ml, bf16[4,64,1024]{2,1,0:T(8,128)(2,1)S(1)} %collective-permute-done.15.mr, ...), custom_call_target="tpu_custom_call" | custom-call | flops 536870912 | bytes 1048576 | tf_op jit(solution)/shard_map/pallas_call | solution.py:174
  65.8 2.7 %collective-permute-start.17 = (bf16[4,64,1024]{2,1,0:T(8,128)(2,1)S(1)}, bf16[4,64,1024]{2,1,0:T(8,128)(2,1)S(1)}, u32[]{:S(2)}, u32[]{:S(2)}) collective-permute-start(bf16[4,64,1024]{2,1,0:T(8,128)(2,1)S(1)} %get-tuple-element.74), channel_id=1, source_target_pairs={{0,24},{8,0},{16,8},{24,16},{1,25},{9,1},{17,9},{25,17},{2,26},{10... | collective-permute-start | bytes 1572872 | tf_op jit(solution)/shard_map/ppermute | solution.py:26
  68.4 5.3 %shard_map.77 = (bf16[2,4,64,1024]{3,2,1,0:T(8,128)(2,1)S(1)}, bf16[2,4,64,1024]{3,2,1,0:T(8,128)(2,1)S(1)}, bf16[2,4,64,1024]{3,2,1,0:T(8,128)(2,1)S(1)}, bf16[2,64,1024]{2,1,0:T(8,128)(2,1)S(1)}) custom-call(s32[2]{0:T(128)S(1)} %add_add_fusion.place, bf16[8,64,1024]{2,1,0:T(8,128)(2,1)S(1)} %get-tuple-element.70.hid, ...), custom_call_target="tpu_custom_call" | custom-call | flops 805306368 | bytes 1048576 | tf_op jit(solution)/shard_map/pallas_call | solution.py:174
  73.9 2.3 %collective-permute-done.16 = bf16[4,64,1024]{2,1,0:T(8,128)(2,1)S(1)} collective-permute-done((bf16[4,64,1024]{2,1,0:T(8,128)(2,1)S(1)}, bf16[4,64,1024]{2,1,0:T(8,128)(2,1)S(1)}, u32[]{:S(2)}, u32[]{:S(2)}) %collective-permute-start.16) | collective-permute-done | bytes 524320 | tf_op jit(solution)/shard_map/ppermute | solution.py:26
  76.5 2.5 %collective-permute-start.21 = (bf16[2,1,64,1024]{3,2,1,0:T(8,128)(2,1)S(1)}, bf16[2,1,64,1024]{3,2,1,0:T(8,128)(2,1)S(1)}, u32[]{:S(2)}, u32[]{:S(2)}) collective-permute-start(bf16[2,1,64,1024]{3,2,1,0:T(8,128)(2,1)S(1)} %pad_maximum_fusion.8), channel_id=1, source_target_pairs={{0,24},{8,0},{16,8},{24,16},{1,25},{9,1},{17,9},{25,17},{2,26},{10... | collective-permute-start | bytes 786440 | tf_op jit(solution)/shard_map/ppermute | solution.py:26
  79.2 2.7 %collective-permute-start.19 = (bf16[2,2,64,1024]{3,2,1,0:T(8,128)(2,1)S(1)}, bf16[2,2,64,1024]{3,2,1,0:T(8,128)(2,1)S(1)}, u32[]{:S(2)}, u32[]{:S(2)}) collective-permute-start(bf16[2,2,64,1024]{3,2,1,0:T(8,128)(2,1)S(1)} %pad_maximum_fusion.4), channel_id=1, source_target_pairs={{0,24},{8,0},{16,8},{24,16},{1,25},{9,1},{17,9},{25,17},{2,26},{10... | collective-permute-start | bytes 1572872 | tf_op jit(solution)/shard_map/ppermute | solution.py:26
  83.0 2.5 %collective-permute-done.20 = bf16[2,1,64,1024]{3,2,1,0:T(8,128)(2,1)S(1)} collective-permute-done((bf16[2,1,64,1024]{3,2,1,0:T(8,128)(2,1)S(1)}, bf16[2,1,64,1024]{3,2,1,0:T(8,128)(2,1)S(1)}, u32[]{:S(2)}, u32[]{:S(2)}) %collective-permute-start.20) | collective-permute-done | bytes 262176 | tf_op jit(solution)/shard_map/ppermute | solution.py:26
  85.7 3.8 %collective-permute-start.22 = (bf16[64,1024]{1,0:T(8,128)(2,1)S(1)}, bf16[64,1024]{1,0:T(8,128)(2,1)S(1)}, u32[]{:S(2)}, u32[]{:S(2)}) collective-permute-start(bf16[64,1024]{1,0:T(8,128)(2,1)S(1)} %get-tuple-element.112), channel_id=1, source_target_pairs={{0,2},{2,4},{4,6},{6,0},{1,3},{3,5},{5,7},{7,1},{8,10},{10,12},{12... | collective-permute-start | bytes 393224 | tf_op jit(solution)/shard_map/ppermute | solution.py:26
  91.8 3.9 %collective-permute-done.23 = bf16[64,1024]{1,0:T(8,128)(2,1)S(1)} collective-permute-done((bf16[64,1024]{1,0:T(8,128)(2,1)S(1)}, bf16[64,1024]{1,0:T(8,128)(2,1)S(1)}, u32[]{:S(2)}, u32[]{:S(2)}) %collective-permute-start.23) | collective-permute-done | bytes 131104 | tf_op jit(solution)/shard_map/ppermute | solution.py:26
  97.4 3.5 %collective-permute-start.24 = (bf16[2,64,1024]{2,1,0:T(8,128)(2,1)S(1)}, bf16[2,64,1024]{2,1,0:T(8,128)(2,1)S(1)}, u32[]{:S(2)}, u32[]{:S(2)}) collective-permute-start(bf16[2,64,1024]{2,1,0:T(8,128)(2,1)S(1)} %pad_maximum_fusion.9), channel_id=1, source_target_pairs={{0,2},{2,4},{4,6},{6,0},{1,3},{3,5},{5,7},{7,1},{8,10},{10,12},{12... | collective-permute-start | bytes 786440 | tf_op jit(solution)/shard_map/ppermute | solution.py:26
  101.4 5.5 %collective-permute-done.25 = bf16[2,64,1024]{2,1,0:T(8,128)(2,1)S(1)} collective-permute-done((bf16[2,64,1024]{2,1,0:T(8,128)(2,1)S(1)}, bf16[2,64,1024]{2,1,0:T(8,128)(2,1)S(1)}, u32[]{:S(2)}, u32[]{:S(2)}) %collective-permute-start.25) | collective-permute-done | bytes 262176 | tf_op jit(solution)/shard_map/ppermute | solution.py:26
  107.5 5.1 %collective-permute-start.28 = (bf16[2,64,512]{2,1,0:T(8,128)(2,1)S(1)}, bf16[2,64,512]{2,1,0:T(8,128)(2,1)S(1)}, u32[]{:S(2)}, u32[]{:S(2)}) collective-permute-start(bf16[2,64,512]{2,1,0:T(8,128)(2,1)S(1)} %get-tuple-element.109), channel_id=1, source_target_pairs={{0,32},{1,33},{32,64},{33,65},{64,96},{65,97},{96,128},{97,129},{1... | collective-permute-start | bytes 393224 | tf_op jit(solution)/shard_map/ppermute | solution.py:38
  112.5 13.5 %collective-permute-start.29 = (bf16[2,64,512]{2,1,0:T(8,128)(2,1)S(1)}, bf16[2,64,512]{2,1,0:T(8,128)(2,1)S(1)}, u32[]{:S(2)}, u32[]{:S(2)}) collective-permute-start(bf16[2,64,512]{2,1,0:T(8,128)(2,1)S(1)} %get-tuple-element.110), channel_id=1, source_target_pairs={{0,33},{1,32},{32,65},{33,64},{64,97},{65,96},{96,129},{97,128},{1... | collective-permute-start | bytes 393224 | tf_op jit(solution)/shard_map/ppermute | solution.py:38
  126.0 7.0 %collective-permute-done.29 = bf16[2,64,512]{2,1,0:T(8,128)(2,1)S(1)} collective-permute-done((bf16[2,64,512]{2,1,0:T(8,128)(2,1)S(1)}, bf16[2,64,512]{2,1,0:T(8,128)(2,1)S(1)}, u32[]{:S(2)}, u32[]{:S(2)}) %collective-permute-start.29) | collective-permute-done | bytes 131104 | tf_op jit(solution)/shard_map/ppermute | solution.py:38
  (97 shorter events, 28.1 us)
Async XLA Ops:
  4.6 18.9 %collective-permute-start.6 = (bf16[4096,512]{1,0:T(8,128)(2,1)}, bf16[4096,512]{1,0:T(8,128)(2,1)}, u32[]{:S(2)}, u32[]{:S(2)}) collective-permute-start(bf16[4096,512]{1,0:T(8,128)(2,1)} %bitcast.117), channel_id=1, source_target_pairs={{0,1},{1,0},{2,3},{3,2},{4,5},{5,4},{6,7},{7,6},{8,9},{9,8},{10,11... | collective-permute-start | bytes 12582920 | tf_op jit(solution)/shard_map/ppermute | solution.py:30
  6.0 12.5 %collective-permute-start.2 = (bf16[2,64,1024]{2,1,0:T(8,128)(2,1)S(1)}, bf16[2,64,1024]{2,1,0:T(8,128)(2,1)S(1)}, u32[]{:S(2)}, u32[]{:S(2)}) collective-permute-start(bf16[2,64,1024]{2,1,0:T(8,128)(2,1)S(1)} %pad_maximum_fusion.5.block), channel_id=1, source_target_pairs={{0,2},{2,4},{4,6},{6,0},{1,3},{3,5},{5,7},{7,1},{8,10},{10,12},{12... | collective-permute-start | bytes 786440 | tf_op jit(solution)/shard_map/ppermute | solution.py:26
  7.3 16.2 %collective-permute-start.3 = (bf16[2,64,1024]{2,1,0:T(8,128)(2,1)S(1)}, bf16[2,64,1024]{2,1,0:T(8,128)(2,1)S(1)}, u32[]{:S(2)}, u32[]{:S(2)}) collective-permute-start(bf16[2,64,1024]{2,1,0:T(8,128)(2,1)S(1)} %pad_maximum_fusion.5.block), channel_id=1, source_target_pairs={{0,6},{2,0},{4,2},{6,4},{1,7},{3,1},{5,3},{7,5},{8,14},{10,8},{12,... | collective-permute-start | bytes 786440 | tf_op jit(solution)/shard_map/ppermute | solution.py:26
  10.4 13.1 %collective-permute-start.4 = (bf16[2,64,1024]{2,1,0:T(8,128)(2,1)S(1)}, bf16[2,64,1024]{2,1,0:T(8,128)(2,1)S(1)}, u32[]{:S(2)}, u32[]{:S(2)}) collective-permute-start(bf16[2,64,1024]{2,1,0:T(8,128)(2,1)S(1)} %pad_maximum_fusion.5.block), channel_id=1, source_target_pairs={{0,8},{8,16},{16,24},{24,0},{1,9},{9,17},{17,25},{25,1},{2,10},{10... | collective-permute-start | bytes 786440 | tf_op jit(solution)/shard_map/ppermute | solution.py:26
  11.6 11.9 %collective-permute-start.5 = (bf16[2,64,1024]{2,1,0:T(8,128)(2,1)S(1)}, bf16[2,64,1024]{2,1,0:T(8,128)(2,1)S(1)}, u32[]{:S(2)}, u32[]{:S(2)}) collective-permute-start(bf16[2,64,1024]{2,1,0:T(8,128)(2,1)S(1)} %pad_maximum_fusion.5.block), channel_id=1, source_target_pairs={{0,24},{8,0},{16,8},{24,16},{1,25},{9,1},{17,9},{25,17},{2,26},{10... | collective-permute-start | bytes 786440 | tf_op jit(solution)/shard_map/ppermute | solution.py:26
  23.5 35.3 %collective-permute-start.13 = (bf16[512,4096]{1,0:T(8,128)(2,1)}, bf16[512,4096]{1,0:T(8,128)(2,1)}, u32[]{:S(2)}, u32[]{:S(2)}) collective-permute-start(bf16[512,4096]{1,0:T(8,128)(2,1)} %bitcast.115), channel_id=1, source_target_pairs={{0,1},{1,0},{2,3},{3,2},{4,5},{5,4},{6,7},{7,6},{8,9},{9,8},{10,11... | collective-permute-start | bytes 12582920 | tf_op jit(solution)/shard_map/ppermute | solution.py:30
  24.5 24.8 %collective-permute-start.7 = (bf16[2,2,64,1024]{3,2,1,0:T(8,128)(2,1)S(1)}, bf16[2,2,64,1024]{3,2,1,0:T(8,128)(2,1)S(1)}, u32[]{:S(2)}, u32[]{:S(2)}) collective-permute-start(bf16[2,2,64,1024]{3,2,1,0:T(8,128)(2,1)S(1)} %pad_maximum_fusion.zs), channel_id=1, source_target_pairs={{0,8},{8,16},{16,24},{24,0},{1,9},{9,17},{17,25},{25,1},{2,10},{10... | collective-permute-start | bytes 1572872 | tf_op jit(solution)/shard_map/ppermute | solution.py:26
  25.8 23.5 %collective-permute-start.8 = (bf16[2,2,64,1024]{3,2,1,0:T(8,128)(2,1)S(1)}, bf16[2,2,64,1024]{3,2,1,0:T(8,128)(2,1)S(1)}, u32[]{:S(2)}, u32[]{:S(2)}) collective-permute-start(bf16[2,2,64,1024]{3,2,1,0:T(8,128)(2,1)S(1)} %pad_maximum_fusion.zs), channel_id=1, source_target_pairs={{0,24},{8,0},{16,8},{24,16},{1,25},{9,1},{17,9},{25,17},{2,26},{10... | collective-permute-start | bytes 1572872 | tf_op jit(solution)/shard_map/ppermute | solution.py:26
  27.3 10.2 %collective-permute-start.10 = (bf16[64,1024]{1,0:T(8,128)(2,1)S(1)}, bf16[64,1024]{1,0:T(8,128)(2,1)S(1)}, u32[]{:S(2)}, u32[]{:S(2)}) collective-permute-start(bf16[64,1024]{1,0:T(8,128)(2,1)S(1)} %slice_bitcast_fusion.10), channel_id=1, source_target_pairs={{0,6},{2,0},{4,2},{6,4},{1,7},{3,1},{5,3},{7,5},{8,14},{10,8},{12,... | collective-permute-start | bytes 393224 | tf_op jit(solution)/shard_map/ppermute | solution.py:26
  29.9 7.9 %collective-permute-start.9 = (bf16[64,1024]{1,0:T(8,128)(2,1)S(1)}, bf16[64,1024]{1,0:T(8,128)(2,1)S(1)}, u32[]{:S(2)}, u32[]{:S(2)}) collective-permute-start(bf16[64,1024]{1,0:T(8,128)(2,1)S(1)} %slice_bitcast_fusion.11), channel_id=1, source_target_pairs={{0,2},{2,4},{4,6},{6,0},{1,3},{3,5},{5,7},{7,1},{8,10},{10,12},{12... | collective-permute-start | bytes 393224 | tf_op jit(solution)/shard_map/ppermute | solution.py:26
  37.8 11.5 %collective-permute-start.11 = (bf16[2,64,1024]{2,1,0:T(8,128)(2,1)S(1)}, bf16[2,64,1024]{2,1,0:T(8,128)(2,1)S(1)}, u32[]{:S(2)}, u32[]{:S(2)}) collective-permute-start(bf16[2,64,1024]{2,1,0:T(8,128)(2,1)S(1)} %pad_maximum_fusion.6.zz), channel_id=1, source_target_pairs={{0,8},{8,16},{16,24},{24,0},{1,9},{9,17},{17,25},{25,1},{2,10},{10... | collective-permute-start | bytes 786440 | tf_op jit(solution)/shard_map/ppermute | solution.py:26
  37.9 11.4 %collective-permute-start.12 = (bf16[2,64,1024]{2,1,0:T(8,128)(2,1)S(1)}, bf16[2,64,1024]{2,1,0:T(8,128)(2,1)S(1)}, u32[]{:S(2)}, u32[]{:S(2)}) collective-permute-start(bf16[2,64,1024]{2,1,0:T(8,128)(2,1)S(1)} %pad_maximum_fusion.6.zz), channel_id=1, source_target_pairs={{0,24},{8,0},{16,8},{24,16},{1,25},{9,1},{17,9},{25,17},{2,26},{10... | collective-permute-start | bytes 786440 | tf_op jit(solution)/shard_map/ppermute | solution.py:26
  49.5 11.9 %collective-permute-start.15 = (bf16[4,64,1024]{2,1,0:T(8,128)(2,1)S(1)}, bf16[4,64,1024]{2,1,0:T(8,128)(2,1)S(1)}, u32[]{:S(2)}, u32[]{:S(2)}) collective-permute-start(bf16[4,64,1024]{2,1,0:T(8,128)(2,1)S(1)} %pad_maximum_fusion.2), channel_id=1, source_target_pairs={{0,24},{8,0},{16,8},{24,16},{1,25},{9,1},{17,9},{25,17},{2,26},{10... | collective-permute-start | bytes 1572872 | tf_op jit(solution)/shard_map/ppermute | solution.py:26
  49.8 11.6 %collective-permute-start.14 = (bf16[4,64,1024]{2,1,0:T(8,128)(2,1)S(1)}, bf16[4,64,1024]{2,1,0:T(8,128)(2,1)S(1)}, u32[]{:S(2)}, u32[]{:S(2)}) collective-permute-start(bf16[4,64,1024]{2,1,0:T(8,128)(2,1)S(1)} %pad_maximum_fusion.1), channel_id=1, source_target_pairs={{0,8},{8,16},{16,24},{24,0},{1,9},{9,17},{17,25},{25,1},{2,10},{10... | collective-permute-start | bytes 1572872 | tf_op jit(solution)/shard_map/ppermute | solution.py:26
  65.7 10.5 %collective-permute-start.16 = (bf16[4,64,1024]{2,1,0:T(8,128)(2,1)S(1)}, bf16[4,64,1024]{2,1,0:T(8,128)(2,1)S(1)}, u32[]{:S(2)}, u32[]{:S(2)}) collective-permute-start(bf16[4,64,1024]{2,1,0:T(8,128)(2,1)S(1)} %get-tuple-element.73), channel_id=1, source_target_pairs={{0,8},{8,16},{16,24},{24,0},{1,9},{9,17},{17,25},{25,1},{2,10},{10... | collective-permute-start | bytes 1572872 | tf_op jit(solution)/shard_map/ppermute | solution.py:26
  65.8 10.4 %collective-permute-start.17 = (bf16[4,64,1024]{2,1,0:T(8,128)(2,1)S(1)}, bf16[4,64,1024]{2,1,0:T(8,128)(2,1)S(1)}, u32[]{:S(2)}, u32[]{:S(2)}) collective-permute-start(bf16[4,64,1024]{2,1,0:T(8,128)(2,1)S(1)} %get-tuple-element.74), channel_id=1, source_target_pairs={{0,24},{8,0},{16,8},{24,16},{1,25},{9,1},{17,9},{25,17},{2,26},{10... | collective-permute-start | bytes 1572872 | tf_op jit(solution)/shard_map/ppermute | solution.py:26
  79.2 16.5 %collective-permute-start.19 = (bf16[2,2,64,1024]{3,2,1,0:T(8,128)(2,1)S(1)}, bf16[2,2,64,1024]{3,2,1,0:T(8,128)(2,1)S(1)}, u32[]{:S(2)}, u32[]{:S(2)}) collective-permute-start(bf16[2,2,64,1024]{3,2,1,0:T(8,128)(2,1)S(1)} %pad_maximum_fusion.4), channel_id=1, source_target_pairs={{0,24},{8,0},{16,8},{24,16},{1,25},{9,1},{17,9},{25,17},{2,26},{10... | collective-permute-start | bytes 1572872 | tf_op jit(solution)/shard_map/ppermute | solution.py:26
  82.0 13.7 %collective-permute-start.18 = (bf16[2,2,64,1024]{3,2,1,0:T(8,128)(2,1)S(1)}, bf16[2,2,64,1024]{3,2,1,0:T(8,128)(2,1)S(1)}, u32[]{:S(2)}, u32[]{:S(2)}) collective-permute-start(bf16[2,2,64,1024]{3,2,1,0:T(8,128)(2,1)S(1)} %pad_maximum_fusion.3), channel_id=1, source_target_pairs={{0,8},{8,16},{16,24},{24,0},{1,9},{9,17},{17,25},{25,1},{2,10},{10... | collective-permute-start | bytes 1572872 | tf_op jit(solution)/shard_map/ppermute | solution.py:26
  89.5 11.5 %collective-permute-start.27 = (bf16[2,1,64,1024]{3,2,0,1:T(8,128)(2,1)S(1)}, bf16[2,1,64,1024]{3,2,0,1:T(8,128)(2,1)S(1)}, u32[]{:S(2)}, u32[]{:S(2)}) collective-permute-start(bf16[2,1,64,1024]{3,2,0,1:T(8,128)(2,1)S(1)} %pad_maximum_fusion.12), channel_id=1, source_target_pairs={{0,24},{8,0},{16,8},{24,16},{1,25},{9,1},{17,9},{25,17},{2,26},{10... | collective-permute-start | bytes 786440 | tf_op jit(solution)/shard_map/ppermute | solution.py:26
  91.8 9.6 %collective-permute-start.26 = (bf16[2,1,64,1024]{3,2,1,0:T(8,128)(2,1)S(1)}, bf16[2,1,64,1024]{3,2,1,0:T(8,128)(2,1)S(1)}, u32[]{:S(2)}, u32[]{:S(2)}) collective-permute-start(bf16[2,1,64,1024]{3,2,1,0:T(8,128)(2,1)S(1)} %pad_maximum_fusion.11), channel_id=1, source_target_pairs={{0,8},{8,16},{16,24},{24,0},{1,9},{9,17},{17,25},{25,1},{2,10},{10... | collective-permute-start | bytes 786440 | tf_op jit(solution)/shard_map/ppermute | solution.py:26
  96.1 10.8 %collective-permute-start.25 = (bf16[2,64,1024]{2,1,0:T(8,128)(2,1)S(1)}, bf16[2,64,1024]{2,1,0:T(8,128)(2,1)S(1)}, u32[]{:S(2)}, u32[]{:S(2)}) collective-permute-start(bf16[2,64,1024]{2,1,0:T(8,128)(2,1)S(1)} %pad_maximum_fusion.10), channel_id=1, source_target_pairs={{0,6},{2,0},{4,2},{6,4},{1,7},{3,1},{5,3},{7,5},{8,14},{10,8},{12,... | collective-permute-start | bytes 786440 | tf_op jit(solution)/shard_map/ppermute | solution.py:26
  97.4 9.7 %collective-permute-start.24 = (bf16[2,64,1024]{2,1,0:T(8,128)(2,1)S(1)}, bf16[2,64,1024]{2,1,0:T(8,128)(2,1)S(1)}, u32[]{:S(2)}, u32[]{:S(2)}) collective-permute-start(bf16[2,64,1024]{2,1,0:T(8,128)(2,1)S(1)} %pad_maximum_fusion.9), channel_id=1, source_target_pairs={{0,2},{2,4},{4,6},{6,0},{1,3},{3,5},{5,7},{7,1},{8,10},{10,12},{12... | collective-permute-start | bytes 786440 | tf_op jit(solution)/shard_map/ppermute | solution.py:26
  107.5 18.6 %collective-permute-start.28 = (bf16[2,64,512]{2,1,0:T(8,128)(2,1)S(1)}, bf16[2,64,512]{2,1,0:T(8,128)(2,1)S(1)}, u32[]{:S(2)}, u32[]{:S(2)}) collective-permute-start(bf16[2,64,512]{2,1,0:T(8,128)(2,1)S(1)} %get-tuple-element.109), channel_id=1, source_target_pairs={{0,32},{1,33},{32,64},{33,65},{64,96},{65,97},{96,128},{97,129},{1... | collective-permute-start | bytes 393224 | tf_op jit(solution)/shard_map/ppermute | solution.py:38
  112.5 20.5 %collective-permute-start.29 = (bf16[2,64,512]{2,1,0:T(8,128)(2,1)S(1)}, bf16[2,64,512]{2,1,0:T(8,128)(2,1)S(1)}, u32[]{:S(2)}, u32[]{:S(2)}) collective-permute-start(bf16[2,64,512]{2,1,0:T(8,128)(2,1)S(1)} %get-tuple-element.110), channel_id=1, source_target_pairs={{0,33},{1,32},{32,65},{33,64},{64,97},{65,96},{96,129},{97,128},{1... | collective-permute-start | bytes 393224 | tf_op jit(solution)/shard_map/ppermute | solution.py:38
  (9 other events, 141.8 us)

commit v5 on v4

--- a/solution.py
+++ b/solution.py
@@ -135,7 +135,7 @@
         plus[n, :, columns] = value[:TILE]
         minus[n, :, columns] = value[TILE:]
 
-    down(z, lambda: hid[6:8].reshape(2 * TILE, 2 * UNITS), downs, send, unroll=4)
+    down(z, lambda: hid[6:8].reshape(2 * TILE, 2 * UNITS), downs, send, wide=PART, unroll=4)
 
 
 def rest_kernel(place, hid, downs, block, xm, ml, mr, xp, own, plus, minus, resid):

time: 134 us -> 134 us (level)
  no operation moved by 1% of the time
where the time goes in v5:
time: 134 us
  starting transfers between devices  58.6 us (44%)
  waiting for transfers between devices  43 us (32%)
  Pallas kernels  21.6 us (16%)
  other arithmetic  6.16 us (5%)
  local copies, waits for them, and re-layouts  3.8 us (3%)
    ppermute x24, starting transfers between devices, sent(): lax.ppermute(block, axis, [(i, (i + distance) % RING) for i in range(RING)])  35.4 us
    ppermute x24, waiting for transfers between devices, sent(): lax.ppermute(block, axis, [(i, (i + distance) % RING) for i in range(RING)])  34.7 us
    ppermute x2, starting transfers between devices, next_section(): return lax.ppermute(block, ('y', 'zl', 'core'), pairs)  18.6 us
    pallas_call x3, Pallas kernels, call(): pl.pallas_call(kernel, in_specs=[SMEM] + [VMEM] * (len(operands) - 1), ou...  16.7 us
    ppermute x2, waiting for transfers between devices, next_section(): return lax.ppermute(block, ('y', 'zl', 'core'), pairs)  7 us
    pallas_call x2, Pallas kernels, loaded(): pl.pallas_call(load_kernel, in_specs=[pl.BlockSpec(memory_space=pltpu.HBM...  4.97 us
    ppermute x4, starting transfers between devices, swapped(): return lax.ppermute(block, 'core', [(0, 1), (1, 0)])  4.6 us
    unnamed x2, other arithmetic  2.78 us
  transfers between devices with their start and end apart: 30, of which 14 were waited for; matrix products, arithmetic and copies ran while one was open for 5% of the time, Pallas kernels for 13%

profile of v5, /device:TPU:1, one launch (start us, length us, event | category | flops | bytes accessed | tf_op | source)
XLA Modules:
  0.0 133.6 jit_solution(9668540547207609259)
XLA Ops:
  0.0 3.2 %collective-permute-start = (bf16[256,512]{1,0:T(8,128)(2,1)}, bf16[256,512]{1,0:T(8,128)(2,1)S(1)}, u32[]{:S(2)}, u32[]{:S(2)}) collective-permute-start(bf16[256,512]{1,0:T(8,128)(2,1)} %bitcast.123), channel_id=1, source_target_pairs={{0,1},{1,0},{2,3},{3,2},{4,5},{5,4},{6,7},{7,6},{8,9},{9,8},{10,11... | collective-permute-start | bytes 786440 | tf_op jit(solution)/shard_map/ppermute | solution.py:30
  7.3 3.1 %collective-permute-start.3 = (bf16[2,64,1024]{2,1,0:T(8,128)(2,1)S(1)}, bf16[2,64,1024]{2,1,0:T(8,128)(2,1)S(1)}, u32[]{:S(2)}, u32[]{:S(2)}) collective-permute-start(bf16[2,64,1024]{2,1,0:T(8,128)(2,1)S(1)} %pad_maximum_fusion.5.block), channel_id=1, source_target_pairs={{0,6},{2,0},{4,2},{6,4},{1,7},{3,1},{5,3},{7,5},{8,14},{10,8},{12,... | collective-permute-start | bytes 786440 | tf_op jit(solution)/shard_map/ppermute | solution.py:26
  13.1 5.3 %collective-permute-done.2 = bf16[2,64,1024]{2,1,0:T(8,128)(2,1)S(1)} collective-permute-done((bf16[2,64,1024]{2,1,0:T(8,128)(2,1)S(1)}, bf16[2,64,1024]{2,1,0:T(8,128)(2,1)S(1)}, u32[]{:S(2)}, u32[]{:S(2)}) %collective-permute-start.2) | collective-permute-done | bytes 262176 | tf_op jit(solution)/shard_map/ppermute | solution.py:26
  18.4 5.0 %collective-permute-done.3 = bf16[2,64,1024]{2,1,0:T(8,128)(2,1)S(1)} collective-permute-done((bf16[2,64,1024]{2,1,0:T(8,128)(2,1)S(1)}, bf16[2,64,1024]{2,1,0:T(8,128)(2,1)S(1)}, u32[]{:S(2)}, u32[]{:S(2)}) %collective-permute-start.3) | collective-permute-done | bytes 262176 | tf_op jit(solution)/shard_map/ppermute | solution.py:26
  27.3 2.6 %collective-permute-start.10 = (bf16[64,1024]{1,0:T(8,128)(2,1)S(1)}, bf16[64,1024]{1,0:T(8,128)(2,1)S(1)}, u32[]{:S(2)}, u32[]{:S(2)}) collective-permute-start(bf16[64,1024]{1,0:T(8,128)(2,1)S(1)} %slice_bitcast_fusion.10), channel_id=1, source_target_pairs={{0,6},{2,0},{4,2},{6,4},{1,7},{3,1},{5,3},{7,5},{8,14},{10,8},{12,... | collective-permute-start | bytes 393224 | tf_op jit(solution)/shard_map/ppermute | solution.py:26
  31.0 6.6 %collective-permute-done.10 = bf16[64,1024]{1,0:T(8,128)(2,1)S(1)} collective-permute-done((bf16[64,1024]{1,0:T(8,128)(2,1)S(1)}, bf16[64,1024]{1,0:T(8,128)(2,1)S(1)}, u32[]{:S(2)}, u32[]{:S(2)}) %collective-permute-start.10) | collective-permute-done | bytes 131104 | tf_op jit(solution)/shard_map/ppermute | solution.py:26
  37.9 2.7 %collective-permute-start.12 = (bf16[2,64,1024]{2,1,0:T(8,128)(2,1)S(1)}, bf16[2,64,1024]{2,1,0:T(8,128)(2,1)S(1)}, u32[]{:S(2)}, u32[]{:S(2)}) collective-permute-start(bf16[2,64,1024]{2,1,0:T(8,128)(2,1)S(1)} %pad_maximum_fusion.6.zz), channel_id=1, source_target_pairs={{0,24},{8,0},{16,8},{24,16},{1,25},{9,1},{17,9},{25,17},{2,26},{10... | collective-permute-start | bytes 786440 | tf_op jit(solution)/shard_map/ppermute | solution.py:26
  46.8 2.5 %shard_map.73 = (bf16[2,4096,512]{2,1,0:T(8,128)(2,1)S(1)}, f32[8,128]{1,0:T(8,128)S(1)}) custom-call(bf16[4096,512]{1,0:T(8,128)(2,1)S(1)} %bitcast.118, bf16[4096,512]{1,0:T(8,128)(2,1)} %collective-permute-done.6.other, f32[2,512]{1,0:T(2,128)S(1)} %pad_maximum_fusion.14.after.b_up), custom_call_target="tpu_custom_call" | custom-call | bytes 16777216 | tf_op jit(solution)/shard_map/pallas_call | solution.py:196
  51.5 7.3 %shard_map.74.after.near = bf16[6,64,1024]{2,1,0:T(8,128)(2,1)S(1)} custom-call(s32[2]{0:T(128)S(1)} %add_add_fusion.place, bf16[2,64,1024]{2,1,0:T(8,128)(2,1)S(1)} %pad_maximum_fusion.5.block, bf16[2,2,64,1024]{3,2,1,0:T(8,128)(2,1)S(1)} %pad_maximum_fusion.zs, bf16[2,64,1024]{2,1,0:T(8,128)(2,1)S(1)} %pad_maximum_fusion.6.zz, ...), custom_call_target="tpu_custom_call" | custom-call | flops 805306368 | bytes 1048576 | tf_op jit(solution)/shard_map/pallas_call | solution.py:174
  58.8 2.5 %shard_map.75 = (bf16[2,512,4096]{2,1,0:T(8,128)(2,1)S(1)}, f32[8,128]{1,0:T(8,128)S(1)}) custom-call(bf16[512,4096]{1,0:T(8,128)(2,1)S(1)} %bitcast.116, bf16[512,4096]{1,0:T(8,128)(2,1)} %collective-permute-done.13.other, bf16[6,64,1024]{2,1,0:T(8,128)(2,1)S(1)} %shard_map.74.after.near), custom_call_target="tpu_custom_call" | custom-call | bytes 16777216 | tf_op jit(solution)/shard_map/pallas_call | solution.py:196
  61.4 4.1 %shard_map.76 = (bf16[4,64,1024]{2,1,0:T(8,128)(2,1)S(1)}, bf16[4,64,1024]{2,1,0:T(8,128)(2,1)S(1)}, bf16[8,64,1024]{2,1,0:T(8,128)(2,1)S(1)}) custom-call(s32[2]{0:T(128)S(1)} %bitcast_add_fusion.2.place, bf16[4,64,1024]{2,1,0:T(8,128)(2,1)S(1)} %collective-permute-done.14.ml, bf16[4,64,1024]{2,1,0:T(8,128)(2,1)S(1)} %collective-permute-done.15.mr, ...), custom_call_target="tpu_custom_call" | custom-call | flops 536870912 | bytes 1048576 | tf_op jit(solution)/shard_map/pallas_call | solution.py:174
  65.6 2.7 %collective-permute-start.17 = (bf16[4,64,1024]{2,1,0:T(8,128)(2,1)S(1)}, bf16[4,64,1024]{2,1,0:T(8,128)(2,1)S(1)}, u32[]{:S(2)}, u32[]{:S(2)}) collective-permute-start(bf16[4,64,1024]{2,1,0:T(8,128)(2,1)S(1)} %get-tuple-element.74), channel_id=1, source_target_pairs={{0,24},{8,0},{16,8},{24,16},{1,25},{9,1},{17,9},{25,17},{2,26},{10... | collective-permute-start | bytes 1572872 | tf_op jit(solution)/shard_map/ppermute | solution.py:26
  68.2 5.3 %shard_map.77 = (bf16[2,4,64,1024]{3,2,1,0:T(8,128)(2,1)S(1)}, bf16[2,4,64,1024]{3,2,1,0:T(8,128)(2,1)S(1)}, bf16[2,4,64,1024]{3,2,1,0:T(8,128)(2,1)S(1)}, bf16[2,64,1024]{2,1,0:T(8,128)(2,1)S(1)}) custom-call(s32[2]{0:T(128)S(1)} %add_add_fusion.place, bf16[8,64,1024]{2,1,0:T(8,128)(2,1)S(1)} %get-tuple-element.70.hid, ...), custom_call_target="tpu_custom_call" | custom-call | flops 805306368 | bytes 1048576 | tf_op jit(solution)/shard_map/pallas_call | solution.py:174
  73.7 2.2 %collective-permute-done.16 = bf16[4,64,1024]{2,1,0:T(8,128)(2,1)S(1)} collective-permute-done((bf16[4,64,1024]{2,1,0:T(8,128)(2,1)S(1)}, bf16[4,64,1024]{2,1,0:T(8,128)(2,1)S(1)}, u32[]{:S(2)}, u32[]{:S(2)}) %collective-permute-start.16) | collective-permute-done | bytes 524320 | tf_op jit(solution)/shard_map/ppermute | solution.py:26
  76.3 2.5 %collective-permute-start.21 = (bf16[2,1,64,1024]{3,2,1,0:T(8,128)(2,1)S(1)}, bf16[2,1,64,1024]{3,2,1,0:T(8,128)(2,1)S(1)}, u32[]{:S(2)}, u32[]{:S(2)}) collective-permute-start(bf16[2,1,64,1024]{3,2,1,0:T(8,128)(2,1)S(1)} %pad_maximum_fusion.8), channel_id=1, source_target_pairs={{0,24},{8,0},{16,8},{24,16},{1,25},{9,1},{17,9},{25,17},{2,26},{10... | collective-permute-start | bytes 786440 | tf_op jit(solution)/shard_map/ppermute | solution.py:26
  79.0 2.7 %collective-permute-start.19 = (bf16[2,2,64,1024]{3,2,1,0:T(8,128)(2,1)S(1)}, bf16[2,2,64,1024]{3,2,1,0:T(8,128)(2,1)S(1)}, u32[]{:S(2)}, u32[]{:S(2)}) collective-permute-start(bf16[2,2,64,1024]{3,2,1,0:T(8,128)(2,1)S(1)} %pad_maximum_fusion.4), channel_id=1, source_target_pairs={{0,24},{8,0},{16,8},{24,16},{1,25},{9,1},{17,9},{25,17},{2,26},{10... | collective-permute-start | bytes 1572872 | tf_op jit(solution)/shard_map/ppermute | solution.py:26
  82.8 2.5 %collective-permute-done.20 = bf16[2,1,64,1024]{3,2,1,0:T(8,128)(2,1)S(1)} collective-permute-done((bf16[2,1,64,1024]{3,2,1,0:T(8,128)(2,1)S(1)}, bf16[2,1,64,1024]{3,2,1,0:T(8,128)(2,1)S(1)}, u32[]{:S(2)}, u32[]{:S(2)}) %collective-permute-start.20) | collective-permute-done | bytes 262176 | tf_op jit(solution)/shard_map/ppermute | solution.py:26
  85.5 3.8 %collective-permute-start.22 = (bf16[64,1024]{1,0:T(8,128)(2,1)S(1)}, bf16[64,1024]{1,0:T(8,128)(2,1)S(1)}, u32[]{:S(2)}, u32[]{:S(2)}) collective-permute-start(bf16[64,1024]{1,0:T(8,128)(2,1)S(1)} %get-tuple-element.112), channel_id=1, source_target_pairs={{0,2},{2,4},{4,6},{6,0},{1,3},{3,5},{5,7},{7,1},{8,10},{10,12},{12... | collective-permute-start | bytes 393224 | tf_op jit(solution)/shard_map/ppermute | solution.py:26
  91.6 3.9 %collective-permute-done.23 = bf16[64,1024]{1,0:T(8,128)(2,1)S(1)} collective-permute-done((bf16[64,1024]{1,0:T(8,128)(2,1)S(1)}, bf16[64,1024]{1,0:T(8,128)(2,1)S(1)}, u32[]{:S(2)}, u32[]{:S(2)}) %collective-permute-start.23) | collective-permute-done | bytes 131104 | tf_op jit(solution)/shard_map/ppermute | solution.py:26
  97.3 3.5 %collective-permute-start.24 = (bf16[2,64,1024]{2,1,0:T(8,128)(2,1)S(1)}, bf16[2,64,1024]{2,1,0:T(8,128)(2,1)S(1)}, u32[]{:S(2)}, u32[]{:S(2)}) collective-permute-start(bf16[2,64,1024]{2,1,0:T(8,128)(2,1)S(1)} %pad_maximum_fusion.9), channel_id=1, source_target_pairs={{0,2},{2,4},{4,6},{6,0},{1,3},{3,5},{5,7},{7,1},{8,10},{10,12},{12... | collective-permute-start | bytes 786440 | tf_op jit(solution)/shard_map/ppermute | solution.py:26
  101.2 5.5 %collective-permute-done.25 = bf16[2,64,1024]{2,1,0:T(8,128)(2,1)S(1)} collective-permute-done((bf16[2,64,1024]{2,1,0:T(8,128)(2,1)S(1)}, bf16[2,64,1024]{2,1,0:T(8,128)(2,1)S(1)}, u32[]{:S(2)}, u32[]{:S(2)}) %collective-permute-start.25) | collective-permute-done | bytes 262176 | tf_op jit(solution)/shard_map/ppermute | solution.py:26
  107.3 5.1 %collective-permute-start.28 = (bf16[2,64,512]{2,1,0:T(8,128)(2,1)S(1)}, bf16[2,64,512]{2,1,0:T(8,128)(2,1)S(1)}, u32[]{:S(2)}, u32[]{:S(2)}) collective-permute-start(bf16[2,64,512]{2,1,0:T(8,128)(2,1)S(1)} %get-tuple-element.109), channel_id=1, source_target_pairs={{0,32},{1,33},{32,64},{33,65},{64,96},{65,97},{96,128},{97,129},{1... | collective-permute-start | bytes 393224 | tf_op jit(solution)/shard_map/ppermute | solution.py:38
  112.4 13.5 %collective-permute-start.29 = (bf16[2,64,512]{2,1,0:T(8,128)(2,1)S(1)}, bf16[2,64,512]{2,1,0:T(8,128)(2,1)S(1)}, u32[]{:S(2)}, u32[]{:S(2)}) collective-permute-start(bf16[2,64,512]{2,1,0:T(8,128)(2,1)S(1)} %get-tuple-element.110), channel_id=1, source_target_pairs={{0,33},{1,32},{32,65},{33,64},{64,97},{65,96},{96,129},{97,128},{1... | collective-permute-start | bytes 393224 | tf_op jit(solution)/shard_map/ppermute | solution.py:38
  125.9 7.0 %collective-permute-done.29 = bf16[2,64,512]{2,1,0:T(8,128)(2,1)S(1)} collective-permute-done((bf16[2,64,512]{2,1,0:T(8,128)(2,1)S(1)}, bf16[2,64,512]{2,1,0:T(8,128)(2,1)S(1)}, u32[]{:S(2)}, u32[]{:S(2)}) %collective-permute-start.29) | collective-permute-done | bytes 131104 | tf_op jit(solution)/shard_map/ppermute | solution.py:38
  (97 shorter events, 28.1 us)
Async XLA Ops:
  4.6 18.9 %collective-permute-start.6 = (bf16[4096,512]{1,0:T(8,128)(2,1)}, bf16[4096,512]{1,0:T(8,128)(2,1)}, u32[]{:S(2)}, u32[]{:S(2)}) collective-permute-start(bf16[4096,512]{1,0:T(8,128)(2,1)} %bitcast.117), channel_id=1, source_target_pairs={{0,1},{1,0},{2,3},{3,2},{4,5},{5,4},{6,7},{7,6},{8,9},{9,8},{10,11... | collective-permute-start | bytes 12582920 | tf_op jit(solution)/shard_map/ppermute | solution.py:30
  6.0 12.5 %collective-permute-start.2 = (bf16[2,64,1024]{2,1,0:T(8,128)(2,1)S(1)}, bf16[2,64,1024]{2,1,0:T(8,128)(2,1)S(1)}, u32[]{:S(2)}, u32[]{:S(2)}) collective-permute-start(bf16[2,64,1024]{2,1,0:T(8,128)(2,1)S(1)} %pad_maximum_fusion.5.block), channel_id=1, source_target_pairs={{0,2},{2,4},{4,6},{6,0},{1,3},{3,5},{5,7},{7,1},{8,10},{10,12},{12... | collective-permute-start | bytes 786440 | tf_op jit(solution)/shard_map/ppermute | solution.py:26
  7.3 16.2 %collective-permute-start.3 = (bf16[2,64,1024]{2,1,0:T(8,128)(2,1)S(1)}, bf16[2,64,1024]{2,1,0:T(8,128)(2,1)S(1)}, u32[]{:S(2)}, u32[]{:S(2)}) collective-permute-start(bf16[2,64,1024]{2,1,0:T(8,128)(2,1)S(1)} %pad_maximum_fusion.5.block), channel_id=1, source_target_pairs={{0,6},{2,0},{4,2},{6,4},{1,7},{3,1},{5,3},{7,5},{8,14},{10,8},{12,... | collective-permute-start | bytes 786440 | tf_op jit(solution)/shard_map/ppermute | solution.py:26
  10.4 13.1 %collective-permute-start.4 = (bf16[2,64,1024]{2,1,0:T(8,128)(2,1)S(1)}, bf16[2,64,1024]{2,1,0:T(8,128)(2,1)S(1)}, u32[]{:S(2)}, u32[]{:S(2)}) collective-permute-start(bf16[2,64,1024]{2,1,0:T(8,128)(2,1)S(1)} %pad_maximum_fusion.5.block), channel_id=1, source_target_pairs={{0,8},{8,16},{16,24},{24,0},{1,9},{9,17},{17,25},{25,1},{2,10},{10... | collective-permute-start | bytes 786440 | tf_op jit(solution)/shard_map/ppermute | solution.py:26
  11.6 11.9 %collective-permute-start.5 = (bf16[2,64,1024]{2,1,0:T(8,128)(2,1)S(1)}, bf16[2,64,1024]{2,1,0:T(8,128)(2,1)S(1)}, u32[]{:S(2)}, u32[]{:S(2)}) collective-permute-start(bf16[2,64,1024]{2,1,0:T(8,128)(2,1)S(1)} %pad_maximum_fusion.5.block), channel_id=1, source_target_pairs={{0,24},{8,0},{16,8},{24,16},{1,25},{9,1},{17,9},{25,17},{2,26},{10... | collective-permute-start | bytes 786440 | tf_op jit(solution)/shard_map/ppermute | solution.py:26
  23.5 35.3 %collective-permute-start.13 = (bf16[512,4096]{1,0:T(8,128)(2,1)}, bf16[512,4096]{1,0:T(8,128)(2,1)}, u32[]{:S(2)}, u32[]{:S(2)}) collective-permute-start(bf16[512,4096]{1,0:T(8,128)(2,1)} %bitcast.115), channel_id=1, source_target_pairs={{0,1},{1,0},{2,3},{3,2},{4,5},{5,4},{6,7},{7,6},{8,9},{9,8},{10,11... | collective-permute-start | bytes 12582920 | tf_op jit(solution)/shard_map/ppermute | solution.py:30
  24.5 24.8 %collective-permute-start.7 = (bf16[2,2,64,1024]{3,2,1,0:T(8,128)(2,1)S(1)}, bf16[2,2,64,1024]{3,2,1,0:T(8,128)(2,1)S(1)}, u32[]{:S(2)}, u32[]{:S(2)}) collective-permute-start(bf16[2,2,64,1024]{3,2,1,0:T(8,128)(2,1)S(1)} %pad_maximum_fusion.zs), channel_id=1, source_target_pairs={{0,8},{8,16},{16,24},{24,0},{1,9},{9,17},{17,25},{25,1},{2,10},{10... | collective-permute-start | bytes 1572872 | tf_op jit(solution)/shard_map/ppermute | solution.py:26
  25.8 23.5 %collective-permute-start.8 = (bf16[2,2,64,1024]{3,2,1,0:T(8,128)(2,1)S(1)}, bf16[2,2,64,1024]{3,2,1,0:T(8,128)(2,1)S(1)}, u32[]{:S(2)}, u32[]{:S(2)}) collective-permute-start(bf16[2,2,64,1024]{3,2,1,0:T(8,128)(2,1)S(1)} %pad_maximum_fusion.zs), channel_id=1, source_target_pairs={{0,24},{8,0},{16,8},{24,16},{1,25},{9,1},{17,9},{25,17},{2,26},{10... | collective-permute-start | bytes 1572872 | tf_op jit(solution)/shard_map/ppermute | solution.py:26
  27.3 10.2 %collective-permute-start.10 = (bf16[64,1024]{1,0:T(8,128)(2,1)S(1)}, bf16[64,1024]{1,0:T(8,128)(2,1)S(1)}, u32[]{:S(2)}, u32[]{:S(2)}) collective-permute-start(bf16[64,1024]{1,0:T(8,128)(2,1)S(1)} %slice_bitcast_fusion.10), channel_id=1, source_target_pairs={{0,6},{2,0},{4,2},{6,4},{1,7},{3,1},{5,3},{7,5},{8,14},{10,8},{12,... | collective-permute-start | bytes 393224 | tf_op jit(solution)/shard_map/ppermute | solution.py:26
  29.9 7.9 %collective-permute-start.9 = (bf16[64,1024]{1,0:T(8,128)(2,1)S(1)}, bf16[64,1024]{1,0:T(8,128)(2,1)S(1)}, u32[]{:S(2)}, u32[]{:S(2)}) collective-permute-start(bf16[64,1024]{1,0:T(8,128)(2,1)S(1)} %slice_bitcast_fusion.11), channel_id=1, source_target_pairs={{0,2},{2,4},{4,6},{6,0},{1,3},{3,5},{5,7},{7,1},{8,10},{10,12},{12... | collective-permute-start | bytes 393224 | tf_op jit(solution)/shard_map/ppermute | solution.py:26
  37.8 11.5 %collective-permute-start.11 = (bf16[2,64,1024]{2,1,0:T(8,128)(2,1)S(1)}, bf16[2,64,1024]{2,1,0:T(8,128)(2,1)S(1)}, u32[]{:S(2)}, u32[]{:S(2)}) collective-permute-start(bf16[2,64,1024]{2,1,0:T(8,128)(2,1)S(1)} %pad_maximum_fusion.6.zz), channel_id=1, source_target_pairs={{0,8},{8,16},{16,24},{24,0},{1,9},{9,17},{17,25},{25,1},{2,10},{10... | collective-permute-start | bytes 786440 | tf_op jit(solution)/shard_map/ppermute | solution.py:26
  37.9 11.4 %collective-permute-start.12 = (bf16[2,64,1024]{2,1,0:T(8,128)(2,1)S(1)}, bf16[2,64,1024]{2,1,0:T(8,128)(2,1)S(1)}, u32[]{:S(2)}, u32[]{:S(2)}) collective-permute-start(bf16[2,64,1024]{2,1,0:T(8,128)(2,1)S(1)} %pad_maximum_fusion.6.zz), channel_id=1, source_target_pairs={{0,24},{8,0},{16,8},{24,16},{1,25},{9,1},{17,9},{25,17},{2,26},{10... | collective-permute-start | bytes 786440 | tf_op jit(solution)/shard_map/ppermute | solution.py:26
  49.5 11.9 %collective-permute-start.15 = (bf16[4,64,1024]{2,1,0:T(8,128)(2,1)S(1)}, bf16[4,64,1024]{2,1,0:T(8,128)(2,1)S(1)}, u32[]{:S(2)}, u32[]{:S(2)}) collective-permute-start(bf16[4,64,1024]{2,1,0:T(8,128)(2,1)S(1)} %pad_maximum_fusion.2), channel_id=1, source_target_pairs={{0,24},{8,0},{16,8},{24,16},{1,25},{9,1},{17,9},{25,17},{2,26},{10... | collective-permute-start | bytes 1572872 | tf_op jit(solution)/shard_map/ppermute | solution.py:26
  49.8 11.6 %collective-permute-start.14 = (bf16[4,64,1024]{2,1,0:T(8,128)(2,1)S(1)}, bf16[4,64,1024]{2,1,0:T(8,128)(2,1)S(1)}, u32[]{:S(2)}, u32[]{:S(2)}) collective-permute-start(bf16[4,64,1024]{2,1,0:T(8,128)(2,1)S(1)} %pad_maximum_fusion.1), channel_id=1, source_target_pairs={{0,8},{8,16},{16,24},{24,0},{1,9},{9,17},{17,25},{25,1},{2,10},{10... | collective-permute-start | bytes 1572872 | tf_op jit(solution)/shard_map/ppermute | solution.py:26
  65.5 10.5 %collective-permute-start.16 = (bf16[4,64,1024]{2,1,0:T(8,128)(2,1)S(1)}, bf16[4,64,1024]{2,1,0:T(8,128)(2,1)S(1)}, u32[]{:S(2)}, u32[]{:S(2)}) collective-permute-start(bf16[4,64,1024]{2,1,0:T(8,128)(2,1)S(1)} %get-tuple-element.73), channel_id=1, source_target_pairs={{0,8},{8,16},{16,24},{24,0},{1,9},{9,17},{17,25},{25,1},{2,10},{10... | collective-permute-start | bytes 1572872 | tf_op jit(solution)/shard_map/ppermute | solution.py:26
  65.6 10.4 %collective-permute-start.17 = (bf16[4,64,1024]{2,1,0:T(8,128)(2,1)S(1)}, bf16[4,64,1024]{2,1,0:T(8,128)(2,1)S(1)}, u32[]{:S(2)}, u32[]{:S(2)}) collective-permute-start(bf16[4,64,1024]{2,1,0:T(8,128)(2,1)S(1)} %get-tuple-element.74), channel_id=1, source_target_pairs={{0,24},{8,0},{16,8},{24,16},{1,25},{9,1},{17,9},{25,17},{2,26},{10... | collective-permute-start | bytes 1572872 | tf_op jit(solution)/shard_map/ppermute | solution.py:26
  79.0 16.5 %collective-permute-start.19 = (bf16[2,2,64,1024]{3,2,1,0:T(8,128)(2,1)S(1)}, bf16[2,2,64,1024]{3,2,1,0:T(8,128)(2,1)S(1)}, u32[]{:S(2)}, u32[]{:S(2)}) collective-permute-start(bf16[2,2,64,1024]{3,2,1,0:T(8,128)(2,1)S(1)} %pad_maximum_fusion.4), channel_id=1, source_target_pairs={{0,24},{8,0},{16,8},{24,16},{1,25},{9,1},{17,9},{25,17},{2,26},{10... | collective-permute-start | bytes 1572872 | tf_op jit(solution)/shard_map/ppermute | solution.py:26
  81.8 13.7 %collective-permute-start.18 = (bf16[2,2,64,1024]{3,2,1,0:T(8,128)(2,1)S(1)}, bf16[2,2,64,1024]{3,2,1,0:T(8,128)(2,1)S(1)}, u32[]{:S(2)}, u32[]{:S(2)}) collective-permute-start(bf16[2,2,64,1024]{3,2,1,0:T(8,128)(2,1)S(1)} %pad_maximum_fusion.3), channel_id=1, source_target_pairs={{0,8},{8,16},{16,24},{24,0},{1,9},{9,17},{17,25},{25,1},{2,10},{10... | collective-permute-start | bytes 1572872 | tf_op jit(solution)/shard_map/ppermute | solution.py:26
  89.3 11.5 %collective-permute-start.27 = (bf16[2,1,64,1024]{3,2,0,1:T(8,128)(2,1)S(1)}, bf16[2,1,64,1024]{3,2,0,1:T(8,128)(2,1)S(1)}, u32[]{:S(2)}, u32[]{:S(2)}) collective-permute-start(bf16[2,1,64,1024]{3,2,0,1:T(8,128)(2,1)S(1)} %pad_maximum_fusion.12), channel_id=1, source_target_pairs={{0,24},{8,0},{16,8},{24,16},{1,25},{9,1},{17,9},{25,17},{2,26},{10... | collective-permute-start | bytes 786440 | tf_op jit(solution)/shard_map/ppermute | solution.py:26
  91.6 9.6 %collective-permute-start.26 = (bf16[2,1,64,1024]{3,2,1,0:T(8,128)(2,1)S(1)}, bf16[2,1,64,1024]{3,2,1,0:T(8,128)(2,1)S(1)}, u32[]{:S(2)}, u32[]{:S(2)}) collective-permute-start(bf16[2,1,64,1024]{3,2,1,0:T(8,128)(2,1)S(1)} %pad_maximum_fusion.11), channel_id=1, source_target_pairs={{0,8},{8,16},{16,24},{24,0},{1,9},{9,17},{17,25},{25,1},{2,10},{10... | collective-permute-start | bytes 786440 | tf_op jit(solution)/shard_map/ppermute | solution.py:26
  95.9 10.8 %collective-permute-start.25 = (bf16[2,64,1024]{2,1,0:T(8,128)(2,1)S(1)}, bf16[2,64,1024]{2,1,0:T(8,128)(2,1)S(1)}, u32[]{:S(2)}, u32[]{:S(2)}) collective-permute-start(bf16[2,64,1024]{2,1,0:T(8,128)(2,1)S(1)} %pad_maximum_fusion.10), channel_id=1, source_target_pairs={{0,6},{2,0},{4,2},{6,4},{1,7},{3,1},{5,3},{7,5},{8,14},{10,8},{12,... | collective-permute-start | bytes 786440 | tf_op jit(solution)/shard_map/ppermute | solution.py:26
  97.3 9.7 %collective-permute-start.24 = (bf16[2,64,1024]{2,1,0:T(8,128)(2,1)S(1)}, bf16[2,64,1024]{2,1,0:T(8,128)(2,1)S(1)}, u32[]{:S(2)}, u32[]{:S(2)}) collective-permute-start(bf16[2,64,1024]{2,1,0:T(8,128)(2,1)S(1)} %pad_maximum_fusion.9), channel_id=1, source_target_pairs={{0,2},{2,4},{4,6},{6,0},{1,3},{3,5},{5,7},{7,1},{8,10},{10,12},{12... | collective-permute-start | bytes 786440 | tf_op jit(solution)/shard_map/ppermute | solution.py:26
  107.3 18.6 %collective-permute-start.28 = (bf16[2,64,512]{2,1,0:T(8,128)(2,1)S(1)}, bf16[2,64,512]{2,1,0:T(8,128)(2,1)S(1)}, u32[]{:S(2)}, u32[]{:S(2)}) collective-permute-start(bf16[2,64,512]{2,1,0:T(8,128)(2,1)S(1)} %get-tuple-element.109), channel_id=1, source_target_pairs={{0,32},{1,33},{32,64},{33,65},{64,96},{65,97},{96,128},{97,129},{1... | collective-permute-start | bytes 393224 | tf_op jit(solution)/shard_map/ppermute | solution.py:38
  112.4 20.5 %collective-permute-start.29 = (bf16[2,64,512]{2,1,0:T(8,128)(2,1)S(1)}, bf16[2,64,512]{2,1,0:T(8,128)(2,1)S(1)}, u32[]{:S(2)}, u32[]{:S(2)}) collective-permute-start(bf16[2,64,512]{2,1,0:T(8,128)(2,1)S(1)} %get-tuple-element.110), channel_id=1, source_target_pairs={{0,33},{1,32},{32,65},{33,64},{64,97},{65,96},{96,129},{97,128},{1... | collective-permute-start | bytes 393224 | tf_op jit(solution)/shard_map/ppermute | solution.py:38
  (9 other events, 141.6 us)
